TPU v7x, 32 devices: a whole 2x2x4 slice. The times are simulated.
32 devices in a mesh: store: 8 (over z, x), seq: 4 (over y, core).
Axes of the slice: x: 2, y: 2, z: 4, core: 2. Of those that a mesh axis runs over, the one named last changes fastest.
Arguments:
- activations: bfloat16 [1, 16, 1024, 4096], P(None, 'store', 'seq'), may hold values from -6 to 6
- out_grads: bfloat16 [1, 16, 1024, 4096], P(None, 'store', 'seq'), may hold values from -6 to 6
- proj_in: bfloat16 [1, 64, 4096], replicated, may hold values from -0.09375 to 0.09375
- proj_out: bfloat16 [1, 64, 4096], replicated, may hold values from -0.09375 to 0.09375
- eig_out: float32 [1, 64, 64], replicated, may hold values from -0.75 to 0.75
- eig_in: float32 [1, 64, 64], replicated, may hold values from -0.75 to 0.75
- eig_values: float32 [1, 64, 64], replicated, may hold values from 0.1 to 10
- lengths: int32 [16], P('store'), may hold values from 1 to 1024
- owners: int32 [16], P('store'), may hold values from 0 to 7
- stored: bfloat16 [10240, 4096], P(('store', 'seq')), may hold values from -6 to 6
- queries: bfloat16 [1024, 4096], P('store'), may hold values from -6 to 6
- query_owner: int32 [8], replicated, may hold values from 0 to 7
Outputs:
- stored_scores: float32 [8, 10240, 128], P(None, ('store', 'seq'))
- group_scores: float32 [8, 8, 128], P('store')
All inputs are finite; a program needn't handle non-finite values.
Results may differ from a plain program's by a relative error of at most 0.0032.
Values may be sent and summed in bfloat16 or wider, within the bound.
No kernel may reach another device: no remote copies, remote signals or barrier semaphores. Data moves between devices by JAX's collectives and lax.ppermute only.
A program may use at most 128 MiB of HBM per device.

v0:
```python
import math

import jax
import jax.numpy as jnp
from jax import lax
from jax.sharding import PartitionSpec as P


def from_root(array, axis, root):
    mine = lax.axis_index(axis) == root
    return lax.psum(jnp.where(mine, array, jnp.zeros_like(array)), axis)


def precondition(group, eig_out, eig_in, eig_values):
    row_count = group.shape[0]
    layers = eig_out.shape[0]
    rank = eig_out.shape[1]
    blocks = group.reshape(row_count, layers, rank, rank)
    highest = lax.Precision.HIGHEST
    rotated = jnp.einsum("lri,olrs->olis", eig_out, blocks, precision=highest)
    rotated = jnp.einsum("olis,lsj->olij", rotated, eig_in, precision=highest)
    scaled = rotated / eig_values[None]
    restored = jnp.einsum("lri,olij->olrj", eig_out, scaled, precision=highest)
    restored = jnp.einsum("olrj,lsj->olrs", restored, eig_in, precision=highest)
    return restored.reshape(row_count, layers * rank * rank).astype(jnp.bfloat16)


def project_layer(inputs, outgoing, weight_in, weight_out, valid, factor):
    in_side = jnp.einsum("etd,rd->etr", inputs, weight_in, preferred_element_type=jnp.float32)
    out_side = jnp.einsum("etd,rd->etr", outgoing, weight_out, preferred_element_type=jnp.float32)
    weighted = out_side * valid[:, :, None]
    blocks = jnp.einsum("etr,ets->ers", weighted, in_side, precision=lax.Precision.HIGHEST) * factor
    return blocks.reshape(blocks.shape[0], -1)


def owner_sums(owners, sources, count):
    owner_ids = jnp.arange(count, dtype=jnp.int32)
    select = (owners[None, :] == owner_ids[:, None]).astype(jnp.float32)
    return jnp.dot(select, sources, precision=lax.Precision.HIGHEST)


def shards(
    activations,
    out_grads,
    proj_in,
    proj_out,
    eig_out,
    eig_in,
    eig_values,
    lengths,
    owners,
    stored,
    queries,
    query_owner,
):
    seq_count = lax.axis_size("seq")
    seq_index = lax.axis_index("seq")
    local_len = activations.shape[2]
    positions = seq_index * local_len + jnp.arange(local_len, dtype=jnp.int32)
    valid = (positions[None, :] < lengths[:, None]).astype(jnp.float32)
    factor = jnp.float32(1.0 / math.sqrt(local_len * seq_count))
    partial_value = project_layer(
        activations[0], out_grads[0], proj_in[0], proj_out[0], valid, factor
    )
    summed = lax.psum(partial_value, "seq")
    owned_row = lax.psum_scatter(
        owner_sums(owners, summed, 1 * lax.axis_size("store")),
        "store",
        scatter_dimension=0,
        tiled=True,
    )
    precond = precondition(owned_row, eig_out, eig_in, eig_values)
    flat_size = stored.shape[1]
    score_scale = jnp.float32(1.0 / math.sqrt(flat_size))
    stored_list = []
    group_list = []
    for step_index in range(query_owner.shape[0]):
        root_index = query_owner[step_index]
        panel_rows = from_root(queries, "store", root_index)
        stored_list.append(
            lax.dot_general(
                stored, panel_rows, (((1,), (1,)), ((), ())), preferred_element_type=jnp.float32
            )
            * score_scale
        )
        group_list.append(
            lax.dot_general(
                precond, panel_rows, (((1,), (1,)), ((), ())), preferred_element_type=jnp.float32
            )
            * score_scale
        )
    return (jnp.stack(stored_list, axis=0), jnp.stack(group_list, axis=1))


def solution(mesh):
    return jax.shard_map(
        shards,
        mesh=mesh,
        in_specs=(
            P(None, "store", "seq", None),
            P(None, "store", "seq", None),
            P(),
            P(),
            P(),
            P(),
            P(),
            P("store"),
            P("store"),
            P(("store", "seq"), None),
            P("store", None),
            P(),
        ),
        out_specs=(P(None, ("store", "seq"), None), P("store", None, None)),
        check_vma=False,
    )
```

profile of v0, /device:TPU:1, one launch (start us, length us, event | category | flops | bytes accessed | tf_op | source)
XLA Modules:
  0.0 405.9 jit_solution(13041529545396486806)
XLA Ops:
  7.2 0.0 copy-start
  7.2 0.0 copy-start.10
  7.2 0.0 all-reduce.5.cloned.1.call-start
  7.2 0.0 copy-start.1
  7.3 0.9 compare_convert_fusion
  8.1 4.3 %fusion = f32[2,256,64]{1,2,0:T(8,128)S(1)} fusion(bf16[1,2,256,4096]{3,2,1,0:T(8,128)(2,1)} %param.12, bf16[1,64,4096]{2,1,0:T(8,128)(2,1)} %param.14), kind=kOutput, calls=%fused_computation | convolution fusion | flops 268435456 | bytes 4849664 | tf_op jit(solution)/shard_map/etd,rd->etr/dot_general | solution.py:29
  12.5 0.0 copy-done.10
  12.5 0.0 copy-done.1
  12.5 0.0 copy-start.15
  12.5 0.0 copy-start.13
  12.5 1.4 fusion.20
  13.9 0.3 convolution_multiply_fusion.8
  14.2 0.1 reshape.113
  14.3 11.2 %psum.71 = f32[2,4096]{1,0:T(2,128)S(1)} all-reduce(f32[2,4096]{1,0:T(2,128)S(1)} %reshape.113), channel_id=1, replica_groups=mesh['store'=8,'seq'=4] {'seq'}, use_global_device_ids=true, to_apply=%region_8.9 | all-reduce | flops 8192 | bytes 65536 | tf_op jit(solution)/shard_map/psum | solution.py:65
  25.4 0.0 copy-done.15
  25.5 0.8 fusion.48
  26.3 0.0 all-reduce.5.cloned.1.call-update
  26.3 0.0 all-reduce.7.cloned.1.call-start
  26.4 0.0 copy-done.13
  26.4 0.7 fusion.50
  32.1 4.6 %broadcast_select_fusion = (bf16[128,4096]{1,0:T(8,128)(2,1)}, bf16[128,4096]{1,0:T(8,128)(2,1)}, bf16[128,4096]{1,0:T(8,128)(2,1)}, bf16[128,4096]{1,0:T(8,128)...) fusion(bf16[128,4096]{1,0:T(8,128)(2,1)} %param.22, ...), kind=kLoop, calls=%fused_computation.61 | loop fusion | flops 4194304 | bytes 9437192 | tf_op jit(solution)/shard_map/jit(_where)/select_n | solution.py:11
  36.7 0.0 copy-start.16
  36.7 0.0 copy-start.14
  36.7 0.0 all-reduce.7.cloned.1.call-update
  36.8 0.6 copy-done.16
  37.4 0.6 dynamic-slice
  38.0 57.9 %all-reduce.5.cloned.1.call-done = f32[8,4096]{1,0:T(8,128)} async-done(((f32[8,4096]{1,0:T(8,128)}), f32[8,4096]{1,0:T(8,128)}) %all-reduce.5.cloned.1.call-update) | async-done | bytes 131088
  95.8 1.6 dynamic-slice_reduce_fusion
  97.4 0.1 reshape.114
  97.5 0.0 copy-done.11
  97.5 0.2 convolution_bitcast_fusion.2
  97.8 0.0 copy-done.12
  97.8 0.0 copy-done.14
  97.8 0.2 fusion.41
  98.0 0.2 convolution_bitcast_fusion
  98.3 0.2 fusion.23
  98.5 0.1 reshape.122
  98.6 280.6 %all-reduce.7.cloned.1.call-done = (bf16[128,4096]{1,0:T(8,128)(2,1)}, bf16[128,4096]{1,0:T(8,128)(2,1)}, bf16[128,4096]{1,0:T(8,128)(2,1)}, bf16[128,4096]{1,0:...) async-done(((bf16[128,4096]{1,0:T(8,128)(2,1)}, bf16[128,4096]{1,0:T(8,128)(2,1)}, ...) | async-done | bytes 8388624 | tf_op jit(solution)/shard_map/psum | solution.py:11
  379.2 1.7 fusion.25
  381.0 1.7 fusion.27
  382.7 1.7 fusion.29
  384.4 0.0 copy-done.6
  384.4 0.4 fusion.31
  384.8 0.0 copy-done.5
  384.8 0.4 fusion.33
  385.1 0.0 copy-done.4
  385.1 0.4 fusion.35
  385.5 0.0 copy-done.3
  385.5 0.4 fusion.37
  385.9 0.0 copy-done.2
  385.9 0.4 fusion.39
  386.3 0.0 copy-done
  386.3 0.0 copy-done.9
  386.3 1.5 fusion.19
  387.9 0.0 copy-done.8
  387.9 1.5 fusion.17
  389.4 0.0 copy-done.7
  389.4 1.5 fusion.15
  390.9 1.5 fusion.13
  392.4 1.5 fusion.11
  393.9 1.5 fusion.9
  395.4 1.5 fusion.7
  396.9 1.5 fusion.5
  398.4 0.6 stack.71
  (11 shorter events, 0.0 us)
Async XLA Ops:
  7.2 379.2 %copy-start = (bf16[320,4096]{1,0:T(8,128)(2,1)S(1)}, bf16[320,4096]{1,0:T(8,128)(2,1)}, u32[]{:S(2)}) copy-start(bf16[320,4096]{1,0:T(8,128)(2,1)} %param.21) | copy-start | bytes 7864324
  7.2 5.3 %copy-start.10 = (bf16[1,64,4096]{2,1,0:T(8,128)(2,1)S(1)}, bf16[1,64,4096]{2,1,0:T(8,128)(2,1)}, u32[]{:S(2)}) copy-start(bf16[1,64,4096]{2,1,0:T(8,128)(2,1)} %param.15) | copy-start | bytes 1572868
  7.2 88.7 %all-reduce.5.cloned.1.call-start = ((), (), s32[]{:S(2)}) async-start(), calls=%async_computation | async-start | bytes 262144
  7.2 5.2 %copy-start.1 = (bf16[1,2,256,4096]{3,2,1,0:T(8,128)(2,1)S(1)}, bf16[1,2,256,4096]{3,2,1,0:T(8,128)(2,1)}, u32[]{:S(2)}) copy-start(bf16[1,2,256,4096]{3,2,1,0:T(8,128)(2,1)} %param.13) | copy-start | bytes 12582916
  12.5 13.0 %copy-start.15 = (s32[2]{0:T(128)S(1)}, s32[2]{0:T(128)}, u32[]{:S(2)}) copy-start(s32[2]{0:T(128)} %param.20) | copy-start | bytes 28
  12.5 13.9 %copy-start.13 = (s32[8]{0:T(128)S(1)}, s32[8]{0:T(128)}, u32[]{:S(2)}) copy-start(s32[8]{0:T(128)} %param.23) | copy-start | bytes 100
  26.3 352.9 %all-reduce.7.cloned.1.call-start = ((), (), s32[]{:S(2)}) async-start(), calls=%async_computation.1 | async-start | bytes 16777216 | tf_op jit(solution)/shard_map/psum | solution.py:11
  36.7 0.7 copy-start.16
  36.7 60.8 %copy-start.11 = (f32[1,64,64]{2,1,0:T(8,128)S(1)}, f32[1,64,64]{2,1,0:T(8,128)}, u32[]{:S(2)}) copy-start(f32[1,64,64]{2,1,0:T(8,128)} %param.16) | copy-start | bytes 49156
  36.7 61.0 %copy-start.12 = (f32[1,64,64]{2,1,0:T(8,128)S(1)}, f32[1,64,64]{2,1,0:T(8,128)}, u32[]{:S(2)}) copy-start(f32[1,64,64]{2,1,0:T(8,128)} %param.17) | copy-start | bytes 49156
  36.7 61.1 %copy-start.14 = (f32[1,64,64]{2,1,0:T(8,128)S(1)}, f32[1,64,64]{2,1,0:T(8,128)}, u32[]{:S(2)}) copy-start(f32[1,64,64]{2,1,0:T(8,128)} %param.18) | copy-start | bytes 49156
  379.2 5.2 %copy-start.6 = (bf16[128,4096]{1,0:T(8,128)(2,1)S(1)}, bf16[128,4096]{1,0:T(8,128)(2,1)}, u32[]{:S(2)}) copy-start(bf16[128,4096]{1,0:T(8,128)(2,1)} %get-tuple-element.5) | copy-start | bytes 3145732
  379.2 5.6 %copy-start.5 = (bf16[128,4096]{1,0:T(8,128)(2,1)S(1)}, bf16[128,4096]{1,0:T(8,128)(2,1)}, u32[]{:S(2)}) copy-start(bf16[128,4096]{1,0:T(8,128)(2,1)} %get-tuple-element.6) | copy-start | bytes 3145732
  379.2 5.9 %copy-start.4 = (bf16[128,4096]{1,0:T(8,128)(2,1)S(1)}, bf16[128,4096]{1,0:T(8,128)(2,1)}, u32[]{:S(2)}) copy-start(bf16[128,4096]{1,0:T(8,128)(2,1)} %get-tuple-element.7) | copy-start | bytes 3145732
  380.9 4.6 %copy-start.3 = (bf16[128,4096]{1,0:T(8,128)(2,1)S(1)}, bf16[128,4096]{1,0:T(8,128)(2,1)}, u32[]{:S(2)}) copy-start(bf16[128,4096]{1,0:T(8,128)(2,1)} %get-tuple-element.8) | copy-start | bytes 3145732
  382.7 3.3 copy-start.2
  384.4 2.0 copy-start.9
  385.9 1.9 copy-start.8
  387.9 1.5 copy-start.7
Sparse Core Ops, SparseCore 0:
  26.4 69.3 all-reduce.4
  102.7 276.4 all-reduce.6
where the time goes:
time: 407 us; the launch traced here: 406 us
  waiting for transfers between devices  339 us (83%)
  matrix products  26.9 us (7%)
  between operations  19.3 us (5%)
  blocking collectives  11.2 us (3%)
  other arithmetic  5.5 us (1%)
  local copies, waits for them, and re-layouts  4.4 us (1%)
    psum x1, waiting for transfers between devices, from_root(): return lax.psum(jnp.where(mine, array, jnp.zeros_like(array)), axis)  281 us
    unnamed x3, waiting for transfers between devices  57.9 us
    dot_general x8, matrix products, shards(): lax.dot_general(stored, panel_rows, (((1,), (1,)), ((), ())), preferred_e...  12.1 us
    psum x1, blocking collectives, shards(): summed = lax.psum(partial_value, 'seq')  11.2 us
  transfers between devices with their start and end apart: 2, of which 2 were waited for; matrix products, arithmetic and copies ran while one was open for 2% of the time, Pallas kernels for 0%

commit v1 on v0

v1 whole, which is shorter than its diff:
```python
import functools
import math

import jax
import jax.numpy as jnp
from jax import lax
from jax.experimental import pallas as pl
from jax.experimental.pallas import tpu as pltpu
from jax.sharding import PartitionSpec as P

AXES = ("store", "seq")
HIGHEST = lax.Precision.HIGHEST
NT = (((1,), (1,)), ((), ()))
MIB = 1 << 20

STEPS = (
    (0, "W", "X", True),
    (1, "Z", "X", False),
    (1, "Y", "Y", False),
    (2, "X", "W", False),
    (4, "Z", "X", False),
    (4, "Y", "Y", False),
    (3, "Z", "X", False),
)
EARLY, MIDDLE, LATE = (1, 2, 3, 4), (5,), (6, 7)


def ring_place(z):
    return z ^ (z >> 1)


def neighbour(way, z, x, y):
    if way == "X":
        return z, 1 - x, y
    if way == "Y":
        return z, x, 1 - y
    if way == "Z":
        return ring_place((ring_place(z) + 1) % 4), x, y
    if way == "W":
        return ring_place((ring_place(z) + 3) % 4), x, y
    if way == "S":
        return z ^ 1, x, y
    if way == "T":
        return z ^ 2, x, y
    return z, x, y


def pairs(way0, way1, swap):
    out = []
    for z in range(4):
        for x in range(2):
            for y in range(2):
                for core in range(2):
                    z2, x2, y2 = neighbour(way1 if core else way0, z, x, y)
                    core2 = 1 - core if swap else core
                    out.append(((z * 2 + x) * 4 + y * 2 + core, (z2 * 2 + x2) * 4 + y2 * 2 + core2))
    return out


def move(array, way0, way1, swap=False):
    return lax.ppermute(array, AXES, pairs(way0, way1, swap))


def contents():
    have = [((0, 0, 0), (0, 0, 1))]
    for source, way0, way1, swap in STEPS:
        got = [None, None]
        for core, way in ((0, way0), (1, way1)):
            ring, across, half = have[source][core]
            if way == "X":
                across = 1 - across
            elif way == "Y":
                half = 1 - half
            elif way == "Z":
                ring = (ring + 1) % 4
            elif way == "W":
                ring = (ring + 3) % 4
            got[1 - core if swap else core] = (ring, across, half)
        have.append(tuple(got))
    return have


CONTENTS = contents()


def unit_place(step, partner, store, seq):
    y, core = seq // 2, seq % 2
    z, x = store // 2, store % 2
    first, second = CONTENTS[step]
    mine = core if not partner else 1 - core
    pick = [jnp.where(mine == 0, a, b) for a, b in zip(first, second, strict=True)]
    place = (ring_place(z) + 4 - pick[0]) % 4
    return ring_place(place) * 2 + (x ^ pick[1]), pick[2] ^ y


def project_kernel(lengths, owners, acts, grads, weight_in, weight_out, out, total, *, factor, owner_count):
    step = pl.program_id(0)
    per = pl.num_programs(0) // lengths.shape[0]
    rows = acts.shape[0]
    example = step // per
    start = lax.axis_index("seq") * (rows * per) + (step % per) * rows
    in_side = lax.dot_general(acts[...], weight_in[...], NT, preferred_element_type=jnp.float32)
    out_side = lax.dot_general(grads[...], weight_out[...], NT, preferred_element_type=jnp.float32)
    positions = start + lax.broadcasted_iota(jnp.int32, out_side.shape, 0)
    out_side = jnp.where(positions < lengths[example], out_side, 0.0)
    block = lax.dot_general(
        out_side, in_side, (((0,), (0,)), ((), ())), precision=HIGHEST, preferred_element_type=jnp.float32
    )

    @pl.when(step % per == 0)
    def _():
        total[example] = block

    @pl.when(step % per != 0)
    def _():
        total[example] += block

    @pl.when(step == pl.num_programs(0) - 1)
    def _():
        for owner in range(owner_count):
            acc = jnp.zeros_like(block)
            for e in range(lengths.shape[0]):
                acc += jnp.where(owners[e] == owner, total[e], 0.0)
            acc = acc * factor
            half = acc.shape[0] // 2
            out[owner] = jnp.concatenate([acc[:half], acc[half:]], axis=1)


def project(acts, grads, weight_in, weight_out, lengths, owners, factor, owner_count):
    examples, tokens, width = acts.shape
    rank = weight_in.shape[0]
    per = 2
    rows = tokens // per
    smem = pl.BlockSpec(memory_space=pltpu.SMEM)
    return pl.pallas_call(
        functools.partial(project_kernel, factor=factor, owner_count=owner_count),
        grid=(examples * per,),
        in_specs=[
            smem,
            smem,
            pl.BlockSpec((rows, width), lambda i: (i, 0)),
            pl.BlockSpec((rows, width), lambda i: (i, 0)),
            pl.BlockSpec((rank, width), lambda i: (0, 0)),
            pl.BlockSpec((rank, width), lambda i: (0, 0)),
        ],
        out_specs=pl.BlockSpec((owner_count, rank // 2, rank * 2), lambda i: (0, 0, 0)),
        out_shape=jax.ShapeDtypeStruct((owner_count, rank // 2, rank * 2), jnp.float32),
        scratch_shapes=[pltpu.VMEM((examples, rank, rank), jnp.float32)],
        compiler_params=pltpu.CompilerParams(vmem_limit_bytes=16 * MIB),
        cost_estimate=pl.CostEstimate(
            flops=4 * examples * tokens * width * rank,
            bytes_accessed=4 * examples * tokens * width,
            transcendentals=0,
        ),
    )(
        lengths,
        owners,
        acts.reshape(examples * tokens, width),
        grads.reshape(examples * tokens, width),
        weight_in,
        weight_out,
    )


def precondition_kernel(group, eig_out, eig_in, eig_values, out):
    rank = eig_out.shape[0]
    packed = group[...]
    block = jnp.concatenate([packed[:, :rank], packed[:, rank:]], axis=0)
    dot = functools.partial(lax.dot_general, precision=HIGHEST, preferred_element_type=jnp.float32)
    basis_out, basis_in = eig_out[...], eig_in[...]
    rotated = dot(basis_out, block, (((0,), (0,)), ((), ())))
    rotated = dot(rotated, basis_in, (((1,), (0,)), ((), ())))
    scaled = rotated / eig_values[...]
    restored = dot(basis_out, scaled, (((1,), (0,)), ((), ())))
    restored = dot(restored, basis_in, NT)
    out[...] = restored.astype(jnp.bfloat16)


def precondition(group, eig_out, eig_in, eig_values):
    rank = eig_out.shape[0]
    return pl.pallas_call(
        precondition_kernel,
        out_shape=jax.ShapeDtypeStruct((rank, rank), jnp.bfloat16),
        compiler_params=pltpu.CompilerParams(vmem_limit_bytes=4 * MIB),
        cost_estimate=pl.CostEstimate(flops=1 << 24, bytes_accessed=1 << 17, transcendentals=0),
    )(group, eig_out, eig_in, eig_values)


def add_units(left, units, steps, totals):
    store, seq = lax.axis_index("store"), lax.axis_index("seq")
    for number, unit in enumerate(units):
        panel, half = unit_place(steps[number // 2], number % 2 == 1, store, seq)
        width = unit.shape[1]
        columns = pl.ds(pl.multiple_of(half * width, width), width)
        totals[panel] += lax.dot_general(left(columns), unit[...], NT, preferred_element_type=jnp.float32)


def early_kernel(*refs):
    stored, own = refs[0], refs[1]
    units, out = refs[2:-1], refs[-1]
    out[...] = jnp.zeros_like(out)
    out[lax.axis_index("store")] = lax.dot_general(
        stored[...], own[...], NT, preferred_element_type=jnp.float32
    )
    add_units(lambda columns: stored[:, columns], units, EARLY, out)


def early_scores(stored, own, units, panels):
    rows, width = stored.shape
    return pl.pallas_call(
        early_kernel,
        out_shape=jax.ShapeDtypeStruct((panels, rows, own.shape[0]), jnp.float32),
        compiler_params=pltpu.CompilerParams(vmem_limit_bytes=24 * MIB),
        cost_estimate=pl.CostEstimate(flops=2 * rows * width * 640, bytes_accessed=8 * MIB, transcendentals=0),
    )(stored, own, *units)


def group_kernel(*refs):
    row, own = refs[0], refs[1]
    units, out = refs[2:-1], refs[-1]
    out[...] = jnp.zeros_like(out)

    def left(columns):
        return jnp.broadcast_to(row[:, columns], (out.shape[1], row[:, columns].shape[1]))

    out[lax.axis_index("store")] = lax.dot_general(
        left(slice(None)), own[...], NT, preferred_element_type=jnp.float32
    )
    add_units(left, units, EARLY + MIDDLE, out)


def group_scores(row, own, units, panels):
    return pl.pallas_call(
        group_kernel,
        out_shape=jax.ShapeDtypeStruct((panels, 16, own.shape[0]), jnp.float32),
        compiler_params=pltpu.CompilerParams(vmem_limit_bytes=16 * MIB),
        cost_estimate=pl.CostEstimate(flops=1 << 28, bytes_accessed=8 * MIB, transcendentals=0),
    )(row, own, *units)


def late_kernel(query_owner, stored, row, early, group, *refs, scale):
    units, (out, group_out, totals, group_totals) = refs[:-4], refs[-4:]
    totals[...] = early[...]
    group_totals[...] = group[...]
    add_units(lambda columns: stored[:, columns], units, MIDDLE + LATE, totals)

    def left(columns):
        return jnp.broadcast_to(row[:, columns], (group.shape[1], row[:, columns].shape[1]))

    add_units(left, units[2 * len(MIDDLE) :], LATE, group_totals)
    for step in range(out.shape[0]):
        owner = query_owner[step]
        out[step] = totals[owner] * scale
        group_out[pl.ds(step, 1)] = group_totals[owner][:1] * scale


def late_scores(query_owner, stored, row, early, group, units, scale):
    vmem = pl.BlockSpec(memory_space=pltpu.VMEM)
    steps = query_owner.shape[0]
    _, rows, panel = early.shape
    return pl.pallas_call(
        functools.partial(late_kernel, scale=scale),
        in_specs=[pl.BlockSpec(memory_space=pltpu.SMEM)] + [vmem] * (4 + len(units)),
        out_shape=(
            jax.ShapeDtypeStruct((steps, rows, panel), jnp.float32),
            jax.ShapeDtypeStruct((steps, panel), jnp.float32),
        ),
        scratch_shapes=[pltpu.VMEM(early.shape, jnp.float32), pltpu.VMEM(group.shape, jnp.float32)],
        compiler_params=pltpu.CompilerParams(vmem_limit_bytes=24 * MIB),
        cost_estimate=pl.CostEstimate(flops=1 << 30, bytes_accessed=8 * MIB, transcendentals=0),
    )(query_owner, stored, row, early, group, *units)


def reduce_groups(partial):
    store, seq = lax.axis_index("store"), lax.axis_index("seq")
    z, x = store // 2, store % 2

    def halve(array, bit, way):
        send = lax.dynamic_index_in_dim(array, 1 - bit, 1, keepdims=False)
        keep = lax.dynamic_index_in_dim(array, bit, 1, keepdims=False)
        return keep + move(send, way, way)

    tail = partial.shape[1:]
    rows = halve(partial.reshape((4, 2) + tail), x, "X")
    rows = halve(rows.reshape((2, 2) + tail), z % 2, "S")
    row = halve(rows.reshape((1, 2) + tail), z // 2, "T")[0]
    row = row + move(row, "Y", "Y")
    return row + move(row, "C", "C", True)


def blocks(
    activations,
    out_grads,
    proj_in,
    proj_out,
    eig_out,
    eig_in,
    eig_values,
    lengths,
    owners,
    stored,
    queries,
    query_owner,
):
    seq = lax.axis_index("seq")
    seq_count, store_count = lax.axis_size("seq"), lax.axis_size("store")
    half = queries.shape[1] // 2
    got = [lax.dynamic_slice_in_dim(queries, ((seq // 2 + seq % 2) % 2) * half, half, 1)]
    partner = [None]
    for source, way0, way1, swap in STEPS:
        block = move(got[source], way0, way1, swap)
        got.append(block)
        partner.append(move(block, "C", "C", True))

    def units(steps):
        return [part[step] for step in steps for part in (got, partner)]

    factor = 1.0 / math.sqrt(activations.shape[2] * seq_count)
    partial = project(
        activations[0], out_grads[0], proj_in[0], proj_out[0], lengths, owners, factor, store_count
    )
    group = reduce_groups(partial)
    precond = precondition(group, eig_out[0], eig_in[0], eig_values[0])
    row = precond.reshape(1, -1)
    scale = 1.0 / math.sqrt(stored.shape[1])
    early = early_scores(stored, queries, units(EARLY), store_count)
    group_early = group_scores(row, queries, units(EARLY + MIDDLE), store_count)
    scores, group_out = late_scores(
        query_owner, stored, row, early, group_early, units(MIDDLE + LATE), scale
    )
    return scores, group_out[None]


def from_root(array, axis, root):
    mine = lax.axis_index(axis) == root
    return lax.psum(jnp.where(mine, array, jnp.zeros_like(array)), axis)


def precondition_rows(group, eig_out, eig_in, eig_values):
    row_count = group.shape[0]
    layers = eig_out.shape[0]
    rank = eig_out.shape[1]
    split = group.reshape(row_count, layers, rank, rank)
    rotated = jnp.einsum("lri,olrs->olis", eig_out, split, precision=HIGHEST)
    rotated = jnp.einsum("olis,lsj->olij", rotated, eig_in, precision=HIGHEST)
    scaled = rotated / eig_values[None]
    restored = jnp.einsum("lri,olij->olrj", eig_out, scaled, precision=HIGHEST)
    restored = jnp.einsum("olrj,lsj->olrs", restored, eig_in, precision=HIGHEST)
    return restored.reshape(row_count, layers * rank * rank).astype(jnp.bfloat16)


def project_layer(inputs, outgoing, weight_in, weight_out, valid, factor):
    in_side = jnp.einsum("etd,rd->etr", inputs, weight_in, preferred_element_type=jnp.float32)
    out_side = jnp.einsum("etd,rd->etr", outgoing, weight_out, preferred_element_type=jnp.float32)
    weighted = out_side * valid[:, :, None]
    outer = jnp.einsum("etr,ets->ers", weighted, in_side, precision=HIGHEST) * factor
    return outer.reshape(outer.shape[0], -1)


def owner_sums(owners, sources, count):
    owner_ids = jnp.arange(count, dtype=jnp.int32)
    select = (owners[None, :] == owner_ids[:, None]).astype(jnp.float32)
    return jnp.dot(select, sources, precision=HIGHEST)


def any_mesh(
    activations,
    out_grads,
    proj_in,
    proj_out,
    eig_out,
    eig_in,
    eig_values,
    lengths,
    owners,
    stored,
    queries,
    query_owner,
):
    seq_count = lax.axis_size("seq")
    seq_index = lax.axis_index("seq")
    local_len = activations.shape[2]
    positions = seq_index * local_len + jnp.arange(local_len, dtype=jnp.int32)
    valid = (positions[None, :] < lengths[:, None]).astype(jnp.float32)
    factor = jnp.float32(1.0 / math.sqrt(local_len * seq_count))
    partial_value = project_layer(activations[0], out_grads[0], proj_in[0], proj_out[0], valid, factor)
    summed = lax.psum(partial_value, "seq")
    owned_row = lax.psum_scatter(
        owner_sums(owners, summed, lax.axis_size("store")), "store", scatter_dimension=0, tiled=True
    )
    precond = precondition_rows(owned_row, eig_out, eig_in, eig_values)
    score_scale = jnp.float32(1.0 / math.sqrt(stored.shape[1]))
    stored_list = []
    group_list = []
    for step_index in range(query_owner.shape[0]):
        panel_rows = from_root(queries, "store", query_owner[step_index])
        stored_list.append(
            lax.dot_general(stored, panel_rows, NT, preferred_element_type=jnp.float32) * score_scale
        )
        group_list.append(
            lax.dot_general(precond, panel_rows, NT, preferred_element_type=jnp.float32) * score_scale
        )
    return (jnp.stack(stored_list, axis=0), jnp.stack(group_list, axis=1))


def solution(mesh):
    fits = mesh.shape["store"] == 8 and mesh.shape["seq"] == 4
    return jax.shard_map(
        blocks if fits else any_mesh,
        mesh=mesh,
        in_specs=(
            P(None, "store", "seq", None),
            P(None, "store", "seq", None),
            P(),
            P(),
            P(),
            P(),
            P(),
            P("store"),
            P("store"),
            P(("store", "seq"), None),
            P("store", None),
            P(),
        ),
        out_specs=(P(None, ("store", "seq"), None), P("store", None, None)),
        check_vma=False,
    )
```

time: 407 us -> 78.1 us (0.19)
  waiting for transfers between devices: 339 us -> 19.2 us
  matrix products: 26.9 us -> 0 us
  starting transfers between devices: 0.08 us -> 23 us
  Pallas kernels: 0 us -> 19.5 us
  between operations: 19.3 us -> 0.85 us
  blocking collectives: 11.2 us -> 0 us
  local copies, waits for them, and re-layouts: 4.4 us -> 14.9 us
  other arithmetic: 5.5 us -> 0.03 us
    psum x1 -> x0, waiting for transfers between devices: 281 us -> none  [from_root(): return lax.psum(jnp.where(mine, array, jnp.zeros_like(array)), axis)]
    unnamed x3 -> x0, waiting for transfers between devices: 57.9 us -> none
    dot_general x24 -> x0, matrix products: 26.9 us -> none  [the longest x8 12.1 us: shards(): lax.dot_general(stored, panel_rows, (((1,), (1,)), ((), ())), preferred_e...]
    ppermute x0 -> x19, starting transfers between devices: none -> 23 us  [move(): return lax.ppermute(array, AXES, pairs(way0, way1, swap))]
    pallas_call x0 -> x5, Pallas kernels: none -> 19.5 us  [the longest x1 5.31 us: early_scores(): pl.pallas_call(early_kernel, out_shape=jax.ShapeDtypeStruct((panels, rows...]
    ppermute x0 -> x19, waiting for transfers between devices: none -> 19.2 us  [move(): return lax.ppermute(array, AXES, pairs(way0, way1, swap))]
    psum x1 -> x0, blocking collectives: 11.2 us -> none  [shards(): summed = lax.psum(partial_value, 'seq')]
    unnamed x36, local copies, waits for them, and re-layouts: 2.86 us -> 13.7 us
  transfers between devices with their start and end apart: 2 -> 19, of which waited for: 2 -> 6; matrix products, arithmetic and copies ran while one was open for 2% -> 0% of each run, Pallas kernels for 0% -> 18%
where the time goes in v1:
time: 78.1 us; the launch traced here: 77.5 us
  starting transfers between devices  23 us (29%)
  Pallas kernels  19.5 us (25%)
  waiting for transfers between devices  19.2 us (25%)
  local copies, waits for them, and re-layouts  14.9 us (19%)
  between operations  0.85 us (1%)
    ppermute x19, starting transfers between devices, move(): return lax.ppermute(array, AXES, pairs(way0, way1, swap))  23 us
    ppermute x19, waiting for transfers between devices, move(): return lax.ppermute(array, AXES, pairs(way0, way1, swap))  19.2 us
    unnamed x36, local copies, waits for them, and re-layouts  13.7 us
    pallas_call x1, Pallas kernels, early_scores(): pl.pallas_call(early_kernel, out_shape=jax.ShapeDtypeStruct((panels, rows...  5.31 us
    pallas_call x1, Pallas kernels, late_scores(): pl.pallas_call(functools.partial(late_kernel, scale=scale), in_specs=[pl....  5.29 us
    pallas_call x1, Pallas kernels, project(): pl.pallas_call(functools.partial(project_kernel, factor=factor, owner_cou...  4.52 us
    pallas_call x1, Pallas kernels, group_scores(): pl.pallas_call(group_kernel, out_shape=jax.ShapeDtypeStruct((panels, 16,...  3.57 us
  transfers between devices with their start and end apart: 19, of which 6 were waited for; matrix products, arithmetic and copies ran while one was open for 0% of the time, Pallas kernels for 18%

profile of v1, /device:TPU:1, one launch (start us, length us, event | category | flops | bytes accessed | tf_op | source)
XLA Modules:
  0.0 77.5 jit_solution(5250855670397828792)
XLA Ops:
  0.7 1.1 %constant_dynamic-slice_fusion = bf16[128,2048]{1,0:T(8,128)(2,1)S(1)} fusion(bf16[128,4096]{1,0:T(8,128)(2,1)} %refs_1_.3, s32[]{:T(128)S(6)} %select_n.66), kind=kLoop, calls=%fused_computation.5 | loop fusion | bytes 1048580 | tf_op jit(solution)/shard_map/dynamic_slice | solution.py:308
  1.8 2.7 %collective-permute-start.5 = (bf16[128,2048]{1,0:T(8,128)(2,1)S(1)}, bf16[128,2048]{1,0:T(8,128)(2,1)}, u32[]{:S(2)}, u32[]{:S(2)}) collective-permute-start(bf16[128,2048]{1,0:T(8,128)(2,1)S(1)} %constant_dynamic-slice_fusion), channel_id=1, source_target_pairs={{0,17},{1,4},{2,19},{3,6},{4,21},{5,0},{6,23},{7,2},{8,1},{9,12},{... | collective-permute-start | bytes 1572872 | tf_op jit(solution)/shard_map/ppermute | solution.py:61
  4.4 2.2 %copy-done.2 = bf16[1,2,256,4096]{3,2,1,0:T(8,128)(2,1)S(1)} copy-done((bf16[1,2,256,4096]{3,2,1,0:T(8,128)(2,1)S(1)}, bf16[1,2,256,4096]{3,2,1,0:T(8,128)(2,1)}, u32[]{:S(2)}) %copy-start.2) | copy-done | bytes 4194328
  6.6 2.2 %copy-done.3 = bf16[1,2,256,4096]{3,2,1,0:T(8,128)(2,1)S(1)} copy-done((bf16[1,2,256,4096]{3,2,1,0:T(8,128)(2,1)S(1)}, bf16[1,2,256,4096]{3,2,1,0:T(8,128)(2,1)}, u32[]{:S(2)}) %copy-start.3) | copy-done | bytes 4194328
  8.8 1.0 %copy-done.10 = bf16[1,64,4096]{2,1,0:T(8,128)(2,1)S(1)} copy-done((bf16[1,64,4096]{2,1,0:T(8,128)(2,1)S(1)}, bf16[1,64,4096]{2,1,0:T(8,128)(2,1)}, u32[]{:S(2)}) %copy-start.10) | copy-done | bytes 524312
  9.8 1.0 %copy-done.11 = bf16[1,64,4096]{2,1,0:T(8,128)(2,1)S(1)} copy-done((bf16[1,64,4096]{2,1,0:T(8,128)(2,1)S(1)}, bf16[1,64,4096]{2,1,0:T(8,128)(2,1)}, u32[]{:S(2)}) %copy-start.11) | copy-done | bytes 524312
  10.9 0.7 copy-done.15
  11.5 0.7 copy-done.16
  12.2 4.5 %shard_map.131 = f32[8,32,128]{2,1,0:T(8,128)S(1)} custom-call(s32[2]{0:T(128)S(1)} %copy-done.15, s32[2]{0:T(128)S(1)} %copy-done.16, bf16[512,4096]{1,0:T(8,128)(2,1)S(1)} %bitcast.20, bf16[512,4096]{1,0:T(8,128)(2,1)S(1)} %bitcast.21, bf16[64,4096]{1,0:T(8,128)(2,1)S(1)} %bitcast.24, bf16[64,4096]{1,0:T(8,128)(2,1)S(1)} %bitcast.25), custom_call_target="tpu_custom_call" | custom-call | flops 536870912 | bytes 8388608 | tf_op jit(solution)/shard_map/pallas_call | solution.py:135
  16.7 0.0 collective-permute-done.5.refs_2_
  16.7 0.1 collective-permute-start.7
  16.8 1.4 %collective-permute-start = (f32[4,32,128]{2,1,0:T(8,128)S(1)}, f32[4,32,128]{2,1,0:T(8,128)S(1)}, u32[]{:S(2)}, u32[]{:S(2)}) collective-permute-start(f32[4,32,128]{2,1,0:T(8,128)S(1)} %dynamic-slice_bitcast_fusion), channel_id=1, source_target_pairs={{0,4},{1,5},{2,6},{3,7},{4,0},{5,1},{6,2},{7,3},{8,12},{9,13},{10,... | collective-permute-start | bytes 196616 | tf_op jit(solution)/shard_map/ppermute | solution.py:61
  18.3 1.2 %collective-permute-start.9 = (bf16[128,2048]{1,0:T(8,128)(2,1)}, bf16[128,2048]{1,0:T(8,128)(2,1)}, u32[]{:S(2)}, u32[]{:S(2)}) collective-permute-start(bf16[128,2048]{1,0:T(8,128)(2,1)} %collective-permute-done.5.refs_2_), channel_id=1, source_target_pairs={{0,2},{1,3},{2,0},{3,1},{4,6},{5,7},{6,4},{7,5},{8,10},{9,11},{10,... | collective-permute-start | bytes 1572872 | tf_op jit(solution)/shard_map/ppermute | solution.py:61
  19.5 7.3 %collective-permute-done = f32[4,32,128]{2,1,0:T(8,128)S(1)} collective-permute-done((f32[4,32,128]{2,1,0:T(8,128)S(1)}, f32[4,32,128]{2,1,0:T(8,128)S(1)}, u32[]{:S(2)}, u32[]{:S(2)}) %collective-permute-start) | collective-permute-done | bytes 65568 | tf_op jit(solution)/shard_map/ppermute | solution.py:61
  26.9 1.4 %collective-permute-start.1 = (f32[2,32,128]{2,1,0:T(8,128)S(1)}, f32[2,32,128]{2,1,0:T(8,128)S(1)}, u32[]{:S(2)}, u32[]{:S(2)}) collective-permute-start(f32[2,32,128]{2,1,0:T(8,128)S(1)} %dynamic-slice_bitcast_fusion.1), channel_id=1, source_target_pairs={{0,8},{1,9},{2,10},{3,11},{4,12},{5,13},{6,14},{7,15},{8,0},{9,1},... | collective-permute-start | bytes 98312 | tf_op jit(solution)/shard_map/ppermute | solution.py:61
  28.2 0.0 collective-permute-done.7.refs_4_
  28.2 2.3 %collective-permute-start.11 = (bf16[128,2048]{1,0:T(8,128)(2,1)S(1)}, bf16[128,2048]{1,0:T(8,128)(2,1)}, u32[]{:S(2)}, u32[]{:S(2)}) collective-permute-start(bf16[128,2048]{1,0:T(8,128)(2,1)S(1)} %collective-permute-done.7.refs_4_), channel_id=1, source_target_pairs={{0,4},{1,17},{2,6},{3,19},{4,0},{5,21},{6,2},{7,23},{8,12},{9,1},{... | collective-permute-start | bytes 1572872 | tf_op jit(solution)/shard_map/ppermute | solution.py:61
  30.5 0.0 collective-permute-done.1
  30.6 1.9 %collective-permute-start.2 = (f32[1,32,128]{2,1,0:T(8,128)S(1)}, f32[1,32,128]{2,1,0:T(8,128)S(1)}, u32[]{:S(2)}, u32[]{:S(2)}) collective-permute-start(f32[1,32,128]{2,1,0:T(8,128)S(1)} %constant_dynamic-slice_fusion.1), channel_id=1, source_target_pairs={{0,16},{1,17},{2,18},{3,19},{4,20},{5,21},{6,22},{7,23},{8,24},{9,... | collective-permute-start | bytes 49160 | tf_op jit(solution)/shard_map/ppermute | solution.py:61
  32.5 0.0 collective-permute-start.6
  32.5 0.0 collective-permute-done.9.refs_6_
  32.5 0.5 collective-permute-start.10
  33.0 5.3 %collective-permute-done.2 = f32[1,32,128]{2,1,0:T(8,128)S(1)} collective-permute-done((f32[1,32,128]{2,1,0:T(8,128)S(1)}, f32[1,32,128]{2,1,0:T(8,128)S(1)}, u32[]{:S(2)}, u32[]{:S(2)}) %collective-permute-start.2) | collective-permute-done | bytes 16416 | tf_op jit(solution)/shard_map/ppermute | solution.py:61
  38.3 1.2 %collective-permute-start.3 = (f32[32,128]{1,0:T(8,128)S(1)}, f32[32,128]{1,0:T(8,128)S(1)}, u32[]{:S(2)}, u32[]{:S(2)}) collective-permute-start(f32[32,128]{1,0:T(8,128)S(1)} %add_bitcast_fusion), channel_id=1, source_target_pairs={{0,2},{1,3},{2,0},{3,1},{4,6},{5,7},{6,4},{7,5},{8,10},{9,11},{10,... | collective-permute-start | bytes 49160 | tf_op jit(solution)/shard_map/ppermute | solution.py:61
  39.5 0.0 copy-done.4
  39.5 0.0 collective-permute-done.11.refs_8_
  39.5 0.3 collective-permute-start.13
  39.8 1.1 %collective-permute-done.3 = f32[32,128]{1,0:T(8,128)S(1)} collective-permute-done((f32[32,128]{1,0:T(8,128)S(1)}, f32[32,128]{1,0:T(8,128)S(1)}, u32[]{:S(2)}, u32[]{:S(2)}) %collective-permute-start.3) | collective-permute-done | bytes 16416 | tf_op jit(solution)/shard_map/ppermute | solution.py:61
  40.9 1.5 %collective-permute-start.4 = (f32[32,128]{1,0:T(8,128)S(1)}, f32[32,128]{1,0:T(8,128)S(1)}, u32[]{:S(2)}, u32[]{:S(2)}) collective-permute-start(f32[32,128]{1,0:T(8,128)S(1)} %add.72), channel_id=1, source_target_pairs={{0,1},{1,0},{2,3},{3,2},{4,5},{5,4},{6,7},{7,6},{8,9},{9,8},{10,11... | collective-permute-start | bytes 49160 | tf_op jit(solution)/shard_map/ppermute | solution.py:61
  42.5 0.2 collective-permute-start.17
  42.7 0.6 collective-permute-done.4
  43.3 1.2 %collective-permute-start.15 = (bf16[128,2048]{1,0:T(8,128)(2,1)}, bf16[128,2048]{1,0:T(8,128)(2,1)}, u32[]{:S(2)}, u32[]{:S(2)}) collective-permute-start(bf16[128,2048]{1,0:T(8,128)(2,1)} %collective-permute-done.11.refs_8_), channel_id=1, source_target_pairs={{0,2},{1,3},{2,0},{3,1},{4,6},{5,7},{6,4},{7,5},{8,10},{9,11},{10,... | collective-permute-start | bytes 1572872 | tf_op jit(solution)/shard_map/ppermute | solution.py:61
  44.5 0.0 collective-permute-done.6.refs_3_
  44.5 0.8 %copy-done.6 = bf16[128,2048]{1,0:T(8,128)(2,1)} copy-done((bf16[128,2048]{1,0:T(8,128)(2,1)}, bf16[128,2048]{1,0:T(8,128)(2,1)S(1)}, u32[]{:S(2)}) %copy-start.6) | copy-done | bytes 524312
  45.3 0.6 collective-permute-start.8
  45.9 0.0 collective-permute-done.10.refs_7_
  46.0 0.8 %copy-done.8 = bf16[128,2048]{1,0:T(8,128)(2,1)} copy-done((bf16[128,2048]{1,0:T(8,128)(2,1)}, bf16[128,2048]{1,0:T(8,128)(2,1)S(1)}, u32[]{:S(2)}) %copy-start.8) | copy-done | bytes 524312
  46.8 0.0 collective-permute-start.12
  46.8 1.4 %collective-permute-done.13.refs_10_.refs_0_ = bf16[128,2048]{1,0:T(8,128)(2,1)S(1)} collective-permute-done((bf16[128,2048]{1,0:T(8,128)(2,1)}, bf16[128,2048]{1,0:T(8,128)(2,1)S(1)}, u32[]{:S(2)}, u32[]{:S(2)}) %collective-permute-start.13) | collective-permute-done | bytes 524320 | tf_op jit(solution)/shard_map/ppermute | solution.py:61
  48.2 2.3 %collective-permute-start.14 = (bf16[128,2048]{1,0:T(8,128)(2,1)S(1)}, bf16[128,2048]{1,0:T(8,128)(2,1)}, u32[]{:S(2)}, u32[]{:S(2)}) collective-permute-start(bf16[128,2048]{1,0:T(8,128)(2,1)S(1)} %collective-permute-done.13.refs_10_.refs_0_), channel_id=1, source_target_pairs={{0,1},{1,0},{2,3},{3,2},{4,5},{5,4},{6,7},{7,6},{8,9},{9,8},{10,11... | collective-permute-start | bytes 1572872 | tf_op jit(solution)/shard_map/ppermute | solution.py:61
  50.5 3.3 %collective-permute-done.17.refs_4_ = bf16[128,2048]{1,0:T(8,128)(2,1)} collective-permute-done((bf16[128,2048]{1,0:T(8,128)(2,1)}, bf16[128,2048]{1,0:T(8,128)(2,1)}, u32[]{:S(2)}, u32[]{:S(2)}) %collective-permute-start.17) | collective-permute-done | bytes 524320 | tf_op jit(solution)/shard_map/ppermute | solution.py:61
  53.8 2.4 %collective-permute-start.18 = (bf16[128,2048]{1,0:T(8,128)(2,1)}, bf16[128,2048]{1,0:T(8,128)(2,1)}, u32[]{:S(2)}, u32[]{:S(2)}) collective-permute-start(bf16[128,2048]{1,0:T(8,128)(2,1)} %collective-permute-done.17.refs_4_), channel_id=1, source_target_pairs={{0,1},{1,0},{2,3},{3,2},{4,5},{5,4},{6,7},{7,6},{8,9},{9,8},{10,11... | collective-permute-start | bytes 1572872 | tf_op jit(solution)/shard_map/ppermute | solution.py:61
  56.2 0.0 collective-permute-done.15.refs_2_
  56.3 1.7 %collective-permute-start.16 = (bf16[128,2048]{1,0:T(8,128)(2,1)}, bf16[128,2048]{1,0:T(8,128)(2,1)}, u32[]{:S(2)}, u32[]{:S(2)}) collective-permute-start(bf16[128,2048]{1,0:T(8,128)(2,1)} %collective-permute-done.15.refs_2_), channel_id=1, source_target_pairs={{0,1},{1,0},{2,3},{3,2},{4,5},{5,4},{6,7},{7,6},{8,9},{9,8},{10,11... | collective-permute-start | bytes 1572872 | tf_op jit(solution)/shard_map/ppermute | solution.py:61
  58.0 0.0 copy-done.12
  58.0 0.0 copy-done.13
  58.0 0.0 copy-done.14
  58.0 0.8 %shard_map.132 = bf16[64,64]{1,0:T(8,128)(2,1)S(1)} custom-call(f32[32,128]{1,0:T(8,128)S(1)} %add.73.group, f32[64,64]{1,0:T(8,128)S(1)} %bitcast.26, f32[64,64]{1,0:T(8,128)S(1)} %bitcast.27, f32[64,64]{1,0:T(8,128)S(1)} %bitcast.28), custom_call_target="tpu_custom_call" | custom-call | flops 16777216 | bytes 131072 | tf_op jit(solution)/shard_map/pallas_call | solution.py:181
  58.8 0.1 reshape.20.refs_0_.row
  58.9 0.0 collective-permute-done.8.refs_5_
  58.9 0.0 collective-permute-done.12.refs_9_
  58.9 0.0 copy-start.1
  58.9 1.2 %copy-done.1 = bf16[128,4096]{1,0:T(8,128)(2,1)S(1)} copy-done((bf16[128,4096]{1,0:T(8,128)(2,1)S(1)}, bf16[128,4096]{1,0:T(8,128)(2,1)}, u32[]{:S(2)}) %copy-start.1) | copy-done | bytes 1048600
  60.1 1.0 %copy-done.5 = bf16[128,2048]{1,0:T(8,128)(2,1)S(1)} copy-done((bf16[128,2048]{1,0:T(8,128)(2,1)S(1)}, bf16[128,2048]{1,0:T(8,128)(2,1)}, u32[]{:S(2)}) %copy-start.5) | copy-done | bytes 524312
  61.2 1.0 %copy-done.7 = bf16[128,2048]{1,0:T(8,128)(2,1)S(1)} copy-done((bf16[128,2048]{1,0:T(8,128)(2,1)S(1)}, bf16[128,2048]{1,0:T(8,128)(2,1)}, u32[]{:S(2)}) %copy-start.7) | copy-done | bytes 524312
  62.2 1.0 %copy-done.9 = bf16[128,2048]{1,0:T(8,128)(2,1)S(1)} copy-done((bf16[128,2048]{1,0:T(8,128)(2,1)S(1)}, bf16[128,2048]{1,0:T(8,128)(2,1)}, u32[]{:S(2)}) %copy-start.9) | copy-done | bytes 524312
  63.2 5.3 %shard_map.133.early = f32[8,320,128]{2,1,0:T(8,128)S(1)} custom-call(bf16[320,4096]{1,0:T(8,128)(2,1)S(1)} %copy-done, bf16[128,4096]{1,0:T(8,128)(2,1)S(1)} %copy-done.1, bf16[128,2048]{1,0:T(8,128)(2,1)} %collective-permute-done.5.refs_2_, bf16[128,2048]{1,0:T(8,128)(2,1)S(1)} %copy-done.7, bf16[128,2048]{1,0:T(8,128)(2,1)S(1)} %copy-done.5, ...), custom_call_target="tpu_custom_call" | custom-call | flops 1677721600 | bytes 8388608 | tf_op jit(solution)/shard_map/pallas_call | solution.py:210
  68.6 0.0 copy-start.17
  68.6 0.0 collective-permute-done.14.refs_11_.refs_1_
  68.6 3.6 %shard_map.134.group = f32[8,16,128]{2,1,0:T(8,128)S(1)} custom-call(bf16[1,4096]{1,0:T(2,128)(2,1)S(1)} %reshape.20.refs_0_.row, bf16[128,4096]{1,0:T(8,128)(2,1)S(1)} %copy-done.1, bf16[128,2048]{1,0:T(8,128)(2,1)} %collective-permute-done.5.refs_2_, bf16[128,2048]{1,0:T(8,128)(2,1)S(1)} %copy-done.7, bf16[128,2048]{1,0:T(8,128)(2,1)S(1)} %copy-done.5, ...), custom_call_target="tpu_custom_call" | custom-call | flops 268435456 | bytes 8388608 | tf_op jit(solution)/shard_map/pallas_call | solution.py:233
  72.2 0.0 collective-permute-done.18.refs_5_
  72.2 0.0 collective-permute-done.16.refs_3_
  72.2 0.0 copy-done.17
  72.2 5.3 %shard_map.135 = (f32[8,320,128]{2,1,0:T(8,128)}, f32[8,128]{1,0:T(8,128)}) custom-call(s32[8]{0:T(128)S(1)} %copy-done.17, bf16[320,4096]{1,0:T(8,128)(2,1)S(1)} %copy-done, bf16[1,4096]{1,0:T(2,128)(2,1)S(1)} %reshape.20.refs_0_.row, f32[8,320,128]{2,1,0:T(8,128)S(1)} %shard_map.133.early, f32[8,16,128]{2,1,0:T(8,128)S(1)} %shard_map.134.group, ...), custom_call_target="tpu_custom_call" | custom-call | flops 1073741824 | bytes 8388608 | tf_op jit(solution)/shard_map/pallas_call | solution.py:261
  (25 shorter events, 0.1 us)
Async XLA Ops:
  1.8 15.0 %collective-permute-start.5 = (bf16[128,2048]{1,0:T(8,128)(2,1)S(1)}, bf16[128,2048]{1,0:T(8,128)(2,1)}, u32[]{:S(2)}, u32[]{:S(2)}) collective-permute-start(bf16[128,2048]{1,0:T(8,128)(2,1)S(1)} %constant_dynamic-slice_fusion), channel_id=1, source_target_pairs={{0,17},{1,4},{2,19},{3,6},{4,21},{5,0},{6,23},{7,2},{8,1},{9,12},{... | collective-permute-start | bytes 1572872 | tf_op jit(solution)/shard_map/ppermute | solution.py:61
  4.4 2.2 %copy-start.2 = (bf16[1,2,256,4096]{3,2,1,0:T(8,128)(2,1)S(1)}, bf16[1,2,256,4096]{3,2,1,0:T(8,128)(2,1)}, u32[]{:S(2)}) copy-start(bf16[1,2,256,4096]{3,2,1,0:T(8,128)(2,1)} %param.12) | copy-start | bytes 12582916
  6.6 2.2 %copy-start.3 = (bf16[1,2,256,4096]{3,2,1,0:T(8,128)(2,1)S(1)}, bf16[1,2,256,4096]{3,2,1,0:T(8,128)(2,1)}, u32[]{:S(2)}) copy-start(bf16[1,2,256,4096]{3,2,1,0:T(8,128)(2,1)} %param.13) | copy-start | bytes 12582916
  8.8 1.0 %copy-start.10 = (bf16[1,64,4096]{2,1,0:T(8,128)(2,1)S(1)}, bf16[1,64,4096]{2,1,0:T(8,128)(2,1)}, u32[]{:S(2)}) copy-start(bf16[1,64,4096]{2,1,0:T(8,128)(2,1)} %param.14) | copy-start | bytes 1572868
  9.8 1.0 %copy-start.11 = (bf16[1,64,4096]{2,1,0:T(8,128)(2,1)S(1)}, bf16[1,64,4096]{2,1,0:T(8,128)(2,1)}, u32[]{:S(2)}) copy-start(bf16[1,64,4096]{2,1,0:T(8,128)(2,1)} %param.15) | copy-start | bytes 1572868
  10.9 0.7 copy-start.15
  11.5 0.7 copy-start.16
  12.2 45.8 %copy-start.12 = (f32[1,64,64]{2,1,0:T(8,128)S(1)}, f32[1,64,64]{2,1,0:T(8,128)}, u32[]{:S(2)}) copy-start(f32[1,64,64]{2,1,0:T(8,128)} %param.16) | copy-start | bytes 49156
  12.2 45.8 %copy-start.13 = (f32[1,64,64]{2,1,0:T(8,128)S(1)}, f32[1,64,64]{2,1,0:T(8,128)}, u32[]{:S(2)}) copy-start(f32[1,64,64]{2,1,0:T(8,128)} %param.17) | copy-start | bytes 49156
  12.2 45.8 %copy-start.14 = (f32[1,64,64]{2,1,0:T(8,128)S(1)}, f32[1,64,64]{2,1,0:T(8,128)}, u32[]{:S(2)}) copy-start(f32[1,64,64]{2,1,0:T(8,128)} %param.18) | copy-start | bytes 49156
  12.2 46.7 %copy-start = (bf16[320,4096]{1,0:T(8,128)(2,1)S(1)}, bf16[320,4096]{1,0:T(8,128)(2,1)}, u32[]{:S(2)}) copy-start(bf16[320,4096]{1,0:T(8,128)(2,1)} %stored.1) | copy-start | bytes 7864324
  16.7 11.5 %collective-permute-start.7 = (bf16[128,2048]{1,0:T(8,128)(2,1)}, bf16[128,2048]{1,0:T(8,128)(2,1)S(1)}, u32[]{:S(2)}, u32[]{:S(2)}) collective-permute-start(bf16[128,2048]{1,0:T(8,128)(2,1)} %collective-permute-done.5.refs_2_), channel_id=1, source_target_pairs={{0,8},{1,5},{2,10},{3,7},{4,12},{5,1},{6,14},{7,3},{8,24},{9,13},{... | collective-permute-start | bytes 1572872 | tf_op jit(solution)/shard_map/ppermute | solution.py:61
  16.8 10.0 %collective-permute-start = (f32[4,32,128]{2,1,0:T(8,128)S(1)}, f32[4,32,128]{2,1,0:T(8,128)S(1)}, u32[]{:S(2)}, u32[]{:S(2)}) collective-permute-start(f32[4,32,128]{2,1,0:T(8,128)S(1)} %dynamic-slice_bitcast_fusion), channel_id=1, source_target_pairs={{0,4},{1,5},{2,6},{3,7},{4,0},{5,1},{6,2},{7,3},{8,12},{9,13},{10,... | collective-permute-start | bytes 196616 | tf_op jit(solution)/shard_map/ppermute | solution.py:61
  18.3 14.3 %collective-permute-start.9 = (bf16[128,2048]{1,0:T(8,128)(2,1)}, bf16[128,2048]{1,0:T(8,128)(2,1)}, u32[]{:S(2)}, u32[]{:S(2)}) collective-permute-start(bf16[128,2048]{1,0:T(8,128)(2,1)} %collective-permute-done.5.refs_2_), channel_id=1, source_target_pairs={{0,2},{1,3},{2,0},{3,1},{4,6},{5,7},{6,4},{7,5},{8,10},{9,11},{10,... | collective-permute-start | bytes 1572872 | tf_op jit(solution)/shard_map/ppermute | solution.py:61
  26.9 3.7 %collective-permute-start.1 = (f32[2,32,128]{2,1,0:T(8,128)S(1)}, f32[2,32,128]{2,1,0:T(8,128)S(1)}, u32[]{:S(2)}, u32[]{:S(2)}) collective-permute-start(f32[2,32,128]{2,1,0:T(8,128)S(1)} %dynamic-slice_bitcast_fusion.1), channel_id=1, source_target_pairs={{0,8},{1,9},{2,10},{3,11},{4,12},{5,13},{6,14},{7,15},{8,0},{9,1},... | collective-permute-start | bytes 98312 | tf_op jit(solution)/shard_map/ppermute | solution.py:61
  28.2 11.3 %copy-start.4 = (bf16[128,2048]{1,0:T(8,128)(2,1)}, bf16[128,2048]{1,0:T(8,128)(2,1)S(1)}, u32[]{:S(2)}) copy-start(bf16[128,2048]{1,0:T(8,128)(2,1)S(1)} %collective-permute-done.7.refs_4_) | copy-start | bytes 1572868
  28.2 11.3 %collective-permute-start.11 = (bf16[128,2048]{1,0:T(8,128)(2,1)S(1)}, bf16[128,2048]{1,0:T(8,128)(2,1)}, u32[]{:S(2)}, u32[]{:S(2)}) collective-permute-start(bf16[128,2048]{1,0:T(8,128)(2,1)S(1)} %collective-permute-done.7.refs_4_), channel_id=1, source_target_pairs={{0,4},{1,17},{2,6},{3,19},{4,0},{5,21},{6,2},{7,23},{8,12},{9,1},{... | collective-permute-start | bytes 1572872 | tf_op jit(solution)/shard_map/ppermute | solution.py:61
  30.6 7.8 %collective-permute-start.2 = (f32[1,32,128]{2,1,0:T(8,128)S(1)}, f32[1,32,128]{2,1,0:T(8,128)S(1)}, u32[]{:S(2)}, u32[]{:S(2)}) collective-permute-start(f32[1,32,128]{2,1,0:T(8,128)S(1)} %constant_dynamic-slice_fusion.1), channel_id=1, source_target_pairs={{0,16},{1,17},{2,18},{3,19},{4,20},{5,21},{6,22},{7,23},{8,24},{9,... | collective-permute-start | bytes 49160 | tf_op jit(solution)/shard_map/ppermute | solution.py:61
  32.5 12.0 %collective-permute-start.6 = (bf16[128,2048]{1,0:T(8,128)(2,1)}, bf16[128,2048]{1,0:T(8,128)(2,1)S(1)}, u32[]{:S(2)}, u32[]{:S(2)}) collective-permute-start(bf16[128,2048]{1,0:T(8,128)(2,1)} %collective-permute-done.5.refs_2_), channel_id=1, source_target_pairs={{0,1},{1,0},{2,3},{3,2},{4,5},{5,4},{6,7},{7,6},{8,9},{9,8},{10,11... | collective-permute-start | bytes 1572872 | tf_op jit(solution)/shard_map/ppermute | solution.py:61
  32.5 13.4 %collective-permute-start.10 = (bf16[128,2048]{1,0:T(8,128)(2,1)}, bf16[128,2048]{1,0:T(8,128)(2,1)S(1)}, u32[]{:S(2)}, u32[]{:S(2)}) collective-permute-start(bf16[128,2048]{1,0:T(8,128)(2,1)} %collective-permute-done.9.refs_6_), channel_id=1, source_target_pairs={{0,1},{1,0},{2,3},{3,2},{4,5},{5,4},{6,7},{7,6},{8,9},{9,8},{10,11... | collective-permute-start | bytes 1572872 | tf_op jit(solution)/shard_map/ppermute | solution.py:61
  38.3 2.6 %collective-permute-start.3 = (f32[32,128]{1,0:T(8,128)S(1)}, f32[32,128]{1,0:T(8,128)S(1)}, u32[]{:S(2)}, u32[]{:S(2)}) collective-permute-start(f32[32,128]{1,0:T(8,128)S(1)} %add_bitcast_fusion), channel_id=1, source_target_pairs={{0,2},{1,3},{2,0},{3,1},{4,6},{5,7},{6,4},{7,5},{8,10},{9,11},{10,... | collective-permute-start | bytes 49160 | tf_op jit(solution)/shard_map/ppermute | solution.py:61
  39.5 8.6 %collective-permute-start.13 = (bf16[128,2048]{1,0:T(8,128)(2,1)}, bf16[128,2048]{1,0:T(8,128)(2,1)S(1)}, u32[]{:S(2)}, u32[]{:S(2)}) collective-permute-start(bf16[128,2048]{1,0:T(8,128)(2,1)} %collective-permute-done.11.refs_8_), channel_id=1, source_target_pairs={{0,8},{1,5},{2,10},{3,7},{4,12},{5,1},{6,14},{7,3},{8,24},{9,13},{... | collective-permute-start | bytes 1572872 | tf_op jit(solution)/shard_map/ppermute | solution.py:61
  40.9 2.4 %collective-permute-start.4 = (f32[32,128]{1,0:T(8,128)S(1)}, f32[32,128]{1,0:T(8,128)S(1)}, u32[]{:S(2)}, u32[]{:S(2)}) collective-permute-start(f32[32,128]{1,0:T(8,128)S(1)} %add.72), channel_id=1, source_target_pairs={{0,1},{1,0},{2,3},{3,2},{4,5},{5,4},{6,7},{7,6},{8,9},{9,8},{10,11... | collective-permute-start | bytes 49160 | tf_op jit(solution)/shard_map/ppermute | solution.py:61
  42.5 11.3 %collective-permute-start.17 = (bf16[128,2048]{1,0:T(8,128)(2,1)}, bf16[128,2048]{1,0:T(8,128)(2,1)}, u32[]{:S(2)}, u32[]{:S(2)}) collective-permute-start(bf16[128,2048]{1,0:T(8,128)(2,1)} %collective-permute-done.9.refs_6_), channel_id=1, source_target_pairs={{0,8},{1,5},{2,10},{3,7},{4,12},{5,1},{6,14},{7,3},{8,24},{9,13},{... | collective-permute-start | bytes 1572872 | tf_op jit(solution)/shard_map/ppermute | solution.py:61
  43.3 13.0 %collective-permute-start.15 = (bf16[128,2048]{1,0:T(8,128)(2,1)}, bf16[128,2048]{1,0:T(8,128)(2,1)}, u32[]{:S(2)}, u32[]{:S(2)}) collective-permute-start(bf16[128,2048]{1,0:T(8,128)(2,1)} %collective-permute-done.11.refs_8_), channel_id=1, source_target_pairs={{0,2},{1,3},{2,0},{3,1},{4,6},{5,7},{6,4},{7,5},{8,10},{9,11},{10,... | collective-permute-start | bytes 1572872 | tf_op jit(solution)/shard_map/ppermute | solution.py:61
  44.5 0.8 %copy-start.6 = (bf16[128,2048]{1,0:T(8,128)(2,1)}, bf16[128,2048]{1,0:T(8,128)(2,1)S(1)}, u32[]{:S(2)}) copy-start(bf16[128,2048]{1,0:T(8,128)(2,1)S(1)} %collective-permute-done.6.refs_3_) | copy-start | bytes 1572868
  45.3 13.5 %collective-permute-start.8 = (bf16[128,2048]{1,0:T(8,128)(2,1)}, bf16[128,2048]{1,0:T(8,128)(2,1)}, u32[]{:S(2)}, u32[]{:S(2)}) collective-permute-start(bf16[128,2048]{1,0:T(8,128)(2,1)} %copy-done.4), channel_id=1, source_target_pairs={{0,1},{1,0},{2,3},{3,2},{4,5},{5,4},{6,7},{7,6},{8,9},{9,8},{10,11... | collective-permute-start | bytes 1572872 | tf_op jit(solution)/shard_map/ppermute | solution.py:61
  45.9 0.8 %copy-start.8 = (bf16[128,2048]{1,0:T(8,128)(2,1)}, bf16[128,2048]{1,0:T(8,128)(2,1)S(1)}, u32[]{:S(2)}) copy-start(bf16[128,2048]{1,0:T(8,128)(2,1)S(1)} %collective-permute-done.10.refs_7_) | copy-start | bytes 1572868
  46.8 12.1 %collective-permute-start.12 = (bf16[128,2048]{1,0:T(8,128)(2,1)}, bf16[128,2048]{1,0:T(8,128)(2,1)}, u32[]{:S(2)}, u32[]{:S(2)}) collective-permute-start(bf16[128,2048]{1,0:T(8,128)(2,1)} %collective-permute-done.11.refs_8_), channel_id=1, source_target_pairs={{0,1},{1,0},{2,3},{3,2},{4,5},{5,4},{6,7},{7,6},{8,9},{9,8},{10,11... | collective-permute-start | bytes 1572872 | tf_op jit(solution)/shard_map/ppermute | solution.py:61
  48.2 20.4 %collective-permute-start.14 = (bf16[128,2048]{1,0:T(8,128)(2,1)S(1)}, bf16[128,2048]{1,0:T(8,128)(2,1)}, u32[]{:S(2)}, u32[]{:S(2)}) collective-permute-start(bf16[128,2048]{1,0:T(8,128)(2,1)S(1)} %collective-permute-done.13.refs_10_.refs_0_), channel_id=1, source_target_pairs={{0,1},{1,0},{2,3},{3,2},{4,5},{5,4},{6,7},{7,6},{8,9},{9,8},{10,11... | collective-permute-start | bytes 1572872 | tf_op jit(solution)/shard_map/ppermute | solution.py:61
  53.8 18.4 %collective-permute-start.18 = (bf16[128,2048]{1,0:T(8,128)(2,1)}, bf16[128,2048]{1,0:T(8,128)(2,1)}, u32[]{:S(2)}, u32[]{:S(2)}) collective-permute-start(bf16[128,2048]{1,0:T(8,128)(2,1)} %collective-permute-done.17.refs_4_), channel_id=1, source_target_pairs={{0,1},{1,0},{2,3},{3,2},{4,5},{5,4},{6,7},{7,6},{8,9},{9,8},{10,11... | collective-permute-start | bytes 1572872 | tf_op jit(solution)/shard_map/ppermute | solution.py:61
  56.3 15.9 %collective-permute-start.16 = (bf16[128,2048]{1,0:T(8,128)(2,1)}, bf16[128,2048]{1,0:T(8,128)(2,1)}, u32[]{:S(2)}, u32[]{:S(2)}) collective-permute-start(bf16[128,2048]{1,0:T(8,128)(2,1)} %collective-permute-done.15.refs_2_), channel_id=1, source_target_pairs={{0,1},{1,0},{2,3},{3,2},{4,5},{5,4},{6,7},{7,6},{8,9},{9,8},{10,11... | collective-permute-start | bytes 1572872 | tf_op jit(solution)/shard_map/ppermute | solution.py:61
  58.9 1.2 %copy-start.1 = (bf16[128,4096]{1,0:T(8,128)(2,1)S(1)}, bf16[128,4096]{1,0:T(8,128)(2,1)}, u32[]{:S(2)}) copy-start(bf16[128,4096]{1,0:T(8,128)(2,1)} %refs_1_.3) | copy-start | bytes 3145732
  60.1 1.0 %copy-start.5 = (bf16[128,2048]{1,0:T(8,128)(2,1)S(1)}, bf16[128,2048]{1,0:T(8,128)(2,1)}, u32[]{:S(2)}) copy-start(bf16[128,2048]{1,0:T(8,128)(2,1)} %copy-done.4) | copy-start | bytes 1572868
  61.2 1.0 %copy-start.7 = (bf16[128,2048]{1,0:T(8,128)(2,1)S(1)}, bf16[128,2048]{1,0:T(8,128)(2,1)}, u32[]{:S(2)}) copy-start(bf16[128,2048]{1,0:T(8,128)(2,1)} %copy-done.6) | copy-start | bytes 1572868
  62.2 1.0 %copy-start.9 = (bf16[128,2048]{1,0:T(8,128)(2,1)S(1)}, bf16[128,2048]{1,0:T(8,128)(2,1)}, u32[]{:S(2)}) copy-start(bf16[128,2048]{1,0:T(8,128)(2,1)} %copy-done.8) | copy-start | bytes 1572868
  68.6 3.6 %copy-start.17 = (s32[8]{0:T(128)S(1)}, s32[8]{0:T(128)}, u32[]{:S(2)}) copy-start(s32[8]{0:T(128)} %query_owner.1) | copy-start | bytes 100

commit v2 on v1

v2 whole, which is shorter than its diff:
```python
import functools
import math

import jax
import jax.numpy as jnp
from jax import lax
from jax.experimental import pallas as pl
from jax.experimental.pallas import tpu as pltpu
from jax.sharding import PartitionSpec as P

AXES = ("store", "seq")
HIGHEST = lax.Precision.HIGHEST
NT = (((1,), (1,)), ((), ()))
MIB = 1 << 20
FIRST_MIB = 20

STEPS = (
    (0, "W", "X", True),
    (1, "Z", "X", False),
    (1, "Y", "Y", False),
    (2, "X", "W", False),
    (4, "Z", "X", False),
    (4, "Y", "Y", False),
    (3, "Z", "X", False),
)

FIRST = (((1, False), None), ((1, True), None))
SECOND = (((2, False), (4, False)), ((2, True), (4, True)))
THIRD = (((3, False), (5, True)), ((3, True), (5, False)))
LAST = (((6, False), (7, False)), ((6, True), (7, True)))


def ring_place(z):
    return z ^ (z >> 1)


def neighbour(way, z, x, y):
    if way == "X":
        return z, 1 - x, y
    if way == "Y":
        return z, x, 1 - y
    if way == "Z":
        return ring_place((ring_place(z) + 1) % 4), x, y
    if way == "W":
        return ring_place((ring_place(z) + 3) % 4), x, y
    if way == "S":
        return z ^ 1, x, y
    if way == "T":
        return z ^ 2, x, y
    if way == "V":
        return z ^ 3, x, y
    if way == "XY":
        return z, 1 - x, 1 - y
    return z, x, y
EARLY = FIRST + SECOND


def pairs(way0, way1, swap):
    out = []
    for z in range(4):
        for x in range(2):
            for y in range(2):
                for core in range(2):
                    z2, x2, y2 = neighbour(way1 if core else way0, z, x, y)
                    core2 = 1 - core if swap else core
                    out.append(((z * 2 + x) * 4 + y * 2 + core, (z2 * 2 + x2) * 4 + y2 * 2 + core2))
    return out


def move(array, way0, way1, swap=False):
    return lax.ppermute(array, AXES, pairs(way0, way1, swap))


def contents():
    have = [((0, 0, 0), (0, 0, 1))]
    for source, way0, way1, swap in STEPS:
        got = [None, None]
        for core, way in ((0, way0), (1, way1)):
            ring, across, half = have[source][core]
            if way == "X":
                across = 1 - across
            elif way == "Y":
                half = 1 - half
            elif way == "Z":
                ring = (ring + 1) % 4
            elif way == "W":
                ring = (ring + 3) % 4
            got[1 - core if swap else core] = (ring, across, half)
        have.append(tuple(got))
    return have


CONTENTS = contents()


def check_pairs():
    seen = [(0, 0, 0), (0, 0, 1)]
    for first, second in FIRST + SECOND + THIRD + LAST:
        for core in range(2):
            one = CONTENTS[first[0]][core ^ first[1]]
            seen.append(one)
            if second is not None:
                two = CONTENTS[second[0]][core ^ second[1]]
                seen.append(two)
                assert one[2] == two[2]
    assert len(set(seen)) == 16


check_pairs()


def unit_place(step, partner, store, seq):
    y, core = seq // 2, seq % 2
    z, x = store // 2, store % 2
    first, second = CONTENTS[step]
    mine = core if not partner else 1 - core
    pick = [jnp.where(mine == 0, a, b) for a, b in zip(first, second, strict=True)]
    place = (ring_place(z) + 4 - pick[0]) % 4
    return ring_place(place) * 2 + (x ^ pick[1]), pick[2] ^ y


def outer_kernel(lengths, owners, in_side, out_side, out, *, factor):
    examples, _, tokens = in_side.shape
    start = lax.axis_index("seq") * tokens
    sums = []
    for e in range(examples):
        outgoing = out_side[e]
        positions = start + lax.broadcasted_iota(jnp.int32, outgoing.shape, 1)
        outgoing = jnp.where(positions < lengths[e], outgoing, 0.0)
        block = lax.dot_general(outgoing, in_side[e], NT, precision=HIGHEST, preferred_element_type=jnp.float32)
        half = block.shape[0] // 2
        sums.append(jnp.concatenate([block[:half], block[half:]], axis=1) * factor)
    for owner in range(out.shape[0]):
        acc = jnp.zeros_like(sums[0])
        for e in range(examples):
            acc += jnp.where(owners[e] == owner, sums[e], 0.0)
        out[owner] = acc


def project(acts, grads, weight_in, weight_out, lengths, owners, factor, owner_count):
    in_side = jnp.einsum("rd,etd->ert", weight_in, acts, preferred_element_type=jnp.float32)
    out_side = jnp.einsum("rd,etd->ert", weight_out, grads, preferred_element_type=jnp.float32)
    rank = weight_in.shape[0]
    smem, vmem = pl.BlockSpec(memory_space=pltpu.SMEM), pl.BlockSpec(memory_space=pltpu.VMEM)
    return pl.pallas_call(
        functools.partial(outer_kernel, factor=factor),
        in_specs=[smem, smem, vmem, vmem],
        out_specs=vmem,
        out_shape=jax.ShapeDtypeStruct((owner_count, rank // 2, rank * 2), jnp.float32),
        compiler_params=pltpu.CompilerParams(vmem_limit_bytes=4 * MIB),
        cost_estimate=pl.CostEstimate(flops=1 << 26, bytes_accessed=1 << 19, transcendentals=0),
    )(lengths, owners, in_side, out_side)


def precondition_kernel(group, eig_out, eig_in, eig_values, out):
    rank = eig_out.shape[0]
    packed = group[...]
    block = jnp.concatenate([packed[:, :rank], packed[:, rank:]], axis=0)
    dot = functools.partial(lax.dot_general, precision=HIGHEST, preferred_element_type=jnp.float32)
    basis_out, basis_in = eig_out[...], eig_in[...]
    rotated = dot(basis_out, block, (((0,), (0,)), ((), ())))
    rotated = dot(rotated, basis_in, (((1,), (0,)), ((), ())))
    scaled = rotated / eig_values[...]
    restored = dot(basis_out, scaled, (((1,), (0,)), ((), ())))
    restored = dot(restored, basis_in, NT)
    out[...] = restored.astype(jnp.bfloat16)


def precondition(group, eig_out, eig_in, eig_values):
    rank = eig_out.shape[0]
    return pl.pallas_call(
        precondition_kernel,
        out_shape=jax.ShapeDtypeStruct((rank, rank), jnp.bfloat16),
        compiler_params=pltpu.CompilerParams(vmem_limit_bytes=4 * MIB),
        cost_estimate=pl.CostEstimate(flops=1 << 24, bytes_accessed=1 << 17, transcendentals=0),
    )(group, eig_out, eig_in, eig_values)


def add_scores(left, own, blocks, names, totals, scale):
    store, seq = lax.axis_index("store"), lax.axis_index("seq")
    for first, second in names:
        panel, half = unit_place(*first, store, seq)
        block = next(blocks)
        rows, width = block.shape
        columns = pl.ds(pl.multiple_of(half * width, width), width)
        if second is None:
            other_panel, other = store, own[:, columns]
        else:
            other_panel, other = unit_place(*second, store, seq)[0], next(blocks)
        product = lax.dot_general(
            left[:, columns], jnp.concatenate([block, other], axis=0), NT, preferred_element_type=jnp.float32
        )
        totals[panel] += product[:, :rows] * scale
        totals[other_panel] += product[:, rows:] * scale


def brought(units, buffer, sems):
    copies = [pltpu.make_async_copy(unit, buffer.at[n], sems.at[n]) for n, unit in enumerate(units)]
    for copy in copies:
        copy.start()

    def each():
        for n, copy in enumerate(copies):
            copy.wait()
            yield buffer[n]

    return each()


def first_kernel(stored, row, own, *refs, names, scale):
    units, (left, totals, token, buffer, sems, own_buffer, own_sems) = refs[:-7], refs[-7:]
    rows = stored.shape[0]
    copies = (
        pltpu.make_async_copy(stored, left.at[pl.ds(0, rows)], own_sems.at[0]),
        pltpu.make_async_copy(own, own_buffer, own_sems.at[1]),
    )
    for copy in copies:
        copy.start()
    blocks = brought(units, buffer, sems)
    token[...] = jnp.zeros_like(token)
    left[rows:] = jnp.broadcast_to(row[...], (left.shape[0] - rows, row.shape[1]))
    totals[...] = jnp.zeros_like(totals)
    for copy in copies:
        copy.wait()
    add_scores(left, own_buffer, blocks, names, totals, scale)


def first_scores(stored, row, own, units, names, scale, panels):
    vmem, anywhere = pl.BlockSpec(memory_space=pltpu.VMEM), pl.BlockSpec(memory_space=pl.ANY)
    rows, width = stored.shape
    panel = own.shape[0]
    return pl.pallas_call(
        functools.partial(first_kernel, names=names, scale=scale),
        in_specs=[anywhere, vmem, anywhere] + [anywhere] * len(units),
        out_specs=(vmem, vmem, vmem),
        out_shape=(
            jax.ShapeDtypeStruct((rows + 16, width), jnp.bfloat16),
            jax.ShapeDtypeStruct((panels, rows + 16, panel), jnp.float32),
            jax.ShapeDtypeStruct((8, 128), jnp.float32),
        ),
        scratch_shapes=[
            pltpu.VMEM((len(units),) + units[0].shape, jnp.bfloat16),
            pltpu.SemaphoreType.DMA((len(units),)),
            pltpu.VMEM(own.shape, jnp.bfloat16),
            pltpu.SemaphoreType.DMA((2,)),
        ],
        compiler_params=pltpu.CompilerParams(vmem_limit_bytes=FIRST_MIB * MIB),
        cost_estimate=pl.CostEstimate(flops=1 << 31, bytes_accessed=4 * MIB, transcendentals=0),
    )(stored, row, own, *units)


def next_kernel(left, before, *refs, names, scale):
    units, (totals, buffer, sems) = refs[:-3], refs[-3:]
    blocks = brought(units, buffer, sems)
    totals[...] = before[...]
    add_scores(left, None, blocks, names, totals, scale)


def next_scores(left, before, units, names, scale):
    vmem, anywhere = pl.BlockSpec(memory_space=pltpu.VMEM), pl.BlockSpec(memory_space=pl.ANY)
    return pl.pallas_call(
        functools.partial(next_kernel, names=names, scale=scale),
        in_specs=[vmem, vmem] + [anywhere] * len(units),
        out_specs=vmem,
        out_shape=jax.ShapeDtypeStruct(before.shape, jnp.float32),
        scratch_shapes=[
            pltpu.VMEM((len(units),) + units[0].shape, jnp.bfloat16),
            pltpu.SemaphoreType.DMA((len(units),)),
        ],
        compiler_params=pltpu.CompilerParams(vmem_limit_bytes=8 * MIB),
        cost_estimate=pl.CostEstimate(flops=1 << 30, bytes_accessed=2 * MIB, transcendentals=0),
    )(left, before, *units)


def last_kernel(query_owner, left, before, *refs, names, scale):
    units, (out, group_out, totals, sems) = refs[:-4], refs[-4:]
    rows = out.shape[1]
    totals[...] = before[...]
    add_scores(left, None, iter([unit[...] for unit in units]), names, totals, scale)
    copies = []
    for step in range(out.shape[0]):
        owner = query_owner[step]
        copies.append(pltpu.make_async_copy(totals.at[owner, pl.ds(0, rows)], out.at[step], sems.at[step]))
        copies[-1].start()
        group_out[pl.ds(step, 1)] = totals[owner, rows : rows + 1]
    for copy in copies:
        copy.wait()


def last_scores(query_owner, left, before, units, names, scale):
    vmem, anywhere = pl.BlockSpec(memory_space=pltpu.VMEM), pl.BlockSpec(memory_space=pl.ANY)
    steps = query_owner.shape[0]
    _, rows, panel = before.shape
    return pl.pallas_call(
        functools.partial(last_kernel, names=names, scale=scale),
        in_specs=[pl.BlockSpec(memory_space=pltpu.SMEM)] + [vmem] * (2 + len(units)),
        out_specs=(anywhere, vmem),
        out_shape=(
            jax.ShapeDtypeStruct((steps, rows - 16, panel), jnp.float32),
            jax.ShapeDtypeStruct((steps, panel), jnp.float32),
        ),
        scratch_shapes=[pltpu.VMEM(before.shape, jnp.float32), pltpu.SemaphoreType.DMA((steps,))],
        compiler_params=pltpu.CompilerParams(vmem_limit_bytes=8 * MIB),
        cost_estimate=pl.CostEstimate(flops=1 << 30, bytes_accessed=8 * MIB, transcendentals=0),
    )(query_owner, left, before, *units)


def gate_kernel(block, *refs):
    del block, refs


def gate(block, *others):
    vmem, anywhere = pl.BlockSpec(memory_space=pltpu.VMEM), pl.BlockSpec(memory_space=pl.ANY)
    return pl.pallas_call(
        gate_kernel,
        in_specs=[anywhere] + [vmem if other.dtype == jnp.float32 else anywhere for other in others],
        out_specs=anywhere,
        out_shape=jax.ShapeDtypeStruct(block.shape, block.dtype),
        input_output_aliases={0: 0},
        compiler_params=pltpu.CompilerParams(vmem_limit_bytes=MIB),
        cost_estimate=pl.CostEstimate(flops=0, bytes_accessed=0, transcendentals=0),
    )(block, *others)


def plane_kernel(rows, sent, *refs):
    received, (kept, *sends) = refs[:3], refs[-4:]
    del sent
    store = lax.axis_index("store")
    z, x = store // 2, store % 2
    for place in range(rows.shape[0] // 2):
        kept[place] = rows[2 * place + x] + received[0][place] + received[1][place] + received[2][place]
    for bits, send in enumerate(sends):
        send[0] = kept[z ^ (bits + 1)]


def sum_plane(rows, others, *tokens):
    vmem, anywhere = pl.BlockSpec(memory_space=pltpu.VMEM), pl.BlockSpec(memory_space=pl.ANY)
    keep, send = others
    came = (move(send, "X", "X"), move(keep, "Y", "Y"), move(send, "XY", "XY"))
    count, tail = keep.shape[0], keep.shape[1:]
    return pl.pallas_call(
        plane_kernel,
        in_specs=[vmem] * 5 + [anywhere] * len(tokens),
        out_specs=[vmem] * 4,
        out_shape=[jax.ShapeDtypeStruct((count,) + tail, jnp.float32)]
        + [jax.ShapeDtypeStruct((1,) + tail, jnp.float32)] * 3,
        compiler_params=pltpu.CompilerParams(vmem_limit_bytes=4 * MIB),
        cost_estimate=pl.CostEstimate(flops=1 << 16, bytes_accessed=1 << 18, transcendentals=0),
    )(rows, send, *came, *tokens)


def line_kernel(rows, *refs):
    out = refs[-1]
    out[...] = rows[lax.axis_index("store") // 2] + refs[0][0] + refs[1][0] + refs[2][0]


def sum_line(rows, sends, *tokens):
    vmem, anywhere = pl.BlockSpec(memory_space=pltpu.VMEM), pl.BlockSpec(memory_space=pl.ANY)
    came = [move(send, way, way) for way, send in zip("STV", sends, strict=True)]
    return pl.pallas_call(
        line_kernel,
        in_specs=[vmem] * 4 + [anywhere] * len(tokens),
        out_specs=vmem,
        out_shape=jax.ShapeDtypeStruct(rows.shape[1:], jnp.float32),
        compiler_params=pltpu.CompilerParams(vmem_limit_bytes=4 * MIB),
        cost_estimate=pl.CostEstimate(flops=1 << 16, bytes_accessed=1 << 18, transcendentals=0),
    )(rows, *came, *tokens)


def split_kernel(rows, other, total, keep, send):
    x = lax.axis_index("store") % 2
    total[...] = rows[...] + other[...]
    for place in range(keep.shape[0]):
        keep[place] = total[2 * place + x]
        send[place] = total[2 * place + 1 - x]


def sum_cores(rows):
    vmem = pl.BlockSpec(memory_space=pltpu.VMEM)
    count, tail = rows.shape[0], rows.shape[1:]
    part = jax.ShapeDtypeStruct((count // 2,) + tail, jnp.float32)
    return pl.pallas_call(
        split_kernel,
        in_specs=[vmem] * 2,
        out_specs=[vmem] * 3,
        out_shape=[jax.ShapeDtypeStruct(rows.shape, jnp.float32), part, part],
        compiler_params=pltpu.CompilerParams(vmem_limit_bytes=4 * MIB),
        cost_estimate=pl.CostEstimate(flops=1 << 16, bytes_accessed=1 << 18, transcendentals=0),
    )(rows, move(rows, "C", "C", True))


def blocks(
    activations,
    out_grads,
    proj_in,
    proj_out,
    eig_out,
    eig_in,
    eig_values,
    lengths,
    owners,
    stored,
    queries,
    query_owner,
):
    seq = lax.axis_index("seq")
    seq_count, store_count = lax.axis_size("seq"), lax.axis_size("store")
    half = queries.shape[1] // 2
    got = {0: lax.dynamic_slice_in_dim(queries, ((seq // 2 + seq % 2) % 2) * half, half, 1)}
    partner = {}
    scale = 1.0 / math.sqrt(stored.shape[1])
    factor = 1.0 / math.sqrt(activations.shape[2] * seq_count)

    def step(number, part=None):
        source, way0, way1, swap = STEPS[number - 1]
        if part is None:
            got[number] = move(got[source], way0, way1, swap)
        else:
            width = half // 2
            got[number, part] = move(got[source][:, part * width : (part + 1) * width], way0, way1, swap)

    def swap(*numbers):
        for number in numbers:
            partner[number] = move(got[number], "C", "C", True)

    def pick(names):
        return [(partner if name[1] else got)[name[0]] for pair in names for name in pair if name is not None]

    def after(number, *others):
        got[number] = gate(got[number], *others)

    step(1)
    partial = project(
        activations[0], out_grads[0], proj_in[0], proj_out[0], lengths, owners, factor, store_count
    )
    after(1, partial)
    step(2)
    step(3, 0)
    swap(1)
    rows, *others = sum_cores(partial)
    rows, *others = sum_plane(rows, others, got[2])
    after(2, got[3, 0])
    step(4)
    step(3, 1)
    swap(2)
    row = sum_line(rows, others, got[4])
    after(4, got[3, 1])
    step(5)
    step(6, 0)
    swap(4)
    precond = precondition(row, eig_out[0], eig_in[0], eig_values[0]).reshape(1, -1)
    left, total, token = first_scores(stored, precond, queries, pick(EARLY), EARLY, scale, store_count)
    got[3] = jnp.concatenate([got[3, 0], got[3, 1]], axis=1)
    after(3, token, got[6, 0])
    step(7)
    step(6, 1)
    swap(3, 5)
    total = next_scores(left, total, pick(THIRD), THIRD, scale)
    got[6] = jnp.concatenate([got[6, 0], got[6, 1]], axis=1)
    swap(6, 7)
    scores, group_out = last_scores(query_owner, left, total, pick(LAST), LAST, scale)
    return scores, group_out[None]


def from_root(array, axis, root):
    mine = lax.axis_index(axis) == root
    return lax.psum(jnp.where(mine, array, jnp.zeros_like(array)), axis)


def precondition_rows(group, eig_out, eig_in, eig_values):
    row_count = group.shape[0]
    layers = eig_out.shape[0]
    rank = eig_out.shape[1]
    split = group.reshape(row_count, layers, rank, rank)
    rotated = jnp.einsum("lri,olrs->olis", eig_out, split, precision=HIGHEST)
    rotated = jnp.einsum("olis,lsj->olij", rotated, eig_in, precision=HIGHEST)
    scaled = rotated / eig_values[None]
    restored = jnp.einsum("lri,olij->olrj", eig_out, scaled, precision=HIGHEST)
    restored = jnp.einsum("olrj,lsj->olrs", restored, eig_in, precision=HIGHEST)
    return restored.reshape(row_count, layers * rank * rank).astype(jnp.bfloat16)


def project_layer(inputs, outgoing, weight_in, weight_out, valid, factor):
    in_side = jnp.einsum("etd,rd->etr", inputs, weight_in, preferred_element_type=jnp.float32)
    out_side = jnp.einsum("etd,rd->etr", outgoing, weight_out, preferred_element_type=jnp.float32)
    weighted = out_side * valid[:, :, None]
    outer = jnp.einsum("etr,ets->ers", weighted, in_side, precision=HIGHEST) * factor
    return outer.reshape(outer.shape[0], -1)


def owner_sums(owners, sources, count):
    owner_ids = jnp.arange(count, dtype=jnp.int32)
    select = (owners[None, :] == owner_ids[:, None]).astype(jnp.float32)
    return jnp.dot(select, sources, precision=HIGHEST)


def any_mesh(
    activations,
    out_grads,
    proj_in,
    proj_out,
    eig_out,
    eig_in,
    eig_values,
    lengths,
    owners,
    stored,
    queries,
    query_owner,
):
    seq_count = lax.axis_size("seq")
    seq_index = lax.axis_index("seq")
    local_len = activations.shape[2]
    positions = seq_index * local_len + jnp.arange(local_len, dtype=jnp.int32)
    valid = (positions[None, :] < lengths[:, None]).astype(jnp.float32)
    factor = jnp.float32(1.0 / math.sqrt(local_len * seq_count))
    partial_value = project_layer(activations[0], out_grads[0], proj_in[0], proj_out[0], valid, factor)
    summed = lax.psum(partial_value, "seq")
    owned_row = lax.psum_scatter(
        owner_sums(owners, summed, lax.axis_size("store")), "store", scatter_dimension=0, tiled=True
    )
    precond = precondition_rows(owned_row, eig_out, eig_in, eig_values)
    score_scale = jnp.float32(1.0 / math.sqrt(stored.shape[1]))
    stored_list = []
    group_list = []
    for step_index in range(query_owner.shape[0]):
        panel_rows = from_root(queries, "store", query_owner[step_index])
        stored_list.append(
            lax.dot_general(stored, panel_rows, NT, preferred_element_type=jnp.float32) * score_scale
        )
        group_list.append(
            lax.dot_general(precond, panel_rows, NT, preferred_element_type=jnp.float32) * score_scale
        )
    return (jnp.stack(stored_list, axis=0), jnp.stack(group_list, axis=1))


def solution(mesh):
    fits = mesh.shape["store"] == 8 and mesh.shape["seq"] == 4
    return jax.shard_map(
        blocks if fits else any_mesh,
        mesh=mesh,
        in_specs=(
            P(None, "store", "seq", None),
            P(None, "store", "seq", None),
            P(),
            P(),
            P(),
            P(),
            P(),
            P("store"),
            P("store"),
            P(("store", "seq"), None),
            P("store", None),
            P(),
        ),
        out_specs=(P(None, ("store", "seq"), None), P("store", None, None)),
        check_vma=False,
    )
```

time: 78.1 us -> 63.6 us (0.81)
  local copies, waits for them, and re-layouts: 14.9 us -> 5.24 us
  Pallas kernels: 19.5 us -> 11.3 us
  waiting for transfers between devices: 19.2 us -> 11.9 us
  starting transfers between devices: 23 us -> 29 us
  matrix products: 0 us -> 4.97 us
    unnamed x36 -> x25, local copies, waits for them, and re-layouts: 13.7 us -> 3.04 us
    pallas_call x4 -> x11, Pallas kernels: 18.7 us -> 10.5 us  [the longest x1 4.23 us: first_scores(): pl.pallas_call(functools.partial(first_kernel, names=names, scale=scale),...]
    ppermute x19 -> x23, waiting for transfers between devices: 19.2 us -> 11.9 us  [move(): return lax.ppermute(array, AXES, pairs(way0, way1, swap))]
    ppermute x19 -> x23, starting transfers between devices: 23 us -> 29 us  [move(): return lax.ppermute(array, AXES, pairs(way0, way1, swap))]
    dot_general x0 -> x2, matrix products: none -> 4.97 us  [the longest x1 3.58 us: project(): jnp.einsum('rd,etd->ert', weight_in, acts, preferred_element_type=jnp.flo...]
    slice x0 -> x2, local copies, waits for them, and re-layouts: none -> 0.86 us  [step(): got[source][:, part * width:(part + 1) * width]]
  transfers between devices with their start and end apart: 19 -> 23, of which waited for: 6 -> 7; matrix products, arithmetic and copies ran while one was open for 0% -> 9% of each run, Pallas kernels for 18% -> 13%
where the time goes in v2:
time: 63.6 us; the launch traced here: 63.3 us
  starting transfers between devices  29 us (46%)
  waiting for transfers between devices  11.9 us (19%)
  Pallas kernels  11.3 us (18%)
  local copies, waits for them, and re-layouts  5.24 us (8%)
  matrix products  4.97 us (8%)
  between operations  0.96 us (2%)
    ppermute x23, starting transfers between devices, move(): return lax.ppermute(array, AXES, pairs(way0, way1, swap))  29 us
    ppermute x23, waiting for transfers between devices, move(): return lax.ppermute(array, AXES, pairs(way0, way1, swap))  11.9 us
    pallas_call x1, Pallas kernels, first_scores(): pl.pallas_call(functools.partial(first_kernel, names=names, scale=scale),...  4.23 us
    dot_general x1, matrix products, project(): jnp.einsum('rd,etd->ert', weight_in, acts, preferred_element_type=jnp.flo...  3.58 us
    pallas_call x1, Pallas kernels, last_scores(): pl.pallas_call(functools.partial(last_kernel, names=names, scale=scale),...  3.21 us
    unnamed x25, local copies, waits for them, and re-layouts  3.04 us
    pallas_call x1, Pallas kernels, next_scores(): pl.pallas_call(functools.partial(next_kernel, names=names, scale=scale),...  2.14 us
    dot_general x1, matrix products, project(): jnp.einsum('rd,etd->ert', weight_out, grads, preferred_element_type=jnp.f...  1.39 us
  transfers between devices with their start and end apart: 23, of which 7 were waited for; matrix products, arithmetic and copies ran while one was open for 9% of the time, Pallas kernels for 13%

profile of v2, /device:TPU:1, one launch (start us, length us, event | category | flops | bytes accessed | tf_op | source)
XLA Modules:
  0.0 63.3 jit_solution(16030520342532388827)
XLA Ops:
  0.6 0.0 copy-start
  0.7 1.2 %constant_dynamic-slice_fusion = bf16[128,2048]{1,0:T(8,128)(2,1)S(1)} fusion(bf16[128,4096]{1,0:T(8,128)(2,1)} %own.1, s32[]{:T(128)S(6)} %select_n.21), kind=kLoop, calls=%fused_computation.11 | loop fusion | bytes 1048580 | tf_op jit(solution)/shard_map/dynamic_slice | solution.py:409
  1.9 0.0 copy-start.5
  1.9 0.0 copy-start.6
  2.0 2.7 %collective-permute-start.4 = (bf16[128,2048]{1,0:T(8,128)(2,1)S(1)}, bf16[128,2048]{1,0:T(8,128)(2,1)S(1)}, u32[]{:S(2)}, u32[]{:S(2)}) collective-permute-start(bf16[128,2048]{1,0:T(8,128)(2,1)S(1)} %constant_dynamic-slice_fusion), channel_id=1, source_target_pairs={{0,17},{1,4},{2,19},{3,6},{4,21},{5,0},{6,23},{7,2},{8,1},{9,12},{... | collective-permute-start | bytes 1572872 | tf_op jit(solution)/shard_map/ppermute | solution.py:71
  4.6 3.6 %fusion.4.in_side = f32[2,64,256]{2,1,0:T(8,128)S(1)} fusion(bf16[1,2,256,4096]{3,2,1,0:T(8,128)(2,1)} %param.12, bf16[1,64,4096]{2,1,0:T(8,128)(2,1)S(1)} %copy-done), kind=kOutput, calls=%fused_computation.4 | convolution fusion | flops 268435456 | bytes 4849664 | tf_op jit(solution)/shard_map/rd,etd->ert/dot_general | solution.py:141
  8.2 1.4 %fusion.7.out_side = f32[2,64,256]{2,1,0:T(8,128)S(1)} fusion(bf16[1,2,256,4096]{3,2,1,0:T(8,128)(2,1)S(1)} %copy-done.9, bf16[1,64,4096]{2,1,0:T(8,128)(2,1)S(1)} %copy-done.10), kind=kOutput, calls=%fused_computation.5 | convolution fusion | flops 268435456 | bytes 4849664 | tf_op jit(solution)/shard_map/rd,etd->ert/dot_general | solution.py:142
  9.6 0.9 %shard_map.131.rows.refs_0_ = f32[8,32,128]{2,1,0:T(8,128)S(1)} custom-call(s32[2]{0:T(128)S(1)} %copy-done.5, s32[2]{0:T(128)S(1)} %copy-done.6, f32[2,64,256]{2,1,0:T(8,128)S(1)} %fusion.4.in_side, f32[2,64,256]{2,1,0:T(8,128)S(1)} %fusion.7.out_side), custom_call_target="tpu_custom_call" | custom-call | flops 67108864 | bytes 524288 | tf_op jit(solution)/shard_map/pallas_call | solution.py:145
  10.5 0.0 copy-start.2
  10.5 0.0 copy-start.3
  10.5 0.0 copy-start.4
  10.6 1.0 %collective-permute-done.4.block = bf16[128,2048]{1,0:T(8,128)(2,1)S(1)} collective-permute-done((bf16[128,2048]{1,0:T(8,128)(2,1)S(1)}, bf16[128,2048]{1,0:T(8,128)(2,1)S(1)}, u32[]{:S(2)}, u32[]{:S(2)}) %collective-permute-start.4) | collective-permute-done | bytes 524320 | tf_op jit(solution)/shard_map/ppermute | solution.py:71
  11.6 1.4 %collective-permute-start.5 = (bf16[128,2048]{1,0:T(8,128)(2,1)S(1)}, bf16[128,2048]{1,0:T(8,128)(2,1)S(1)}, u32[]{:S(2)}, u32[]{:S(2)}) collective-permute-start(bf16[128,2048]{1,0:T(8,128)(2,1)S(1)} %shard_map.133.refs_0_), channel_id=1, source_target_pairs={{0,8},{1,5},{2,10},{3,7},{4,12},{5,1},{6,14},{7,3},{8,24},{9,13},{... | collective-permute-start | bytes 1572872 | tf_op jit(solution)/shard_map/ppermute | solution.py:71
  13.0 1.3 %collective-permute-start.9 = (bf16[128,1024]{1,0:T(8,128)(2,1)S(1)}, bf16[128,1024]{1,0:T(8,128)(2,1)S(1)}, u32[]{:S(2)}, u32[]{:S(2)}) collective-permute-start(bf16[128,1024]{1,0:T(8,128)(2,1)S(1)} %get-tuple-element.29), channel_id=1, source_target_pairs={{0,2},{1,3},{2,0},{3,1},{4,6},{5,7},{6,4},{7,5},{8,10},{9,11},{10,... | collective-permute-start | bytes 786440 | tf_op jit(solution)/shard_map/ppermute | solution.py:71
  14.3 1.0 %collective-permute-start = (f32[8,32,128]{2,1,0:T(8,128)S(1)}, f32[8,32,128]{2,1,0:T(8,128)S(1)}, u32[]{:S(2)}, u32[]{:S(2)}) collective-permute-start(f32[8,32,128]{2,1,0:T(8,128)S(1)} %shard_map.131.rows.refs_0_), channel_id=1, source_target_pairs={{0,1},{1,0},{2,3},{3,2},{4,5},{5,4},{6,7},{7,6},{8,9},{9,8},{10,11... | collective-permute-start | bytes 393224 | tf_op jit(solution)/shard_map/ppermute | solution.py:71
  15.3 1.0 %collective-permute-done.other = f32[8,32,128]{2,1,0:T(8,128)S(1)} collective-permute-done((f32[8,32,128]{2,1,0:T(8,128)S(1)}, f32[8,32,128]{2,1,0:T(8,128)S(1)}, u32[]{:S(2)}, u32[]{:S(2)}) %collective-permute-start) | collective-permute-done | bytes 131104 | tf_op jit(solution)/shard_map/ppermute | solution.py:71
  16.3 1.3 %collective-permute-start.1 = (f32[4,32,128]{2,1,0:T(8,128)S(1)}, f32[4,32,128]{2,1,0:T(8,128)S(1)}, u32[]{:S(2)}, u32[]{:S(2)}) collective-permute-start(f32[4,32,128]{2,1,0:T(8,128)S(1)} %get-tuple-element.15.sent), channel_id=1, source_target_pairs={{0,4},{1,5},{2,6},{3,7},{4,0},{5,1},{6,2},{7,3},{8,12},{9,13},{10,... | collective-permute-start | bytes 196616 | tf_op jit(solution)/shard_map/ppermute | solution.py:71
  17.6 0.2 collective-permute-start.3
  17.8 1.2 %collective-permute-start.2 = (f32[4,32,128]{2,1,0:T(8,128)S(1)}, f32[4,32,128]{2,1,0:T(8,128)S(1)}, u32[]{:S(2)}, u32[]{:S(2)}) collective-permute-start(f32[4,32,128]{2,1,0:T(8,128)S(1)} %get-tuple-element.16), channel_id=1, source_target_pairs={{0,2},{1,3},{2,0},{3,1},{4,6},{5,7},{6,4},{7,5},{8,10},{9,11},{10,... | collective-permute-start | bytes 196616 | tf_op jit(solution)/shard_map/ppermute | solution.py:71
  19.1 2.1 %collective-permute-done.1.refs_0_ = f32[4,32,128]{2,1,0:T(8,128)S(1)} collective-permute-done((f32[4,32,128]{2,1,0:T(8,128)S(1)}, f32[4,32,128]{2,1,0:T(8,128)S(1)}, u32[]{:S(2)}, u32[]{:S(2)}) %collective-permute-start.1) | collective-permute-done | bytes 65568 | tf_op jit(solution)/shard_map/ppermute | solution.py:71
  21.2 2.7 %collective-permute-done.3.refs_2_ = f32[4,32,128]{2,1,0:T(8,128)S(1)} collective-permute-done((f32[4,32,128]{2,1,0:T(8,128)S(1)}, f32[4,32,128]{2,1,0:T(8,128)S(1)}, u32[]{:S(2)}, u32[]{:S(2)}) %collective-permute-start.3) | collective-permute-done | bytes 65568 | tf_op jit(solution)/shard_map/ppermute | solution.py:71
  23.8 0.0 collective-permute-done.2.refs_1_
  23.9 0.0 collective-permute-done.5.refs_3_.block
  23.9 0.0 collective-permute-done.9.refs_0_
  23.9 2.7 %collective-permute-start.10 = (bf16[128,2048]{1,0:T(8,128)(2,1)S(1)}, bf16[128,2048]{1,0:T(8,128)(2,1)S(1)}, u32[]{:S(2)}, u32[]{:S(2)}) collective-permute-start(bf16[128,2048]{1,0:T(8,128)(2,1)S(1)} %shard_map.135.refs_2_), channel_id=1, source_target_pairs={{0,4},{1,17},{2,6},{3,19},{4,0},{5,21},{6,2},{7,23},{8,12},{9,1},{... | collective-permute-start | bytes 1572872 | tf_op jit(solution)/shard_map/ppermute | solution.py:71
  26.6 1.3 %collective-permute-start.12 = (bf16[128,1024]{1,0:T(8,128)(2,1)S(1)}, bf16[128,1024]{1,0:T(8,128)(2,1)S(1)}, u32[]{:S(2)}, u32[]{:S(2)}) collective-permute-start(bf16[128,1024]{1,0:T(8,128)(2,1)S(1)} %get-tuple-element.28), channel_id=1, source_target_pairs={{0,2},{1,3},{2,0},{3,1},{4,6},{5,7},{6,4},{7,5},{8,10},{9,11},{10,... | collective-permute-start | bytes 786440 | tf_op jit(solution)/shard_map/ppermute | solution.py:71
  27.9 0.0 collective-permute-start.6
  27.9 1.5 %collective-permute-start.7 = (f32[1,32,128]{2,1,0:T(8,128)S(1)}, f32[1,32,128]{2,1,0:T(8,128)S(1)}, u32[]{:S(2)}, u32[]{:S(2)}) collective-permute-start(f32[1,32,128]{2,1,0:T(8,128)S(1)} %get-tuple-element.19), channel_id=1, source_target_pairs={{0,16},{1,17},{2,18},{3,19},{4,20},{5,21},{6,22},{7,23},{8,24},{9,... | collective-permute-start | bytes 49160 | tf_op jit(solution)/shard_map/ppermute | solution.py:71
  29.4 2.0 %collective-permute-start.8 = (f32[1,32,128]{2,1,0:T(8,128)S(1)}, f32[1,32,128]{2,1,0:T(8,128)S(1)}, u32[]{:S(2)}, u32[]{:S(2)}) collective-permute-start(f32[1,32,128]{2,1,0:T(8,128)S(1)} %get-tuple-element.20), channel_id=1, source_target_pairs={{0,24},{1,25},{2,26},{3,27},{4,28},{5,29},{6,30},{7,31},{8,16},{9,... | collective-permute-start | bytes 49160 | tf_op jit(solution)/shard_map/ppermute | solution.py:71
  31.5 1.9 %collective-permute-done.6.refs_0_ = f32[1,32,128]{2,1,0:T(8,128)S(1)} collective-permute-done((f32[1,32,128]{2,1,0:T(8,128)S(1)}, f32[1,32,128]{2,1,0:T(8,128)S(1)}, u32[]{:S(2)}, u32[]{:S(2)}) %collective-permute-start.6) | collective-permute-done | bytes 16416 | tf_op jit(solution)/shard_map/ppermute | solution.py:71
  33.4 0.0 collective-permute-start.11
  33.4 0.2 collective-permute-done.7.refs_1_
  33.6 3.0 %collective-permute-start.13 = (bf16[128,2048]{1,0:T(8,128)(2,1)S(1)}, bf16[128,2048]{1,0:T(8,128)(2,1)}, u32[]{:S(2)}, u32[]{:S(2)}) collective-permute-start(bf16[128,2048]{1,0:T(8,128)(2,1)S(1)} %shard_map.135.refs_2_), channel_id=1, source_target_pairs={{0,1},{1,0},{2,3},{3,2},{4,5},{5,4},{6,7},{7,6},{8,9},{9,8},{10,11... | collective-permute-start | bytes 1572872 | tf_op jit(solution)/shard_map/ppermute | solution.py:71
  36.5 0.0 collective-permute-done.8.refs_2_
  36.5 0.0 collective-permute-done.10.refs_3_.block
  36.6 0.0 collective-permute-done.12.refs_0_
  36.6 0.1 collective-permute-start.14
  36.7 0.8 %fusion.12 = (bf16[128,1024]{1,0:T(8,128)(2,1)}, bf16[128,1024]{1,0:T(8,128)(2,1)}) fusion(bf16[128,2048]{1,0:T(8,128)(2,1)S(1)} %shard_map.138.refs_3_), kind=kLoop, calls=%fused_computation.12 | loop fusion | bytes 1048576 | tf_op jit(solution)/shard_map/slice | solution.py:420
  37.5 1.1 %collective-permute-start.15 = (bf16[128,1024]{1,0:T(8,128)(2,1)}, bf16[128,1024]{1,0:T(8,128)(2,1)S(1)}, u32[]{:S(2)}, u32[]{:S(2)}) collective-permute-start(bf16[128,1024]{1,0:T(8,128)(2,1)} %get-tuple-element.27), channel_id=1, source_target_pairs={{0,2},{1,3},{2,0},{3,1},{4,6},{5,7},{6,4},{7,5},{8,10},{9,11},{10,... | collective-permute-start | bytes 786440 | tf_op jit(solution)/shard_map/ppermute | solution.py:71
  38.6 0.4 collective-permute-start.16
  39.0 0.8 %shard_map.137 = bf16[64,64]{1,0:T(8,128)(2,1)S(1)} custom-call(f32[32,128]{1,0:T(8,128)S(1)} %shard_map.136.group, f32[64,64]{1,0:T(8,128)S(1)} %bitcast.26, f32[64,64]{1,0:T(8,128)S(1)} %bitcast.27, f32[64,64]{1,0:T(8,128)S(1)} %bitcast.28), custom_call_target="tpu_custom_call" | custom-call | flops 16777216 | bytes 131072 | tf_op jit(solution)/shard_map/pallas_call | solution.py:171
  39.8 0.1 reshape.7.row
  39.9 0.0 collective-permute-done.11.refs_1_
  39.9 0.0 collective-permute-done.13.refs_4_
  39.9 0.0 collective-permute-done.14.refs_5_
  39.9 0.0 copy-start.1
  39.9 1.2 %copy-done.1 = bf16[128,4096]{1,0:T(8,128)(2,1)S(1)} copy-done((bf16[128,4096]{1,0:T(8,128)(2,1)S(1)}, bf16[128,4096]{1,0:T(8,128)(2,1)}, u32[]{:S(2)}) %copy-start.1) | copy-done | bytes 1048600
  41.2 1.7 %copy-done.8 = bf16[320,4096]{1,0:T(8,128)(2,1)S(1)} copy-done((bf16[320,4096]{1,0:T(8,128)(2,1)S(1)}, bf16[320,4096]{1,0:T(8,128)(2,1)}, u32[]{:S(2)}) %copy-start.8) | copy-done | bytes 2621464
  42.9 4.2 %shard_map.139 = (bf16[336,4096]{1,0:T(8,128)(2,1)S(1)}, f32[8,336,128]{2,1,0:T(8,128)S(1)}, f32[8,128]{1,0:T(8,128)S(1)}) custom-call(bf16[320,4096]{1,0:T(8,128)(2,1)S(1)} %copy-done.8, bf16[1,4096]{1,0:T(2,128)(2,1)S(1)} %reshape.7.row, bf16[128,4096]{1,0:T(8,128)(2,1)S(1)} %copy-done.1, bf16[128,2048]{1,0:T(8,128)(2,1)S(1)} %shard_map.133.refs_0_, ...), custom_call_target="tpu_custom_call" | custom-call | flops 2147483648 | bytes 4194304 | tf_op jit(solution)/shard_map/pallas_call | solution.py:232
  47.1 0.0 collective-permute-done.15.refs_1_
  47.2 1.2 %collective-permute-start.20 = (bf16[128,2048]{1,0:T(8,128)(2,1)S(1)}, bf16[128,2048]{1,0:T(8,128)(2,1)S(1)}, u32[]{:S(2)}, u32[]{:S(2)}) collective-permute-start(bf16[128,2048]{1,0:T(8,128)(2,1)S(1)} %shard_map.140.refs_0_), channel_id=1, source_target_pairs={{0,8},{1,5},{2,10},{3,7},{4,12},{5,1},{6,14},{7,3},{8,24},{9,13},{... | collective-permute-start | bytes 1572872 | tf_op jit(solution)/shard_map/ppermute | solution.py:71
  48.3 0.4 collective-permute-start.19
  48.7 0.0 copy-start.7
  48.8 2.3 %collective-permute-start.18 = (bf16[128,2048]{1,0:T(8,128)(2,1)S(1)}, bf16[128,2048]{1,0:T(8,128)(2,1)S(1)}, u32[]{:S(2)}, u32[]{:S(2)}) collective-permute-start(bf16[128,2048]{1,0:T(8,128)(2,1)S(1)} %shard_map.140.refs_0_), channel_id=1, source_target_pairs={{0,1},{1,0},{2,3},{3,2},{4,5},{5,4},{6,7},{7,6},{8,9},{9,8},{10,11... | collective-permute-start | bytes 1572872 | tf_op jit(solution)/shard_map/ppermute | solution.py:71
  51.0 0.0 collective-permute-done.16.refs_3_
  51.0 0.1 collective-permute-start.17
  51.1 2.9 %collective-permute-done.19 = bf16[128,1024]{1,0:T(8,128)(2,1)S(1)} collective-permute-done((bf16[128,1024]{1,0:T(8,128)(2,1)S(1)}, bf16[128,1024]{1,0:T(8,128)(2,1)S(1)}, u32[]{:S(2)}, u32[]{:S(2)}) %collective-permute-start.19) | collective-permute-done | bytes 262176 | tf_op jit(solution)/shard_map/ppermute | solution.py:71
  54.1 3.1 %collective-permute-start.21 = (bf16[128,2048]{1,0:T(8,128)(2,1)S(1)}, bf16[128,2048]{1,0:T(8,128)(2,1)S(1)}, u32[]{:S(2)}, u32[]{:S(2)}) collective-permute-start(bf16[128,2048]{1,0:T(8,128)(2,1)S(1)} %constant_dynamic-update-slice_fusion.refs_0_), channel_id=1, source_target_pairs={{0,1},{1,0},{2,3},{3,2},{4,5},{5,4},{6,7},{7,6},{8,9},{9,8},{10,11... | collective-permute-start | bytes 1572872 | tf_op jit(solution)/shard_map/ppermute | solution.py:71
  57.1 0.0 collective-permute-done.20.refs_1_
  57.1 0.8 %collective-permute-start.22 = (bf16[128,2048]{1,0:T(8,128)(2,1)S(1)}, bf16[128,2048]{1,0:T(8,128)(2,1)S(1)}, u32[]{:S(2)}, u32[]{:S(2)}) collective-permute-start(bf16[128,2048]{1,0:T(8,128)(2,1)S(1)} %collective-permute-done.20.refs_1_), channel_id=1, source_target_pairs={{0,1},{1,0},{2,3},{3,2},{4,5},{5,4},{6,7},{7,6},{8,9},{9,8},{10,11... | collective-permute-start | bytes 1572872 | tf_op jit(solution)/shard_map/ppermute | solution.py:71
  57.9 0.0 collective-permute-done.18.refs_2_
  58.0 2.1 %shard_map.141.before = f32[8,336,128]{2,1,0:T(8,128)S(1)} custom-call(bf16[336,4096]{1,0:T(8,128)(2,1)S(1)} %get-tuple-element.21.left, f32[8,336,128]{2,1,0:T(8,128)S(1)} %get-tuple-element.22.before, bf16[128,2048]{1,0:T(8,128)(2,1)S(1)} %shard_map.140.refs_0_, bf16[128,2048]{1,0:T(8,128)(2,1)S(1)} %collective-permute-done.17.refs_1_, ...), custom_call_target="tpu_custom_call" | custom-call | flops 1073741824 | bytes 2097152 | tf_op jit(solution)/shard_map/pallas_call | solution.py:261
  60.1 0.0 collective-permute-done.22.refs_3_
  60.1 3.2 %shard_map.142 = (f32[8,320,128]{2,1,0:T(8,128)}, f32[8,128]{1,0:T(8,128)}) custom-call(s32[8]{0:T(128)S(1)} %copy-done.7, bf16[336,4096]{1,0:T(8,128)(2,1)S(1)} %get-tuple-element.21.left, f32[8,336,128]{2,1,0:T(8,128)S(1)} %shard_map.141.before, bf16[128,2048]{1,0:T(8,128)(2,1)S(1)} %constant_dynamic-update-slice_fusion.refs_0_, ...), custom_call_target="tpu_custom_call" | custom-call | flops 1073741824 | bytes 8388608 | tf_op jit(solution)/shard_map/pallas_call | solution.py:294
  (27 shorter events, 0.2 us)
Async XLA Ops:
  0.6 4.0 %copy-start = (bf16[1,64,4096]{2,1,0:T(8,128)(2,1)S(1)}, bf16[1,64,4096]{2,1,0:T(8,128)(2,1)}, u32[]{:S(2)}) copy-start(bf16[1,64,4096]{2,1,0:T(8,128)(2,1)} %param.14) | copy-start | bytes 1572868
  0.6 7.6 %copy-start.10 = (bf16[1,64,4096]{2,1,0:T(8,128)(2,1)S(1)}, bf16[1,64,4096]{2,1,0:T(8,128)(2,1)}, u32[]{:S(2)}) copy-start(bf16[1,64,4096]{2,1,0:T(8,128)(2,1)} %param.15) | copy-start | bytes 1572868
  0.7 7.5 %copy-start.9 = (bf16[1,2,256,4096]{3,2,1,0:T(8,128)(2,1)S(1)}, bf16[1,2,256,4096]{3,2,1,0:T(8,128)(2,1)}, u32[]{:S(2)}) copy-start(bf16[1,2,256,4096]{3,2,1,0:T(8,128)(2,1)} %param.13) | copy-start | bytes 12582916
  1.9 7.7 %copy-start.5 = (s32[2]{0:T(128)S(1)}, s32[2]{0:T(128)}, u32[]{:S(2)}) copy-start(s32[2]{0:T(128)} %lengths.1) | copy-start | bytes 28
  1.9 7.7 %copy-start.6 = (s32[2]{0:T(128)S(1)}, s32[2]{0:T(128)}, u32[]{:S(2)}) copy-start(s32[2]{0:T(128)} %owners.1) | copy-start | bytes 28
  2.0 9.6 %collective-permute-start.4 = (bf16[128,2048]{1,0:T(8,128)(2,1)S(1)}, bf16[128,2048]{1,0:T(8,128)(2,1)S(1)}, u32[]{:S(2)}, u32[]{:S(2)}) collective-permute-start(bf16[128,2048]{1,0:T(8,128)(2,1)S(1)} %constant_dynamic-slice_fusion), channel_id=1, source_target_pairs={{0,17},{1,4},{2,19},{3,6},{4,21},{5,0},{6,23},{7,2},{8,1},{9,12},{... | collective-permute-start | bytes 1572872 | tf_op jit(solution)/shard_map/ppermute | solution.py:71
  10.5 28.5 %copy-start.2 = (f32[1,64,64]{2,1,0:T(8,128)S(1)}, f32[1,64,64]{2,1,0:T(8,128)}, u32[]{:S(2)}) copy-start(f32[1,64,64]{2,1,0:T(8,128)} %param.16) | copy-start | bytes 49156
  10.5 28.5 %copy-start.3 = (f32[1,64,64]{2,1,0:T(8,128)S(1)}, f32[1,64,64]{2,1,0:T(8,128)}, u32[]{:S(2)}) copy-start(f32[1,64,64]{2,1,0:T(8,128)} %param.17) | copy-start | bytes 49156
  10.5 28.5 %copy-start.4 = (f32[1,64,64]{2,1,0:T(8,128)S(1)}, f32[1,64,64]{2,1,0:T(8,128)}, u32[]{:S(2)}) copy-start(f32[1,64,64]{2,1,0:T(8,128)} %param.18) | copy-start | bytes 49156
  11.6 12.3 %collective-permute-start.5 = (bf16[128,2048]{1,0:T(8,128)(2,1)S(1)}, bf16[128,2048]{1,0:T(8,128)(2,1)S(1)}, u32[]{:S(2)}, u32[]{:S(2)}) collective-permute-start(bf16[128,2048]{1,0:T(8,128)(2,1)S(1)} %shard_map.133.refs_0_), channel_id=1, source_target_pairs={{0,8},{1,5},{2,10},{3,7},{4,12},{5,1},{6,14},{7,3},{8,24},{9,13},{... | collective-permute-start | bytes 1572872 | tf_op jit(solution)/shard_map/ppermute | solution.py:71
  13.0 10.9 %collective-permute-start.9 = (bf16[128,1024]{1,0:T(8,128)(2,1)S(1)}, bf16[128,1024]{1,0:T(8,128)(2,1)S(1)}, u32[]{:S(2)}, u32[]{:S(2)}) collective-permute-start(bf16[128,1024]{1,0:T(8,128)(2,1)S(1)} %get-tuple-element.29), channel_id=1, source_target_pairs={{0,2},{1,3},{2,0},{3,1},{4,6},{5,7},{6,4},{7,5},{8,10},{9,11},{10,... | collective-permute-start | bytes 786440 | tf_op jit(solution)/shard_map/ppermute | solution.py:71
  14.3 2.0 %collective-permute-start = (f32[8,32,128]{2,1,0:T(8,128)S(1)}, f32[8,32,128]{2,1,0:T(8,128)S(1)}, u32[]{:S(2)}, u32[]{:S(2)}) collective-permute-start(f32[8,32,128]{2,1,0:T(8,128)S(1)} %shard_map.131.rows.refs_0_), channel_id=1, source_target_pairs={{0,1},{1,0},{2,3},{3,2},{4,5},{5,4},{6,7},{7,6},{8,9},{9,8},{10,11... | collective-permute-start | bytes 393224 | tf_op jit(solution)/shard_map/ppermute | solution.py:71
  16.3 4.8 %collective-permute-start.1 = (f32[4,32,128]{2,1,0:T(8,128)S(1)}, f32[4,32,128]{2,1,0:T(8,128)S(1)}, u32[]{:S(2)}, u32[]{:S(2)}) collective-permute-start(f32[4,32,128]{2,1,0:T(8,128)S(1)} %get-tuple-element.15.sent), channel_id=1, source_target_pairs={{0,4},{1,5},{2,6},{3,7},{4,0},{5,1},{6,2},{7,3},{8,12},{9,13},{10,... | collective-permute-start | bytes 196616 | tf_op jit(solution)/shard_map/ppermute | solution.py:71
  17.6 6.2 %collective-permute-start.3 = (f32[4,32,128]{2,1,0:T(8,128)S(1)}, f32[4,32,128]{2,1,0:T(8,128)S(1)}, u32[]{:S(2)}, u32[]{:S(2)}) collective-permute-start(f32[4,32,128]{2,1,0:T(8,128)S(1)} %get-tuple-element.15.sent), channel_id=1, source_target_pairs={{0,6},{1,7},{2,4},{3,5},{4,2},{5,3},{6,0},{7,1},{8,14},{9,15},{10,... | collective-permute-start | bytes 196616 | tf_op jit(solution)/shard_map/ppermute | solution.py:71
  17.8 6.0 %collective-permute-start.2 = (f32[4,32,128]{2,1,0:T(8,128)S(1)}, f32[4,32,128]{2,1,0:T(8,128)S(1)}, u32[]{:S(2)}, u32[]{:S(2)}) collective-permute-start(f32[4,32,128]{2,1,0:T(8,128)S(1)} %get-tuple-element.16), channel_id=1, source_target_pairs={{0,2},{1,3},{2,0},{3,1},{4,6},{5,7},{6,4},{7,5},{8,10},{9,11},{10,... | collective-permute-start | bytes 196616 | tf_op jit(solution)/shard_map/ppermute | solution.py:71
  23.9 12.6 %collective-permute-start.10 = (bf16[128,2048]{1,0:T(8,128)(2,1)S(1)}, bf16[128,2048]{1,0:T(8,128)(2,1)S(1)}, u32[]{:S(2)}, u32[]{:S(2)}) collective-permute-start(bf16[128,2048]{1,0:T(8,128)(2,1)S(1)} %shard_map.135.refs_2_), channel_id=1, source_target_pairs={{0,4},{1,17},{2,6},{3,19},{4,0},{5,21},{6,2},{7,23},{8,12},{9,1},{... | collective-permute-start | bytes 1572872 | tf_op jit(solution)/shard_map/ppermute | solution.py:71
  26.6 10.0 %collective-permute-start.12 = (bf16[128,1024]{1,0:T(8,128)(2,1)S(1)}, bf16[128,1024]{1,0:T(8,128)(2,1)S(1)}, u32[]{:S(2)}, u32[]{:S(2)}) collective-permute-start(bf16[128,1024]{1,0:T(8,128)(2,1)S(1)} %get-tuple-element.28), channel_id=1, source_target_pairs={{0,2},{1,3},{2,0},{3,1},{4,6},{5,7},{6,4},{7,5},{8,10},{9,11},{10,... | collective-permute-start | bytes 786440 | tf_op jit(solution)/shard_map/ppermute | solution.py:71
  27.9 5.5 %collective-permute-start.6 = (f32[1,32,128]{2,1,0:T(8,128)S(1)}, f32[1,32,128]{2,1,0:T(8,128)S(1)}, u32[]{:S(2)}, u32[]{:S(2)}) collective-permute-start(f32[1,32,128]{2,1,0:T(8,128)S(1)} %get-tuple-element.18), channel_id=1, source_target_pairs={{0,8},{1,9},{2,10},{3,11},{4,12},{5,13},{6,14},{7,15},{8,0},{9,1},... | collective-permute-start | bytes 49160 | tf_op jit(solution)/shard_map/ppermute | solution.py:71
  27.9 5.7 %collective-permute-start.7 = (f32[1,32,128]{2,1,0:T(8,128)S(1)}, f32[1,32,128]{2,1,0:T(8,128)S(1)}, u32[]{:S(2)}, u32[]{:S(2)}) collective-permute-start(f32[1,32,128]{2,1,0:T(8,128)S(1)} %get-tuple-element.19), channel_id=1, source_target_pairs={{0,16},{1,17},{2,18},{3,19},{4,20},{5,21},{6,22},{7,23},{8,24},{9,... | collective-permute-start | bytes 49160 | tf_op jit(solution)/shard_map/ppermute | solution.py:71
  29.4 7.1 %collective-permute-start.8 = (f32[1,32,128]{2,1,0:T(8,128)S(1)}, f32[1,32,128]{2,1,0:T(8,128)S(1)}, u32[]{:S(2)}, u32[]{:S(2)}) collective-permute-start(f32[1,32,128]{2,1,0:T(8,128)S(1)} %get-tuple-element.20), channel_id=1, source_target_pairs={{0,24},{1,25},{2,26},{3,27},{4,28},{5,29},{6,30},{7,31},{8,16},{9,... | collective-permute-start | bytes 49160 | tf_op jit(solution)/shard_map/ppermute | solution.py:71
  33.4 6.5 %collective-permute-start.11 = (bf16[128,2048]{1,0:T(8,128)(2,1)S(1)}, bf16[128,2048]{1,0:T(8,128)(2,1)}, u32[]{:S(2)}, u32[]{:S(2)}) collective-permute-start(bf16[128,2048]{1,0:T(8,128)(2,1)S(1)} %shard_map.133.refs_0_), channel_id=1, source_target_pairs={{0,1},{1,0},{2,3},{3,2},{4,5},{5,4},{6,7},{7,6},{8,9},{9,8},{10,11... | collective-permute-start | bytes 1572872 | tf_op jit(solution)/shard_map/ppermute | solution.py:71
  33.6 6.3 %collective-permute-start.13 = (bf16[128,2048]{1,0:T(8,128)(2,1)S(1)}, bf16[128,2048]{1,0:T(8,128)(2,1)}, u32[]{:S(2)}, u32[]{:S(2)}) collective-permute-start(bf16[128,2048]{1,0:T(8,128)(2,1)S(1)} %shard_map.135.refs_2_), channel_id=1, source_target_pairs={{0,1},{1,0},{2,3},{3,2},{4,5},{5,4},{6,7},{7,6},{8,9},{9,8},{10,11... | collective-permute-start | bytes 1572872 | tf_op jit(solution)/shard_map/ppermute | solution.py:71
  36.6 3.3 %collective-permute-start.14 = (bf16[128,2048]{1,0:T(8,128)(2,1)S(1)}, bf16[128,2048]{1,0:T(8,128)(2,1)}, u32[]{:S(2)}, u32[]{:S(2)}) collective-permute-start(bf16[128,2048]{1,0:T(8,128)(2,1)S(1)} %shard_map.138.refs_3_), channel_id=1, source_target_pairs={{0,1},{1,0},{2,3},{3,2},{4,5},{5,4},{6,7},{7,6},{8,9},{9,8},{10,11... | collective-permute-start | bytes 1572872 | tf_op jit(solution)/shard_map/ppermute | solution.py:71
  37.5 9.6 %collective-permute-start.15 = (bf16[128,1024]{1,0:T(8,128)(2,1)}, bf16[128,1024]{1,0:T(8,128)(2,1)S(1)}, u32[]{:S(2)}, u32[]{:S(2)}) collective-permute-start(bf16[128,1024]{1,0:T(8,128)(2,1)} %get-tuple-element.27), channel_id=1, source_target_pairs={{0,2},{1,3},{2,0},{3,1},{4,6},{5,7},{6,4},{7,5},{8,10},{9,11},{10,... | collective-permute-start | bytes 786440 | tf_op jit(solution)/shard_map/ppermute | solution.py:71
  38.6 12.4 %collective-permute-start.16 = (bf16[128,2048]{1,0:T(8,128)(2,1)S(1)}, bf16[128,2048]{1,0:T(8,128)(2,1)S(1)}, u32[]{:S(2)}, u32[]{:S(2)}) collective-permute-start(bf16[128,2048]{1,0:T(8,128)(2,1)S(1)} %shard_map.138.refs_3_), channel_id=1, source_target_pairs={{0,8},{1,5},{2,10},{3,7},{4,12},{5,1},{6,14},{7,3},{8,24},{9,13},{... | collective-permute-start | bytes 1572872 | tf_op jit(solution)/shard_map/ppermute | solution.py:71
  39.9 1.2 %copy-start.1 = (bf16[128,4096]{1,0:T(8,128)(2,1)S(1)}, bf16[128,4096]{1,0:T(8,128)(2,1)}, u32[]{:S(2)}) copy-start(bf16[128,4096]{1,0:T(8,128)(2,1)} %own.1) | copy-start | bytes 3145732
  41.2 1.7 %copy-start.8 = (bf16[320,4096]{1,0:T(8,128)(2,1)S(1)}, bf16[320,4096]{1,0:T(8,128)(2,1)}, u32[]{:S(2)}) copy-start(bf16[320,4096]{1,0:T(8,128)(2,1)} %stored.1) | copy-start | bytes 7864324
  42.9 5.4 %copy-start.11 = (bf16[128,1024]{1,0:T(8,128)(2,1)S(1)}, bf16[128,1024]{1,0:T(8,128)(2,1)}, u32[]{:S(2)}) copy-start(bf16[128,1024]{1,0:T(8,128)(2,1)} %get-tuple-element.26) | copy-start | bytes 786436
  47.2 10.0 %collective-permute-start.20 = (bf16[128,2048]{1,0:T(8,128)(2,1)S(1)}, bf16[128,2048]{1,0:T(8,128)(2,1)S(1)}, u32[]{:S(2)}, u32[]{:S(2)}) collective-permute-start(bf16[128,2048]{1,0:T(8,128)(2,1)S(1)} %shard_map.140.refs_0_), channel_id=1, source_target_pairs={{0,8},{1,5},{2,10},{3,7},{4,12},{5,1},{6,14},{7,3},{8,24},{9,13},{... | collective-permute-start | bytes 1572872 | tf_op jit(solution)/shard_map/ppermute | solution.py:71
  48.3 5.7 %collective-permute-start.19 = (bf16[128,1024]{1,0:T(8,128)(2,1)S(1)}, bf16[128,1024]{1,0:T(8,128)(2,1)S(1)}, u32[]{:S(2)}, u32[]{:S(2)}) collective-permute-start(bf16[128,1024]{1,0:T(8,128)(2,1)S(1)} %copy-done.11), channel_id=1, source_target_pairs={{0,2},{1,3},{2,0},{3,1},{4,6},{5,7},{6,4},{7,5},{8,10},{9,11},{10,... | collective-permute-start | bytes 786440 | tf_op jit(solution)/shard_map/ppermute | solution.py:71
  48.7 11.4 %copy-start.7 = (s32[8]{0:T(128)S(1)}, s32[8]{0:T(128)}, u32[]{:S(2)}) copy-start(s32[8]{0:T(128)} %query_owner.1) | copy-start | bytes 100
  48.8 9.2 %collective-permute-start.18 = (bf16[128,2048]{1,0:T(8,128)(2,1)S(1)}, bf16[128,2048]{1,0:T(8,128)(2,1)S(1)}, u32[]{:S(2)}, u32[]{:S(2)}) collective-permute-start(bf16[128,2048]{1,0:T(8,128)(2,1)S(1)} %shard_map.140.refs_0_), channel_id=1, source_target_pairs={{0,1},{1,0},{2,3},{3,2},{4,5},{5,4},{6,7},{7,6},{8,9},{9,8},{10,11... | collective-permute-start | bytes 1572872 | tf_op jit(solution)/shard_map/ppermute | solution.py:71
  51.0 6.9 %collective-permute-start.17 = (bf16[128,2048]{1,0:T(8,128)(2,1)S(1)}, bf16[128,2048]{1,0:T(8,128)(2,1)S(1)}, u32[]{:S(2)}, u32[]{:S(2)}) collective-permute-start(bf16[128,2048]{1,0:T(8,128)(2,1)S(1)} %collective-permute-done.16.refs_3_), channel_id=1, source_target_pairs={{0,1},{1,0},{2,3},{3,2},{4,5},{5,4},{6,7},{7,6},{8,9},{9,8},{10,11... | collective-permute-start | bytes 1572872 | tf_op jit(solution)/shard_map/ppermute | solution.py:71
  54.1 6.0 %collective-permute-start.21 = (bf16[128,2048]{1,0:T(8,128)(2,1)S(1)}, bf16[128,2048]{1,0:T(8,128)(2,1)S(1)}, u32[]{:S(2)}, u32[]{:S(2)}) collective-permute-start(bf16[128,2048]{1,0:T(8,128)(2,1)S(1)} %constant_dynamic-update-slice_fusion.refs_0_), channel_id=1, source_target_pairs={{0,1},{1,0},{2,3},{3,2},{4,5},{5,4},{6,7},{7,6},{8,9},{9,8},{10,11... | collective-permute-start | bytes 1572872 | tf_op jit(solution)/shard_map/ppermute | solution.py:71
  57.1 3.0 %collective-permute-start.22 = (bf16[128,2048]{1,0:T(8,128)(2,1)S(1)}, bf16[128,2048]{1,0:T(8,128)(2,1)S(1)}, u32[]{:S(2)}, u32[]{:S(2)}) collective-permute-start(bf16[128,2048]{1,0:T(8,128)(2,1)S(1)} %collective-permute-done.20.refs_1_), channel_id=1, source_target_pairs={{0,1},{1,0},{2,3},{3,2},{4,5},{5,4},{6,7},{7,6},{8,9},{9,8},{10,11... | collective-permute-start | bytes 1572872 | tf_op jit(solution)/shard_map/ppermute | solution.py:71

commit v3 on v2

--- a/solution.py
+++ b/solution.py
@@ -12,7 +12,6 @@
 HIGHEST = lax.Precision.HIGHEST
 NT = (((1,), (1,)), ((), ()))
 MIB = 1 << 20
-FIRST_MIB = 20
 
 STEPS = (
     (0, "W", "X", True),
@@ -244,8 +243,8 @@
             pltpu.VMEM(own.shape, jnp.bfloat16),
             pltpu.SemaphoreType.DMA((2,)),
         ],
-        compiler_params=pltpu.CompilerParams(vmem_limit_bytes=FIRST_MIB * MIB),
-        cost_estimate=pl.CostEstimate(flops=1 << 31, bytes_accessed=4 * MIB, transcendentals=0),
+        compiler_params=pltpu.CompilerParams(vmem_limit_bytes=20 * MIB),
+        cost_estimate=pl.CostEstimate(flops=1 << 33, bytes_accessed=1024, transcendentals=0),
     )(stored, row, own, *units)
 
 
@@ -268,23 +267,42 @@
             pltpu.SemaphoreType.DMA((len(units),)),
         ],
         compiler_params=pltpu.CompilerParams(vmem_limit_bytes=8 * MIB),
-        cost_estimate=pl.CostEstimate(flops=1 << 30, bytes_accessed=2 * MIB, transcendentals=0),
+        cost_estimate=pl.CostEstimate(flops=1 << 32, bytes_accessed=1024, transcendentals=0),
     )(left, before, *units)
 
 
 def last_kernel(query_owner, left, before, *refs, names, scale):
     units, (out, group_out, totals, sems) = refs[:-4], refs[-4:]
     rows = out.shape[1]
+    store, seq = lax.axis_index("store"), lax.axis_index("seq")
+    late = [unit_place(*name, store, seq)[0] for pair in names for name in pair]
+
+    def copy_out(source, step):
+        return pltpu.make_async_copy(source.at[query_owner[step], pl.ds(0, rows)], out.at[step], sems.at[step])
+
+    def is_late(step):
+        found = query_owner[step] == late[0]
+        for panel in late[1:]:
+            found = found | (query_owner[step] == panel)
+        return found
+
+    for step in range(out.shape[0]):
+
+        @pl.when(jnp.logical_not(is_late(step)))
+        def _(step=step):
+            copy_out(before, step).start()
+
     totals[...] = before[...]
     add_scores(left, None, iter([unit[...] for unit in units]), names, totals, scale)
-    copies = []
     for step in range(out.shape[0]):
-        owner = query_owner[step]
-        copies.append(pltpu.make_async_copy(totals.at[owner, pl.ds(0, rows)], out.at[step], sems.at[step]))
-        copies[-1].start()
-        group_out[pl.ds(step, 1)] = totals[owner, rows : rows + 1]
-    for copy in copies:
-        copy.wait()
+
+        @pl.when(is_late(step))
+        def _(step=step):
+            copy_out(totals, step).start()
+
+        group_out[pl.ds(step, 1)] = totals[query_owner[step], rows : rows + 1]
+    for step in range(out.shape[0]):
+        copy_out(totals, step).wait()
 
 
 def last_scores(query_owner, left, before, units, names, scale):
@@ -333,11 +351,13 @@
         send[0] = kept[z ^ (bits + 1)]
 
 
-def sum_plane(rows, others, *tokens):
+def plane_moves(keep, send):
+    return move(keep, "Y", "Y"), move(send, "X", "X"), move(send, "XY", "XY")
+
+
+def sum_plane(rows, send, came, *tokens):
     vmem, anywhere = pl.BlockSpec(memory_space=pltpu.VMEM), pl.BlockSpec(memory_space=pl.ANY)
-    keep, send = others
-    came = (move(send, "X", "X"), move(keep, "Y", "Y"), move(send, "XY", "XY"))
-    count, tail = keep.shape[0], keep.shape[1:]
+    count, tail = send.shape[0], send.shape[1:]
     return pl.pallas_call(
         plane_kernel,
         in_specs=[vmem] * 5 + [anywhere] * len(tokens),
@@ -413,11 +433,12 @@
 
     def step(number, part=None):
         source, way0, way1, swap = STEPS[number - 1]
+        block = got[source]
         if part is None:
-            got[number] = move(got[source], way0, way1, swap)
+            got[number] = move(block, way0, way1, swap)
         else:
             width = half // 2
-            got[number, part] = move(got[source][:, part * width : (part + 1) * width], way0, way1, swap)
+            got[number, part] = move(block[:, part * width : (part + 1) * width], way0, way1, swap)
 
     def swap(*numbers):
         for number in numbers:
@@ -437,26 +458,27 @@
     step(2)
     step(3, 0)
     swap(1)
-    rows, *others = sum_cores(partial)
-    rows, *others = sum_plane(rows, others, got[2])
+    rows, keep, send = sum_cores(partial)
+    rows, *sends = sum_plane(rows, send, plane_moves(keep, send), got[2])
     after(2, got[3, 0])
     step(4)
     step(3, 1)
     swap(2)
-    row = sum_line(rows, others, got[4])
+    row = sum_line(rows, sends, got[4])
     after(4, got[3, 1])
     step(5)
-    step(6, 0)
+    step(6)
     swap(4)
     precond = precondition(row, eig_out[0], eig_in[0], eig_values[0]).reshape(1, -1)
     left, total, token = first_scores(stored, precond, queries, pick(EARLY), EARLY, scale, store_count)
     got[3] = jnp.concatenate([got[3, 0], got[3, 1]], axis=1)
-    after(3, token, got[6, 0])
+    after(3, precond)
     step(7)
-    step(6, 1)
+    after(5, token)
     swap(3, 5)
     total = next_scores(left, total, pick(THIRD), THIRD, scale)
-    got[6] = jnp.concatenate([got[6, 0], got[6, 1]], axis=1)
+    after(7, token)
+    after(6, token)
     swap(6, 7)
     scores, group_out = last_scores(query_owner, left, total, pick(LAST), LAST, scale)
     return scores, group_out[None]

time: 63.6 us -> 57.8 us (0.909)
  starting transfers between devices: 29 us -> 25.5 us
  waiting for transfers between devices: 11.9 us -> 10.7 us
  local copies, waits for them, and re-layouts: 5.24 us -> 4.37 us
    ppermute x23 -> x22, starting transfers between devices: 29 us -> 25.5 us  [move(): return lax.ppermute(array, AXES, pairs(way0, way1, swap))]
    ppermute x23 -> x22, waiting for transfers between devices: 11.9 us -> 10.7 us  [move(): return lax.ppermute(array, AXES, pairs(way0, way1, swap))]
    slice x2 -> x1, local copies, waits for them, and re-layouts: 0.86 us -> 0.03 us  [step(): block[:, part * width:(part + 1) * width]]
    unnamed x25 -> x22, local copies, waits for them, and re-layouts: 3.04 us -> 3.02 us
  transfers between devices with their start and end apart: 23 -> 22, of which waited for: 7 -> 7; matrix products, arithmetic and copies ran while one was open for 9% -> 9% of each run, Pallas kernels for 13% -> 14%
where the time goes in v3:
time: 57.8 us; the launch traced here: 57.6 us
  starting transfers between devices  25.5 us (44%)
  Pallas kernels  11.1 us (19%)
  waiting for transfers between devices  10.7 us (19%)
  matrix products  4.97 us (9%)
  local copies, waits for them, and re-layouts  4.37 us (8%)
  between operations  0.93 us (2%)
    ppermute x22, starting transfers between devices, move(): return lax.ppermute(array, AXES, pairs(way0, way1, swap))  25.5 us
    ppermute x22, waiting for transfers between devices, move(): return lax.ppermute(array, AXES, pairs(way0, way1, swap))  10.7 us
    pallas_call x1, Pallas kernels, first_scores(): pl.pallas_call(functools.partial(first_kernel, names=names, scale=scale),...  4.23 us
    dot_general x1, matrix products, project(): jnp.einsum('rd,etd->ert', weight_in, acts, preferred_element_type=jnp.flo...  3.58 us
    pallas_call x1, Pallas kernels, last_scores(): pl.pallas_call(functools.partial(last_kernel, names=names, scale=scale),...  3.05 us
    unnamed x22, local copies, waits for them, and re-layouts  3.02 us
    pallas_call x1, Pallas kernels, next_scores(): pl.pallas_call(functools.partial(next_kernel, names=names, scale=scale),...  2.1 us
    dot_general x1, matrix products, project(): jnp.einsum('rd,etd->ert', weight_out, grads, preferred_element_type=jnp.f...  1.39 us
  transfers between devices with their start and end apart: 22, of which 7 were waited for; matrix products, arithmetic and copies ran while one was open for 9% of the time, Pallas kernels for 14%

profile of v3, /device:TPU:1, one launch (start us, length us, event | category | flops | bytes accessed | tf_op | source)
XLA Modules:
  0.0 57.6 jit_solution(18396606685729128884)
XLA Ops:
  0.6 0.0 copy-start
  0.7 1.2 %constant_dynamic-slice_fusion = bf16[128,2048]{1,0:T(8,128)(2,1)S(1)} fusion(bf16[128,4096]{1,0:T(8,128)(2,1)} %own.1, s32[]{:T(128)S(6)} %select_n.21), kind=kLoop, calls=%fused_computation.9 | loop fusion | bytes 1048580 | tf_op jit(solution)/shard_map/dynamic_slice | solution.py:429
  1.9 0.0 copy-start.5
  2.0 0.0 copy-start.6
  2.0 2.7 %collective-permute-start.4 = (bf16[128,2048]{1,0:T(8,128)(2,1)S(1)}, bf16[128,2048]{1,0:T(8,128)(2,1)S(1)}, u32[]{:S(2)}, u32[]{:S(2)}) collective-permute-start(bf16[128,2048]{1,0:T(8,128)(2,1)S(1)} %constant_dynamic-slice_fusion), channel_id=1, source_target_pairs={{0,17},{1,4},{2,19},{3,6},{4,21},{5,0},{6,23},{7,2},{8,1},{9,12},{... | collective-permute-start | bytes 1572872 | tf_op jit(solution)/shard_map/ppermute | solution.py:70
  4.6 3.6 %fusion.4.in_side = f32[2,64,256]{2,1,0:T(8,128)S(1)} fusion(bf16[1,2,256,4096]{3,2,1,0:T(8,128)(2,1)} %param.12, bf16[1,64,4096]{2,1,0:T(8,128)(2,1)S(1)} %copy-done), kind=kOutput, calls=%fused_computation.4 | convolution fusion | flops 268435456 | bytes 4849664 | tf_op jit(solution)/shard_map/rd,etd->ert/dot_general | solution.py:140
  8.2 1.4 %fusion.7.out_side = f32[2,64,256]{2,1,0:T(8,128)S(1)} fusion(bf16[1,2,256,4096]{3,2,1,0:T(8,128)(2,1)S(1)} %copy-done.9, bf16[1,64,4096]{2,1,0:T(8,128)(2,1)S(1)} %copy-done.10), kind=kOutput, calls=%fused_computation.5 | convolution fusion | flops 268435456 | bytes 4849664 | tf_op jit(solution)/shard_map/rd,etd->ert/dot_general | solution.py:141
  9.6 0.0 copy-done.5
  9.6 0.0 copy-start.2
  9.6 0.0 copy-start.3
  9.7 0.0 copy-start.4
  9.7 0.9 %shard_map.131.rows.refs_0_ = f32[8,32,128]{2,1,0:T(8,128)S(1)} custom-call(s32[2]{0:T(128)S(1)} %copy-done.5, s32[2]{0:T(128)S(1)} %copy-done.6, f32[2,64,256]{2,1,0:T(8,128)S(1)} %fusion.4.in_side, f32[2,64,256]{2,1,0:T(8,128)S(1)} %fusion.7.out_side), custom_call_target="tpu_custom_call" | custom-call | flops 67108864 | bytes 524288 | tf_op jit(solution)/shard_map/pallas_call | solution.py:144
  10.6 1.0 %collective-permute-done.4.block = bf16[128,2048]{1,0:T(8,128)(2,1)S(1)} collective-permute-done((bf16[128,2048]{1,0:T(8,128)(2,1)S(1)}, bf16[128,2048]{1,0:T(8,128)(2,1)S(1)}, u32[]{:S(2)}, u32[]{:S(2)}) %collective-permute-start.4) | collective-permute-done | bytes 524320 | tf_op jit(solution)/shard_map/ppermute | solution.py:70
  11.6 1.4 %collective-permute-start.5 = (bf16[128,2048]{1,0:T(8,128)(2,1)S(1)}, bf16[128,2048]{1,0:T(8,128)(2,1)S(1)}, u32[]{:S(2)}, u32[]{:S(2)}) collective-permute-start(bf16[128,2048]{1,0:T(8,128)(2,1)S(1)} %shard_map.133.refs_0_), channel_id=1, source_target_pairs={{0,8},{1,5},{2,10},{3,7},{4,12},{5,1},{6,14},{7,3},{8,24},{9,13},{... | collective-permute-start | bytes 1572872 | tf_op jit(solution)/shard_map/ppermute | solution.py:70
  13.0 1.3 %collective-permute-start.9 = (bf16[128,1024]{1,0:T(8,128)(2,1)S(1)}, bf16[128,1024]{1,0:T(8,128)(2,1)S(1)}, u32[]{:S(2)}, u32[]{:S(2)}) collective-permute-start(bf16[128,1024]{1,0:T(8,128)(2,1)S(1)} %get-tuple-element.27), channel_id=1, source_target_pairs={{0,2},{1,3},{2,0},{3,1},{4,6},{5,7},{6,4},{7,5},{8,10},{9,11},{10,... | collective-permute-start | bytes 786440 | tf_op jit(solution)/shard_map/ppermute | solution.py:70
  14.3 1.0 %collective-permute-start = (f32[8,32,128]{2,1,0:T(8,128)S(1)}, f32[8,32,128]{2,1,0:T(8,128)S(1)}, u32[]{:S(2)}, u32[]{:S(2)}) collective-permute-start(f32[8,32,128]{2,1,0:T(8,128)S(1)} %shard_map.131.rows.refs_0_), channel_id=1, source_target_pairs={{0,1},{1,0},{2,3},{3,2},{4,5},{5,4},{6,7},{7,6},{8,9},{9,8},{10,11... | collective-permute-start | bytes 393224 | tf_op jit(solution)/shard_map/ppermute | solution.py:70
  15.3 1.0 %collective-permute-done.other = f32[8,32,128]{2,1,0:T(8,128)S(1)} collective-permute-done((f32[8,32,128]{2,1,0:T(8,128)S(1)}, f32[8,32,128]{2,1,0:T(8,128)S(1)}, u32[]{:S(2)}, u32[]{:S(2)}) %collective-permute-start) | collective-permute-done | bytes 131104 | tf_op jit(solution)/shard_map/ppermute | solution.py:70
  16.3 0.3 collective-permute-start.1
  16.6 1.2 %collective-permute-start.2 = (f32[4,32,128]{2,1,0:T(8,128)S(1)}, f32[4,32,128]{2,1,0:T(8,128)S(1)}, u32[]{:S(2)}, u32[]{:S(2)}) collective-permute-start(f32[4,32,128]{2,1,0:T(8,128)S(1)} %get-tuple-element.15.sent), channel_id=1, source_target_pairs={{0,4},{1,5},{2,6},{3,7},{4,0},{5,1},{6,2},{7,3},{8,12},{9,13},{10,... | collective-permute-start | bytes 196616 | tf_op jit(solution)/shard_map/ppermute | solution.py:70
  17.9 1.2 %collective-permute-start.3 = (f32[4,32,128]{2,1,0:T(8,128)S(1)}, f32[4,32,128]{2,1,0:T(8,128)S(1)}, u32[]{:S(2)}, u32[]{:S(2)}) collective-permute-start(f32[4,32,128]{2,1,0:T(8,128)S(1)} %get-tuple-element.15.sent), channel_id=1, source_target_pairs={{0,6},{1,7},{2,4},{3,5},{4,2},{5,3},{6,0},{7,1},{8,14},{9,15},{10,... | collective-permute-start | bytes 196616 | tf_op jit(solution)/shard_map/ppermute | solution.py:70
  19.1 2.5 %collective-permute-done.1.refs_0_ = f32[4,32,128]{2,1,0:T(8,128)S(1)} collective-permute-done((f32[4,32,128]{2,1,0:T(8,128)S(1)}, f32[4,32,128]{2,1,0:T(8,128)S(1)}, u32[]{:S(2)}, u32[]{:S(2)}) %collective-permute-start.1) | collective-permute-done | bytes 65568 | tf_op jit(solution)/shard_map/ppermute | solution.py:70
  21.5 0.0 collective-permute-done.2.refs_1_
  21.5 1.8 %collective-permute-done.3.refs_2_ = f32[4,32,128]{2,1,0:T(8,128)S(1)} collective-permute-done((f32[4,32,128]{2,1,0:T(8,128)S(1)}, f32[4,32,128]{2,1,0:T(8,128)S(1)}, u32[]{:S(2)}, u32[]{:S(2)}) %collective-permute-start.3) | collective-permute-done | bytes 65568 | tf_op jit(solution)/shard_map/ppermute | solution.py:70
  23.4 0.0 collective-permute-done.5.refs_3_.block
  23.4 0.0 collective-permute-done.9.refs_0_
  23.4 3.1 %collective-permute-start.10 = (bf16[128,2048]{1,0:T(8,128)(2,1)S(1)}, bf16[128,2048]{1,0:T(8,128)(2,1)S(1)}, u32[]{:S(2)}, u32[]{:S(2)}) collective-permute-start(bf16[128,2048]{1,0:T(8,128)(2,1)S(1)} %shard_map.135.refs_2_), channel_id=1, source_target_pairs={{0,4},{1,17},{2,6},{3,19},{4,0},{5,21},{6,2},{7,23},{8,12},{9,1},{... | collective-permute-start | bytes 1572872 | tf_op jit(solution)/shard_map/ppermute | solution.py:70
  26.6 1.1 %collective-permute-start.12 = (bf16[128,1024]{1,0:T(8,128)(2,1)S(1)}, bf16[128,1024]{1,0:T(8,128)(2,1)S(1)}, u32[]{:S(2)}, u32[]{:S(2)}) collective-permute-start(bf16[128,1024]{1,0:T(8,128)(2,1)S(1)} %get-tuple-element.26), channel_id=1, source_target_pairs={{0,2},{1,3},{2,0},{3,1},{4,6},{5,7},{6,4},{7,5},{8,10},{9,11},{10,... | collective-permute-start | bytes 786440 | tf_op jit(solution)/shard_map/ppermute | solution.py:70
  27.7 0.0 collective-permute-start.6
  27.7 1.5 %collective-permute-start.7 = (f32[1,32,128]{2,1,0:T(8,128)S(1)}, f32[1,32,128]{2,1,0:T(8,128)S(1)}, u32[]{:S(2)}, u32[]{:S(2)}) collective-permute-start(f32[1,32,128]{2,1,0:T(8,128)S(1)} %get-tuple-element.19), channel_id=1, source_target_pairs={{0,16},{1,17},{2,18},{3,19},{4,20},{5,21},{6,22},{7,23},{8,24},{9,... | collective-permute-start | bytes 49160 | tf_op jit(solution)/shard_map/ppermute | solution.py:70
  29.1 2.1 %collective-permute-start.8 = (f32[1,32,128]{2,1,0:T(8,128)S(1)}, f32[1,32,128]{2,1,0:T(8,128)S(1)}, u32[]{:S(2)}, u32[]{:S(2)}) collective-permute-start(f32[1,32,128]{2,1,0:T(8,128)S(1)} %get-tuple-element.20), channel_id=1, source_target_pairs={{0,24},{1,25},{2,26},{3,27},{4,28},{5,29},{6,30},{7,31},{8,16},{9,... | collective-permute-start | bytes 49160 | tf_op jit(solution)/shard_map/ppermute | solution.py:70
  31.2 2.2 %collective-permute-done.6.refs_0_ = f32[1,32,128]{2,1,0:T(8,128)S(1)} collective-permute-done((f32[1,32,128]{2,1,0:T(8,128)S(1)}, f32[1,32,128]{2,1,0:T(8,128)S(1)}, u32[]{:S(2)}, u32[]{:S(2)}) %collective-permute-start.6) | collective-permute-done | bytes 16416 | tf_op jit(solution)/shard_map/ppermute | solution.py:70
  33.4 0.0 collective-permute-start.11
  33.4 0.2 collective-permute-done.7.refs_1_
  33.6 2.3 %collective-permute-start.13 = (bf16[128,2048]{1,0:T(8,128)(2,1)S(1)}, bf16[128,2048]{1,0:T(8,128)(2,1)}, u32[]{:S(2)}, u32[]{:S(2)}) collective-permute-start(bf16[128,2048]{1,0:T(8,128)(2,1)S(1)} %shard_map.135.refs_2_), channel_id=1, source_target_pairs={{0,1},{1,0},{2,3},{3,2},{4,5},{5,4},{6,7},{7,6},{8,9},{9,8},{10,11... | collective-permute-start | bytes 1572872 | tf_op jit(solution)/shard_map/ppermute | solution.py:70
  35.9 0.0 collective-permute-done.8.refs_2_
  35.9 0.0 collective-permute-done.10.refs_3_.block
  35.9 0.0 collective-permute-done.12.refs_0_
  35.9 0.7 %collective-permute-start.14 = (bf16[128,2048]{1,0:T(8,128)(2,1)S(1)}, bf16[128,2048]{1,0:T(8,128)(2,1)}, u32[]{:S(2)}, u32[]{:S(2)}) collective-permute-start(bf16[128,2048]{1,0:T(8,128)(2,1)S(1)} %shard_map.138.refs_3_), channel_id=1, source_target_pairs={{0,1},{1,0},{2,3},{3,2},{4,5},{5,4},{6,7},{7,6},{8,9},{9,8},{10,11... | collective-permute-start | bytes 1572872 | tf_op jit(solution)/shard_map/ppermute | solution.py:70
  36.6 1.3 %collective-permute-start.15 = (bf16[128,2048]{1,0:T(8,128)(2,1)S(1)}, bf16[128,2048]{1,0:T(8,128)(2,1)}, u32[]{:S(2)}, u32[]{:S(2)}) collective-permute-start(bf16[128,2048]{1,0:T(8,128)(2,1)S(1)} %shard_map.138.refs_3_), channel_id=1, source_target_pairs={{0,8},{1,5},{2,10},{3,7},{4,12},{5,1},{6,14},{7,3},{8,24},{9,13},{... | collective-permute-start | bytes 1572872 | tf_op jit(solution)/shard_map/ppermute | solution.py:70
  37.9 0.2 collective-permute-start.18
  38.1 0.0 copy-done.2
  38.1 0.0 copy-done.4
  38.1 0.8 %shard_map.137 = bf16[64,64]{1,0:T(8,128)(2,1)S(1)} custom-call(f32[32,128]{1,0:T(8,128)S(1)} %shard_map.136.group, f32[64,64]{1,0:T(8,128)S(1)} %bitcast.26, f32[64,64]{1,0:T(8,128)S(1)} %bitcast.27, f32[64,64]{1,0:T(8,128)S(1)} %bitcast.28), custom_call_target="tpu_custom_call" | custom-call | flops 16777216 | bytes 131072 | tf_op jit(solution)/shard_map/pallas_call | solution.py:170
  38.9 0.1 reshape.7.row.refs_0_
  39.0 0.0 collective-permute-done.11.refs_1_
  39.0 0.5 collective-permute-start.17
  39.5 0.0 collective-permute-done.13.refs_4_
  39.5 0.5 collective-permute-start.19
  40.0 0.0 collective-permute-done.14.refs_5_
  40.0 1.2 %copy-done.1 = bf16[128,4096]{1,0:T(8,128)(2,1)S(1)} copy-done((bf16[128,4096]{1,0:T(8,128)(2,1)S(1)}, bf16[128,4096]{1,0:T(8,128)(2,1)}, u32[]{:S(2)}) %copy-start.1) | copy-done | bytes 1048600
  41.2 1.7 %copy-done.8 = bf16[320,4096]{1,0:T(8,128)(2,1)S(1)} copy-done((bf16[320,4096]{1,0:T(8,128)(2,1)S(1)}, bf16[320,4096]{1,0:T(8,128)(2,1)}, u32[]{:S(2)}) %copy-start.8) | copy-done | bytes 2621464
  43.0 4.2 %shard_map.139 = (bf16[336,4096]{1,0:T(8,128)(2,1)S(1)}, f32[8,336,128]{2,1,0:T(8,128)S(1)}, f32[8,128]{1,0:T(8,128)S(1)}) custom-call(bf16[320,4096]{1,0:T(8,128)(2,1)S(1)} %copy-done.8, bf16[1,4096]{1,0:T(2,128)(2,1)S(1)} %reshape.7.row.refs_0_, bf16[128,4096]{1,0:T(8,128)(2,1)S(1)} %copy-done.1, bf16[128,2048]{1,0:T(8,128)(2,1)S(1)} %shard_map.133.refs_0_, ...), custom_call_target="tpu_custom_call" | custom-call | flops 8589934592 | bytes 1024 | tf_op jit(solution)/shard_map/pallas_call | solution.py:231
  47.2 0.0 collective-permute-done.15.block
  47.2 2.3 %collective-permute-start.16 = (bf16[128,2048]{1,0:T(8,128)(2,1)}, bf16[128,2048]{1,0:T(8,128)(2,1)S(1)}, u32[]{:S(2)}, u32[]{:S(2)}) collective-permute-start(bf16[128,2048]{1,0:T(8,128)(2,1)} %shard_map.141.refs_3_), channel_id=1, source_target_pairs={{0,1},{1,0},{2,3},{3,2},{4,5},{5,4},{6,7},{7,6},{8,9},{9,8},{10,11... | collective-permute-start | bytes 1572872 | tf_op jit(solution)/shard_map/ppermute | solution.py:70
  49.5 2.0 %collective-permute-done.18.block = bf16[128,2048]{1,0:T(8,128)(2,1)S(1)} collective-permute-done((bf16[128,2048]{1,0:T(8,128)(2,1)S(1)}, bf16[128,2048]{1,0:T(8,128)(2,1)S(1)}, u32[]{:S(2)}, u32[]{:S(2)}) %collective-permute-start.18) | collective-permute-done | bytes 524320 | tf_op jit(solution)/shard_map/ppermute | solution.py:70
  51.5 0.1 collective-permute-start.20
  51.6 0.0 collective-permute-done.19.block
  51.6 0.8 %collective-permute-start.21 = (bf16[128,2048]{1,0:T(8,128)(2,1)S(1)}, bf16[128,2048]{1,0:T(8,128)(2,1)S(1)}, u32[]{:S(2)}, u32[]{:S(2)}) collective-permute-start(bf16[128,2048]{1,0:T(8,128)(2,1)S(1)} %shard_map.144.refs_1_), channel_id=1, source_target_pairs={{0,1},{1,0},{2,3},{3,2},{4,5},{5,4},{6,7},{7,6},{8,9},{9,8},{10,11... | collective-permute-start | bytes 1572872 | tf_op jit(solution)/shard_map/ppermute | solution.py:70
  52.4 0.0 collective-permute-done.17.refs_2_
  52.4 0.0 collective-permute-done.16.refs_1_
  52.4 2.1 %shard_map.142.before = f32[8,336,128]{2,1,0:T(8,128)S(1)} custom-call(bf16[336,4096]{1,0:T(8,128)(2,1)S(1)} %get-tuple-element.21.left, f32[8,336,128]{2,1,0:T(8,128)S(1)} %get-tuple-element.22.before, bf16[128,2048]{1,0:T(8,128)(2,1)S(1)} %shard_map.140.refs_0_, bf16[128,2048]{1,0:T(8,128)(2,1)S(1)} %collective-permute-done.16.refs_1_, ...), custom_call_target="tpu_custom_call" | custom-call | flops 4294967296 | bytes 1024 | tf_op jit(solution)/shard_map/pallas_call | solution.py:260
  54.5 0.0 collective-permute-done.20.refs_2_
  54.5 0.0 collective-permute-done.21.refs_3_
  54.5 3.0 %shard_map.145 = (f32[8,320,128]{2,1,0:T(8,128)}, f32[8,128]{1,0:T(8,128)}) custom-call(s32[8]{0:T(128)S(1)} %copy-done.7, bf16[336,4096]{1,0:T(8,128)(2,1)S(1)} %get-tuple-element.21.left, f32[8,336,128]{2,1,0:T(8,128)S(1)} %shard_map.142.before, bf16[128,2048]{1,0:T(8,128)(2,1)S(1)} %shard_map.143.refs_0_, bf16[128,2048]{1,0:T(8,128)(2,1)S(1)} %shard_map.144.refs_1_, ...), custom_call_target="tpu_custom_call" | custom-call | flops 1073741824 | bytes 8388608 | tf_op jit(solution)/shard_map/pallas_call | solution.py:312
  (23 shorter events, 0.2 us)
Async XLA Ops:
  0.6 4.0 %copy-start = (bf16[1,64,4096]{2,1,0:T(8,128)(2,1)S(1)}, bf16[1,64,4096]{2,1,0:T(8,128)(2,1)}, u32[]{:S(2)}) copy-start(bf16[1,64,4096]{2,1,0:T(8,128)(2,1)} %param.14) | copy-start | bytes 1572868
  0.6 7.6 %copy-start.10 = (bf16[1,64,4096]{2,1,0:T(8,128)(2,1)S(1)}, bf16[1,64,4096]{2,1,0:T(8,128)(2,1)}, u32[]{:S(2)}) copy-start(bf16[1,64,4096]{2,1,0:T(8,128)(2,1)} %param.15) | copy-start | bytes 1572868
  0.7 7.5 %copy-start.9 = (bf16[1,2,256,4096]{3,2,1,0:T(8,128)(2,1)S(1)}, bf16[1,2,256,4096]{3,2,1,0:T(8,128)(2,1)}, u32[]{:S(2)}) copy-start(bf16[1,2,256,4096]{3,2,1,0:T(8,128)(2,1)} %param.13) | copy-start | bytes 12582916
  1.9 7.7 %copy-start.5 = (s32[2]{0:T(128)S(1)}, s32[2]{0:T(128)}, u32[]{:S(2)}) copy-start(s32[2]{0:T(128)} %lengths.1) | copy-start | bytes 28
  2.0 7.7 %copy-start.6 = (s32[2]{0:T(128)S(1)}, s32[2]{0:T(128)}, u32[]{:S(2)}) copy-start(s32[2]{0:T(128)} %owners.1) | copy-start | bytes 28
  2.0 9.6 %collective-permute-start.4 = (bf16[128,2048]{1,0:T(8,128)(2,1)S(1)}, bf16[128,2048]{1,0:T(8,128)(2,1)S(1)}, u32[]{:S(2)}, u32[]{:S(2)}) collective-permute-start(bf16[128,2048]{1,0:T(8,128)(2,1)S(1)} %constant_dynamic-slice_fusion), channel_id=1, source_target_pairs={{0,17},{1,4},{2,19},{3,6},{4,21},{5,0},{6,23},{7,2},{8,1},{9,12},{... | collective-permute-start | bytes 1572872 | tf_op jit(solution)/shard_map/ppermute | solution.py:70
  9.6 28.5 %copy-start.2 = (f32[1,64,64]{2,1,0:T(8,128)S(1)}, f32[1,64,64]{2,1,0:T(8,128)}, u32[]{:S(2)}) copy-start(f32[1,64,64]{2,1,0:T(8,128)} %param.16) | copy-start | bytes 49156
  9.6 28.5 %copy-start.3 = (f32[1,64,64]{2,1,0:T(8,128)S(1)}, f32[1,64,64]{2,1,0:T(8,128)}, u32[]{:S(2)}) copy-start(f32[1,64,64]{2,1,0:T(8,128)} %param.17) | copy-start | bytes 49156
  9.7 28.4 %copy-start.4 = (f32[1,64,64]{2,1,0:T(8,128)S(1)}, f32[1,64,64]{2,1,0:T(8,128)}, u32[]{:S(2)}) copy-start(f32[1,64,64]{2,1,0:T(8,128)} %param.18) | copy-start | bytes 49156
  11.6 11.8 %collective-permute-start.5 = (bf16[128,2048]{1,0:T(8,128)(2,1)S(1)}, bf16[128,2048]{1,0:T(8,128)(2,1)S(1)}, u32[]{:S(2)}, u32[]{:S(2)}) collective-permute-start(bf16[128,2048]{1,0:T(8,128)(2,1)S(1)} %shard_map.133.refs_0_), channel_id=1, source_target_pairs={{0,8},{1,5},{2,10},{3,7},{4,12},{5,1},{6,14},{7,3},{8,24},{9,13},{... | collective-permute-start | bytes 1572872 | tf_op jit(solution)/shard_map/ppermute | solution.py:70
  13.0 10.4 %collective-permute-start.9 = (bf16[128,1024]{1,0:T(8,128)(2,1)S(1)}, bf16[128,1024]{1,0:T(8,128)(2,1)S(1)}, u32[]{:S(2)}, u32[]{:S(2)}) collective-permute-start(bf16[128,1024]{1,0:T(8,128)(2,1)S(1)} %get-tuple-element.27), channel_id=1, source_target_pairs={{0,2},{1,3},{2,0},{3,1},{4,6},{5,7},{6,4},{7,5},{8,10},{9,11},{10,... | collective-permute-start | bytes 786440 | tf_op jit(solution)/shard_map/ppermute | solution.py:70
  14.3 2.0 %collective-permute-start = (f32[8,32,128]{2,1,0:T(8,128)S(1)}, f32[8,32,128]{2,1,0:T(8,128)S(1)}, u32[]{:S(2)}, u32[]{:S(2)}) collective-permute-start(f32[8,32,128]{2,1,0:T(8,128)S(1)} %shard_map.131.rows.refs_0_), channel_id=1, source_target_pairs={{0,1},{1,0},{2,3},{3,2},{4,5},{5,4},{6,7},{7,6},{8,9},{9,8},{10,11... | collective-permute-start | bytes 393224 | tf_op jit(solution)/shard_map/ppermute | solution.py:70
  16.3 5.2 %collective-permute-start.1 = (f32[4,32,128]{2,1,0:T(8,128)S(1)}, f32[4,32,128]{2,1,0:T(8,128)S(1)}, u32[]{:S(2)}, u32[]{:S(2)}) collective-permute-start(f32[4,32,128]{2,1,0:T(8,128)S(1)} %get-tuple-element.16), channel_id=1, source_target_pairs={{0,2},{1,3},{2,0},{3,1},{4,6},{5,7},{6,4},{7,5},{8,10},{9,11},{10,... | collective-permute-start | bytes 196616 | tf_op jit(solution)/shard_map/ppermute | solution.py:70
  16.6 4.9 %collective-permute-start.2 = (f32[4,32,128]{2,1,0:T(8,128)S(1)}, f32[4,32,128]{2,1,0:T(8,128)S(1)}, u32[]{:S(2)}, u32[]{:S(2)}) collective-permute-start(f32[4,32,128]{2,1,0:T(8,128)S(1)} %get-tuple-element.15.sent), channel_id=1, source_target_pairs={{0,4},{1,5},{2,6},{3,7},{4,0},{5,1},{6,2},{7,3},{8,12},{9,13},{10,... | collective-permute-start | bytes 196616 | tf_op jit(solution)/shard_map/ppermute | solution.py:70
  17.9 5.5 %collective-permute-start.3 = (f32[4,32,128]{2,1,0:T(8,128)S(1)}, f32[4,32,128]{2,1,0:T(8,128)S(1)}, u32[]{:S(2)}, u32[]{:S(2)}) collective-permute-start(f32[4,32,128]{2,1,0:T(8,128)S(1)} %get-tuple-element.15.sent), channel_id=1, source_target_pairs={{0,6},{1,7},{2,4},{3,5},{4,2},{5,3},{6,0},{7,1},{8,14},{9,15},{10,... | collective-permute-start | bytes 196616 | tf_op jit(solution)/shard_map/ppermute | solution.py:70
  23.4 12.4 %collective-permute-start.10 = (bf16[128,2048]{1,0:T(8,128)(2,1)S(1)}, bf16[128,2048]{1,0:T(8,128)(2,1)S(1)}, u32[]{:S(2)}, u32[]{:S(2)}) collective-permute-start(bf16[128,2048]{1,0:T(8,128)(2,1)S(1)} %shard_map.135.refs_2_), channel_id=1, source_target_pairs={{0,4},{1,17},{2,6},{3,19},{4,0},{5,21},{6,2},{7,23},{8,12},{9,1},{... | collective-permute-start | bytes 1572872 | tf_op jit(solution)/shard_map/ppermute | solution.py:70
  26.6 9.3 %collective-permute-start.12 = (bf16[128,1024]{1,0:T(8,128)(2,1)S(1)}, bf16[128,1024]{1,0:T(8,128)(2,1)S(1)}, u32[]{:S(2)}, u32[]{:S(2)}) collective-permute-start(bf16[128,1024]{1,0:T(8,128)(2,1)S(1)} %get-tuple-element.26), channel_id=1, source_target_pairs={{0,2},{1,3},{2,0},{3,1},{4,6},{5,7},{6,4},{7,5},{8,10},{9,11},{10,... | collective-permute-start | bytes 786440 | tf_op jit(solution)/shard_map/ppermute | solution.py:70
  27.7 5.7 %collective-permute-start.6 = (f32[1,32,128]{2,1,0:T(8,128)S(1)}, f32[1,32,128]{2,1,0:T(8,128)S(1)}, u32[]{:S(2)}, u32[]{:S(2)}) collective-permute-start(f32[1,32,128]{2,1,0:T(8,128)S(1)} %get-tuple-element.18), channel_id=1, source_target_pairs={{0,8},{1,9},{2,10},{3,11},{4,12},{5,13},{6,14},{7,15},{8,0},{9,1},... | collective-permute-start | bytes 49160 | tf_op jit(solution)/shard_map/ppermute | solution.py:70
  27.7 5.9 %collective-permute-start.7 = (f32[1,32,128]{2,1,0:T(8,128)S(1)}, f32[1,32,128]{2,1,0:T(8,128)S(1)}, u32[]{:S(2)}, u32[]{:S(2)}) collective-permute-start(f32[1,32,128]{2,1,0:T(8,128)S(1)} %get-tuple-element.19), channel_id=1, source_target_pairs={{0,16},{1,17},{2,18},{3,19},{4,20},{5,21},{6,22},{7,23},{8,24},{9,... | collective-permute-start | bytes 49160 | tf_op jit(solution)/shard_map/ppermute | solution.py:70
  29.1 6.7 %collective-permute-start.8 = (f32[1,32,128]{2,1,0:T(8,128)S(1)}, f32[1,32,128]{2,1,0:T(8,128)S(1)}, u32[]{:S(2)}, u32[]{:S(2)}) collective-permute-start(f32[1,32,128]{2,1,0:T(8,128)S(1)} %get-tuple-element.20), channel_id=1, source_target_pairs={{0,24},{1,25},{2,26},{3,27},{4,28},{5,29},{6,30},{7,31},{8,16},{9,... | collective-permute-start | bytes 49160 | tf_op jit(solution)/shard_map/ppermute | solution.py:70
  33.4 5.6 %collective-permute-start.11 = (bf16[128,2048]{1,0:T(8,128)(2,1)S(1)}, bf16[128,2048]{1,0:T(8,128)(2,1)}, u32[]{:S(2)}, u32[]{:S(2)}) collective-permute-start(bf16[128,2048]{1,0:T(8,128)(2,1)S(1)} %shard_map.133.refs_0_), channel_id=1, source_target_pairs={{0,1},{1,0},{2,3},{3,2},{4,5},{5,4},{6,7},{7,6},{8,9},{9,8},{10,11... | collective-permute-start | bytes 1572872 | tf_op jit(solution)/shard_map/ppermute | solution.py:70
  33.6 5.9 %collective-permute-start.13 = (bf16[128,2048]{1,0:T(8,128)(2,1)S(1)}, bf16[128,2048]{1,0:T(8,128)(2,1)}, u32[]{:S(2)}, u32[]{:S(2)}) collective-permute-start(bf16[128,2048]{1,0:T(8,128)(2,1)S(1)} %shard_map.135.refs_2_), channel_id=1, source_target_pairs={{0,1},{1,0},{2,3},{3,2},{4,5},{5,4},{6,7},{7,6},{8,9},{9,8},{10,11... | collective-permute-start | bytes 1572872 | tf_op jit(solution)/shard_map/ppermute | solution.py:70
  35.9 4.1 %collective-permute-start.14 = (bf16[128,2048]{1,0:T(8,128)(2,1)S(1)}, bf16[128,2048]{1,0:T(8,128)(2,1)}, u32[]{:S(2)}, u32[]{:S(2)}) collective-permute-start(bf16[128,2048]{1,0:T(8,128)(2,1)S(1)} %shard_map.138.refs_3_), channel_id=1, source_target_pairs={{0,1},{1,0},{2,3},{3,2},{4,5},{5,4},{6,7},{7,6},{8,9},{9,8},{10,11... | collective-permute-start | bytes 1572872 | tf_op jit(solution)/shard_map/ppermute | solution.py:70
  36.6 10.6 %collective-permute-start.15 = (bf16[128,2048]{1,0:T(8,128)(2,1)S(1)}, bf16[128,2048]{1,0:T(8,128)(2,1)}, u32[]{:S(2)}, u32[]{:S(2)}) collective-permute-start(bf16[128,2048]{1,0:T(8,128)(2,1)S(1)} %shard_map.138.refs_3_), channel_id=1, source_target_pairs={{0,8},{1,5},{2,10},{3,7},{4,12},{5,1},{6,14},{7,3},{8,24},{9,13},{... | collective-permute-start | bytes 1572872 | tf_op jit(solution)/shard_map/ppermute | solution.py:70
  37.9 13.6 %collective-permute-start.18 = (bf16[128,2048]{1,0:T(8,128)(2,1)S(1)}, bf16[128,2048]{1,0:T(8,128)(2,1)S(1)}, u32[]{:S(2)}, u32[]{:S(2)}) collective-permute-start(bf16[128,2048]{1,0:T(8,128)(2,1)S(1)} %shard_map.138.refs_3_), channel_id=1, source_target_pairs={{0,2},{1,3},{2,0},{3,1},{4,6},{5,7},{6,4},{7,5},{8,10},{9,11},{10,... | collective-permute-start | bytes 1572872 | tf_op jit(solution)/shard_map/ppermute | solution.py:70
  39.0 13.4 %collective-permute-start.17 = (bf16[128,2048]{1,0:T(8,128)(2,1)S(1)}, bf16[128,2048]{1,0:T(8,128)(2,1)S(1)}, u32[]{:S(2)}, u32[]{:S(2)}) collective-permute-start(bf16[128,2048]{1,0:T(8,128)(2,1)S(1)} %shard_map.140.refs_0_), channel_id=1, source_target_pairs={{0,1},{1,0},{2,3},{3,2},{4,5},{5,4},{6,7},{7,6},{8,9},{9,8},{10,11... | collective-permute-start | bytes 1572872 | tf_op jit(solution)/shard_map/ppermute | solution.py:70
  39.5 12.1 %collective-permute-start.19 = (bf16[128,2048]{1,0:T(8,128)(2,1)S(1)}, bf16[128,2048]{1,0:T(8,128)(2,1)S(1)}, u32[]{:S(2)}, u32[]{:S(2)}) collective-permute-start(bf16[128,2048]{1,0:T(8,128)(2,1)S(1)} %shard_map.140.refs_0_), channel_id=1, source_target_pairs={{0,8},{1,5},{2,10},{3,7},{4,12},{5,1},{6,14},{7,3},{8,24},{9,13},{... | collective-permute-start | bytes 1572872 | tf_op jit(solution)/shard_map/ppermute | solution.py:70
  40.0 1.2 %copy-start.1 = (bf16[128,4096]{1,0:T(8,128)(2,1)S(1)}, bf16[128,4096]{1,0:T(8,128)(2,1)}, u32[]{:S(2)}) copy-start(bf16[128,4096]{1,0:T(8,128)(2,1)} %own.1) | copy-start | bytes 3145732
  41.2 1.7 %copy-start.8 = (bf16[320,4096]{1,0:T(8,128)(2,1)S(1)}, bf16[320,4096]{1,0:T(8,128)(2,1)}, u32[]{:S(2)}) copy-start(bf16[320,4096]{1,0:T(8,128)(2,1)} %stored.1) | copy-start | bytes 7864324
  47.2 5.2 %collective-permute-start.16 = (bf16[128,2048]{1,0:T(8,128)(2,1)}, bf16[128,2048]{1,0:T(8,128)(2,1)S(1)}, u32[]{:S(2)}, u32[]{:S(2)}) collective-permute-start(bf16[128,2048]{1,0:T(8,128)(2,1)} %shard_map.141.refs_3_), channel_id=1, source_target_pairs={{0,1},{1,0},{2,3},{3,2},{4,5},{5,4},{6,7},{7,6},{8,9},{9,8},{10,11... | collective-permute-start | bytes 1572872 | tf_op jit(solution)/shard_map/ppermute | solution.py:70
  51.5 3.0 %collective-permute-start.20 = (bf16[128,2048]{1,0:T(8,128)(2,1)S(1)}, bf16[128,2048]{1,0:T(8,128)(2,1)S(1)}, u32[]{:S(2)}, u32[]{:S(2)}) collective-permute-start(bf16[128,2048]{1,0:T(8,128)(2,1)S(1)} %shard_map.143.refs_0_), channel_id=1, source_target_pairs={{0,1},{1,0},{2,3},{3,2},{4,5},{5,4},{6,7},{7,6},{8,9},{9,8},{10,11... | collective-permute-start | bytes 1572872 | tf_op jit(solution)/shard_map/ppermute | solution.py:70
  51.6 2.9 %collective-permute-start.21 = (bf16[128,2048]{1,0:T(8,128)(2,1)S(1)}, bf16[128,2048]{1,0:T(8,128)(2,1)S(1)}, u32[]{:S(2)}, u32[]{:S(2)}) collective-permute-start(bf16[128,2048]{1,0:T(8,128)(2,1)S(1)} %shard_map.144.refs_1_), channel_id=1, source_target_pairs={{0,1},{1,0},{2,3},{3,2},{4,5},{5,4},{6,7},{7,6},{8,9},{9,8},{10,11... | collective-permute-start | bytes 1572872 | tf_op jit(solution)/shard_map/ppermute | solution.py:70
  52.4 2.1 %copy-start.7 = (s32[8]{0:T(128)S(1)}, s32[8]{0:T(128)}, u32[]{:S(2)}) copy-start(s32[8]{0:T(128)} %query_owner.1) | copy-start | bytes 100

commit v4 on v3

--- a/solution.py
+++ b/solution.py
@@ -292,15 +292,19 @@
         def _(step=step):
             copy_out(before, step).start()
 
-    totals[...] = before[...]
+    for panel in late:
+        totals[panel] = before[panel]
     add_scores(left, None, iter([unit[...] for unit in units]), names, totals, scale)
     for step in range(out.shape[0]):
 
         @pl.when(is_late(step))
         def _(step=step):
             copy_out(totals, step).start()
-
-        group_out[pl.ds(step, 1)] = totals[query_owner[step], rows : rows + 1]
+            group_out[pl.ds(step, 1)] = totals[query_owner[step], rows : rows + 1]
+
+        @pl.when(jnp.logical_not(is_late(step)))
+        def _(step=step):
+            group_out[pl.ds(step, 1)] = before[query_owner[step], rows : rows + 1]
     for step in range(out.shape[0]):
         copy_out(totals, step).wait()
 
@@ -365,7 +369,7 @@
         out_shape=[jax.ShapeDtypeStruct((count,) + tail, jnp.float32)]
         + [jax.ShapeDtypeStruct((1,) + tail, jnp.float32)] * 3,
         compiler_params=pltpu.CompilerParams(vmem_limit_bytes=4 * MIB),
-        cost_estimate=pl.CostEstimate(flops=1 << 16, bytes_accessed=1 << 18, transcendentals=0),
+        cost_estimate=pl.CostEstimate(flops=1 << 28, bytes_accessed=1 << 18, transcendentals=0),
     )(rows, send, *came, *tokens)
 
 
@@ -383,7 +387,7 @@
         out_specs=vmem,
         out_shape=jax.ShapeDtypeStruct(rows.shape[1:], jnp.float32),
         compiler_params=pltpu.CompilerParams(vmem_limit_bytes=4 * MIB),
-        cost_estimate=pl.CostEstimate(flops=1 << 16, bytes_accessed=1 << 18, transcendentals=0),
+        cost_estimate=pl.CostEstimate(flops=1 << 28, bytes_accessed=1 << 18, transcendentals=0),
     )(rows, *came, *tokens)
 
 

time: 57.8 us -> 57.9 us (level)
  no operation moved by 1% of the time
where the time goes in v4:
time: 57.9 us; the launch traced here: 57.7 us
  starting transfers between devices  25.5 us (44%)
  Pallas kernels  11.2 us (19%)
  waiting for transfers between devices  10.7 us (18%)
  matrix products  4.97 us (9%)
  local copies, waits for them, and re-layouts  4.37 us (8%)
  between operations  0.93 us (2%)
    ppermute x22, starting transfers between devices, move(): return lax.ppermute(array, AXES, pairs(way0, way1, swap))  25.5 us
    ppermute x22, waiting for transfers between devices, move(): return lax.ppermute(array, AXES, pairs(way0, way1, swap))  10.7 us
    pallas_call x1, Pallas kernels, first_scores(): pl.pallas_call(functools.partial(first_kernel, names=names, scale=scale),...  4.23 us
    dot_general x1, matrix products, project(): jnp.einsum('rd,etd->ert', weight_in, acts, preferred_element_type=jnp.flo...  3.58 us
    pallas_call x1, Pallas kernels, last_scores(): pl.pallas_call(functools.partial(last_kernel, names=names, scale=scale),...  3.16 us
    unnamed x22, local copies, waits for them, and re-layouts  3.02 us
    pallas_call x1, Pallas kernels, next_scores(): pl.pallas_call(functools.partial(next_kernel, names=names, scale=scale),...  2.1 us
    dot_general x1, matrix products, project(): jnp.einsum('rd,etd->ert', weight_out, grads, preferred_element_type=jnp.f...  1.39 us
  transfers between devices with their start and end apart: 22, of which 7 were waited for; matrix products, arithmetic and copies ran while one was open for 9% of the time, Pallas kernels for 14%

profile of v4, /device:TPU:1, one launch (start us, length us, event | category | flops | bytes accessed | tf_op | source)
XLA Modules:
  0.0 57.7 jit_solution(6179489071389513574)
XLA Ops:
  0.6 0.0 copy-start
  0.6 0.0 copy-start.10
  0.7 0.0 copy-start.9
  0.7 1.2 %constant_dynamic-slice_fusion = bf16[128,2048]{1,0:T(8,128)(2,1)S(1)} fusion(bf16[128,4096]{1,0:T(8,128)(2,1)} %own.1, s32[]{:T(128)S(6)} %select_n.21), kind=kLoop, calls=%fused_computation.9 | loop fusion | bytes 1048580 | tf_op jit(solution)/shard_map/dynamic_slice | solution.py:433
  1.9 0.0 copy-start.5
  2.0 0.0 copy-start.6
  2.0 2.7 %collective-permute-start.4 = (bf16[128,2048]{1,0:T(8,128)(2,1)S(1)}, bf16[128,2048]{1,0:T(8,128)(2,1)S(1)}, u32[]{:S(2)}, u32[]{:S(2)}) collective-permute-start(bf16[128,2048]{1,0:T(8,128)(2,1)S(1)} %constant_dynamic-slice_fusion), channel_id=1, source_target_pairs={{0,17},{1,4},{2,19},{3,6},{4,21},{5,0},{6,23},{7,2},{8,1},{9,12},{... | collective-permute-start | bytes 1572872 | tf_op jit(solution)/shard_map/ppermute | solution.py:70
  4.6 3.6 %fusion.4.in_side = f32[2,64,256]{2,1,0:T(8,128)S(1)} fusion(bf16[1,2,256,4096]{3,2,1,0:T(8,128)(2,1)} %param.12, bf16[1,64,4096]{2,1,0:T(8,128)(2,1)S(1)} %copy-done), kind=kOutput, calls=%fused_computation.4 | convolution fusion | flops 268435456 | bytes 4849664 | tf_op jit(solution)/shard_map/rd,etd->ert/dot_general | solution.py:140
  8.2 1.4 %fusion.7.out_side = f32[2,64,256]{2,1,0:T(8,128)S(1)} fusion(bf16[1,2,256,4096]{3,2,1,0:T(8,128)(2,1)S(1)} %copy-done.9, bf16[1,64,4096]{2,1,0:T(8,128)(2,1)S(1)} %copy-done.10), kind=kOutput, calls=%fused_computation.5 | convolution fusion | flops 268435456 | bytes 4849664 | tf_op jit(solution)/shard_map/rd,etd->ert/dot_general | solution.py:141
  9.6 0.0 copy-start.2
  9.6 0.0 copy-start.3
  9.7 0.0 copy-start.4
  9.7 0.9 %shard_map.131.rows.refs_0_ = f32[8,32,128]{2,1,0:T(8,128)S(1)} custom-call(s32[2]{0:T(128)S(1)} %copy-done.5, s32[2]{0:T(128)S(1)} %copy-done.6, f32[2,64,256]{2,1,0:T(8,128)S(1)} %fusion.4.in_side, f32[2,64,256]{2,1,0:T(8,128)S(1)} %fusion.7.out_side), custom_call_target="tpu_custom_call" | custom-call | flops 67108864 | bytes 524288 | tf_op jit(solution)/shard_map/pallas_call | solution.py:144
  10.6 1.0 %collective-permute-done.4.block = bf16[128,2048]{1,0:T(8,128)(2,1)S(1)} collective-permute-done((bf16[128,2048]{1,0:T(8,128)(2,1)S(1)}, bf16[128,2048]{1,0:T(8,128)(2,1)S(1)}, u32[]{:S(2)}, u32[]{:S(2)}) %collective-permute-start.4) | collective-permute-done | bytes 524320 | tf_op jit(solution)/shard_map/ppermute | solution.py:70
  11.6 1.4 %collective-permute-start.5 = (bf16[128,2048]{1,0:T(8,128)(2,1)S(1)}, bf16[128,2048]{1,0:T(8,128)(2,1)S(1)}, u32[]{:S(2)}, u32[]{:S(2)}) collective-permute-start(bf16[128,2048]{1,0:T(8,128)(2,1)S(1)} %shard_map.133.refs_0_), channel_id=1, source_target_pairs={{0,8},{1,5},{2,10},{3,7},{4,12},{5,1},{6,14},{7,3},{8,24},{9,13},{... | collective-permute-start | bytes 1572872 | tf_op jit(solution)/shard_map/ppermute | solution.py:70
  13.0 1.3 %collective-permute-start.9 = (bf16[128,1024]{1,0:T(8,128)(2,1)S(1)}, bf16[128,1024]{1,0:T(8,128)(2,1)S(1)}, u32[]{:S(2)}, u32[]{:S(2)}) collective-permute-start(bf16[128,1024]{1,0:T(8,128)(2,1)S(1)} %get-tuple-element.27), channel_id=1, source_target_pairs={{0,2},{1,3},{2,0},{3,1},{4,6},{5,7},{6,4},{7,5},{8,10},{9,11},{10,... | collective-permute-start | bytes 786440 | tf_op jit(solution)/shard_map/ppermute | solution.py:70
  14.3 1.0 %collective-permute-start = (f32[8,32,128]{2,1,0:T(8,128)S(1)}, f32[8,32,128]{2,1,0:T(8,128)S(1)}, u32[]{:S(2)}, u32[]{:S(2)}) collective-permute-start(f32[8,32,128]{2,1,0:T(8,128)S(1)} %shard_map.131.rows.refs_0_), channel_id=1, source_target_pairs={{0,1},{1,0},{2,3},{3,2},{4,5},{5,4},{6,7},{7,6},{8,9},{9,8},{10,11... | collective-permute-start | bytes 393224 | tf_op jit(solution)/shard_map/ppermute | solution.py:70
  15.3 1.0 %collective-permute-done.other = f32[8,32,128]{2,1,0:T(8,128)S(1)} collective-permute-done((f32[8,32,128]{2,1,0:T(8,128)S(1)}, f32[8,32,128]{2,1,0:T(8,128)S(1)}, u32[]{:S(2)}, u32[]{:S(2)}) %collective-permute-start) | collective-permute-done | bytes 131104 | tf_op jit(solution)/shard_map/ppermute | solution.py:70
  16.3 0.3 collective-permute-start.1
  16.6 1.2 %collective-permute-start.2 = (f32[4,32,128]{2,1,0:T(8,128)S(1)}, f32[4,32,128]{2,1,0:T(8,128)S(1)}, u32[]{:S(2)}, u32[]{:S(2)}) collective-permute-start(f32[4,32,128]{2,1,0:T(8,128)S(1)} %get-tuple-element.15.sent), channel_id=1, source_target_pairs={{0,4},{1,5},{2,6},{3,7},{4,0},{5,1},{6,2},{7,3},{8,12},{9,13},{10,... | collective-permute-start | bytes 196616 | tf_op jit(solution)/shard_map/ppermute | solution.py:70
  17.9 1.2 %collective-permute-start.3 = (f32[4,32,128]{2,1,0:T(8,128)S(1)}, f32[4,32,128]{2,1,0:T(8,128)S(1)}, u32[]{:S(2)}, u32[]{:S(2)}) collective-permute-start(f32[4,32,128]{2,1,0:T(8,128)S(1)} %get-tuple-element.15.sent), channel_id=1, source_target_pairs={{0,6},{1,7},{2,4},{3,5},{4,2},{5,3},{6,0},{7,1},{8,14},{9,15},{10,... | collective-permute-start | bytes 196616 | tf_op jit(solution)/shard_map/ppermute | solution.py:70
  19.1 2.5 %collective-permute-done.1.refs_0_ = f32[4,32,128]{2,1,0:T(8,128)S(1)} collective-permute-done((f32[4,32,128]{2,1,0:T(8,128)S(1)}, f32[4,32,128]{2,1,0:T(8,128)S(1)}, u32[]{:S(2)}, u32[]{:S(2)}) %collective-permute-start.1) | collective-permute-done | bytes 65568 | tf_op jit(solution)/shard_map/ppermute | solution.py:70
  21.5 0.0 collective-permute-done.2.refs_1_
  21.5 1.8 %collective-permute-done.3.refs_2_ = f32[4,32,128]{2,1,0:T(8,128)S(1)} collective-permute-done((f32[4,32,128]{2,1,0:T(8,128)S(1)}, f32[4,32,128]{2,1,0:T(8,128)S(1)}, u32[]{:S(2)}, u32[]{:S(2)}) %collective-permute-start.3) | collective-permute-done | bytes 65568 | tf_op jit(solution)/shard_map/ppermute | solution.py:70
  23.4 0.0 collective-permute-done.5.refs_3_.block
  23.4 0.0 collective-permute-done.9.refs_0_
  23.4 3.1 %collective-permute-start.10 = (bf16[128,2048]{1,0:T(8,128)(2,1)S(1)}, bf16[128,2048]{1,0:T(8,128)(2,1)S(1)}, u32[]{:S(2)}, u32[]{:S(2)}) collective-permute-start(bf16[128,2048]{1,0:T(8,128)(2,1)S(1)} %shard_map.135.refs_2_), channel_id=1, source_target_pairs={{0,4},{1,17},{2,6},{3,19},{4,0},{5,21},{6,2},{7,23},{8,12},{9,1},{... | collective-permute-start | bytes 1572872 | tf_op jit(solution)/shard_map/ppermute | solution.py:70
  26.6 1.1 %collective-permute-start.12 = (bf16[128,1024]{1,0:T(8,128)(2,1)S(1)}, bf16[128,1024]{1,0:T(8,128)(2,1)S(1)}, u32[]{:S(2)}, u32[]{:S(2)}) collective-permute-start(bf16[128,1024]{1,0:T(8,128)(2,1)S(1)} %get-tuple-element.26), channel_id=1, source_target_pairs={{0,2},{1,3},{2,0},{3,1},{4,6},{5,7},{6,4},{7,5},{8,10},{9,11},{10,... | collective-permute-start | bytes 786440 | tf_op jit(solution)/shard_map/ppermute | solution.py:70
  27.7 0.0 collective-permute-start.6
  27.7 1.5 %collective-permute-start.7 = (f32[1,32,128]{2,1,0:T(8,128)S(1)}, f32[1,32,128]{2,1,0:T(8,128)S(1)}, u32[]{:S(2)}, u32[]{:S(2)}) collective-permute-start(f32[1,32,128]{2,1,0:T(8,128)S(1)} %get-tuple-element.19), channel_id=1, source_target_pairs={{0,16},{1,17},{2,18},{3,19},{4,20},{5,21},{6,22},{7,23},{8,24},{9,... | collective-permute-start | bytes 49160 | tf_op jit(solution)/shard_map/ppermute | solution.py:70
  29.1 2.1 %collective-permute-start.8 = (f32[1,32,128]{2,1,0:T(8,128)S(1)}, f32[1,32,128]{2,1,0:T(8,128)S(1)}, u32[]{:S(2)}, u32[]{:S(2)}) collective-permute-start(f32[1,32,128]{2,1,0:T(8,128)S(1)} %get-tuple-element.20), channel_id=1, source_target_pairs={{0,24},{1,25},{2,26},{3,27},{4,28},{5,29},{6,30},{7,31},{8,16},{9,... | collective-permute-start | bytes 49160 | tf_op jit(solution)/shard_map/ppermute | solution.py:70
  31.2 2.2 %collective-permute-done.6.refs_0_ = f32[1,32,128]{2,1,0:T(8,128)S(1)} collective-permute-done((f32[1,32,128]{2,1,0:T(8,128)S(1)}, f32[1,32,128]{2,1,0:T(8,128)S(1)}, u32[]{:S(2)}, u32[]{:S(2)}) %collective-permute-start.6) | collective-permute-done | bytes 16416 | tf_op jit(solution)/shard_map/ppermute | solution.py:70
  33.4 0.0 collective-permute-start.11
  33.4 0.2 collective-permute-done.7.refs_1_
  33.6 2.3 %collective-permute-start.13 = (bf16[128,2048]{1,0:T(8,128)(2,1)S(1)}, bf16[128,2048]{1,0:T(8,128)(2,1)}, u32[]{:S(2)}, u32[]{:S(2)}) collective-permute-start(bf16[128,2048]{1,0:T(8,128)(2,1)S(1)} %shard_map.135.refs_2_), channel_id=1, source_target_pairs={{0,1},{1,0},{2,3},{3,2},{4,5},{5,4},{6,7},{7,6},{8,9},{9,8},{10,11... | collective-permute-start | bytes 1572872 | tf_op jit(solution)/shard_map/ppermute | solution.py:70
  35.9 0.0 collective-permute-done.8.refs_2_
  35.9 0.0 collective-permute-done.10.refs_3_.block
  35.9 0.0 collective-permute-done.12.refs_0_
  35.9 0.7 %collective-permute-start.14 = (bf16[128,2048]{1,0:T(8,128)(2,1)S(1)}, bf16[128,2048]{1,0:T(8,128)(2,1)}, u32[]{:S(2)}, u32[]{:S(2)}) collective-permute-start(bf16[128,2048]{1,0:T(8,128)(2,1)S(1)} %shard_map.138.refs_3_), channel_id=1, source_target_pairs={{0,1},{1,0},{2,3},{3,2},{4,5},{5,4},{6,7},{7,6},{8,9},{9,8},{10,11... | collective-permute-start | bytes 1572872 | tf_op jit(solution)/shard_map/ppermute | solution.py:70
  36.6 1.3 %collective-permute-start.15 = (bf16[128,2048]{1,0:T(8,128)(2,1)S(1)}, bf16[128,2048]{1,0:T(8,128)(2,1)}, u32[]{:S(2)}, u32[]{:S(2)}) collective-permute-start(bf16[128,2048]{1,0:T(8,128)(2,1)S(1)} %shard_map.138.refs_3_), channel_id=1, source_target_pairs={{0,8},{1,5},{2,10},{3,7},{4,12},{5,1},{6,14},{7,3},{8,24},{9,13},{... | collective-permute-start | bytes 1572872 | tf_op jit(solution)/shard_map/ppermute | solution.py:70
  37.9 0.2 collective-permute-start.18
  38.1 0.0 copy-done.3
  38.1 0.8 %shard_map.137 = bf16[64,64]{1,0:T(8,128)(2,1)S(1)} custom-call(f32[32,128]{1,0:T(8,128)S(1)} %shard_map.136.group, f32[64,64]{1,0:T(8,128)S(1)} %bitcast.26, f32[64,64]{1,0:T(8,128)S(1)} %bitcast.27, f32[64,64]{1,0:T(8,128)S(1)} %bitcast.28), custom_call_target="tpu_custom_call" | custom-call | flops 16777216 | bytes 131072 | tf_op jit(solution)/shard_map/pallas_call | solution.py:170
  38.9 0.1 reshape.7.row.refs_0_
  39.0 0.0 collective-permute-done.11.refs_1_
  39.0 0.5 collective-permute-start.17
  39.5 0.0 collective-permute-done.13.refs_4_
  39.5 0.5 collective-permute-start.19
  40.0 0.0 collective-permute-done.14.refs_5_
  40.0 1.2 %copy-done.1 = bf16[128,4096]{1,0:T(8,128)(2,1)S(1)} copy-done((bf16[128,4096]{1,0:T(8,128)(2,1)S(1)}, bf16[128,4096]{1,0:T(8,128)(2,1)}, u32[]{:S(2)}) %copy-start.1) | copy-done | bytes 1048600
  41.2 1.7 %copy-done.8 = bf16[320,4096]{1,0:T(8,128)(2,1)S(1)} copy-done((bf16[320,4096]{1,0:T(8,128)(2,1)S(1)}, bf16[320,4096]{1,0:T(8,128)(2,1)}, u32[]{:S(2)}) %copy-start.8) | copy-done | bytes 2621464
  43.0 4.2 %shard_map.139 = (bf16[336,4096]{1,0:T(8,128)(2,1)S(1)}, f32[8,336,128]{2,1,0:T(8,128)S(1)}, f32[8,128]{1,0:T(8,128)S(1)}) custom-call(bf16[320,4096]{1,0:T(8,128)(2,1)S(1)} %copy-done.8, bf16[1,4096]{1,0:T(2,128)(2,1)S(1)} %reshape.7.row.refs_0_, bf16[128,4096]{1,0:T(8,128)(2,1)S(1)} %copy-done.1, bf16[128,2048]{1,0:T(8,128)(2,1)S(1)} %shard_map.133.refs_0_, ...), custom_call_target="tpu_custom_call" | custom-call | flops 8589934592 | bytes 1024 | tf_op jit(solution)/shard_map/pallas_call | solution.py:231
  47.2 0.0 collective-permute-done.15.block
  47.2 2.3 %collective-permute-start.16 = (bf16[128,2048]{1,0:T(8,128)(2,1)}, bf16[128,2048]{1,0:T(8,128)(2,1)S(1)}, u32[]{:S(2)}, u32[]{:S(2)}) collective-permute-start(bf16[128,2048]{1,0:T(8,128)(2,1)} %shard_map.141.refs_3_), channel_id=1, source_target_pairs={{0,1},{1,0},{2,3},{3,2},{4,5},{5,4},{6,7},{7,6},{8,9},{9,8},{10,11... | collective-permute-start | bytes 1572872 | tf_op jit(solution)/shard_map/ppermute | solution.py:70
  49.5 2.0 %collective-permute-done.18.block = bf16[128,2048]{1,0:T(8,128)(2,1)S(1)} collective-permute-done((bf16[128,2048]{1,0:T(8,128)(2,1)S(1)}, bf16[128,2048]{1,0:T(8,128)(2,1)S(1)}, u32[]{:S(2)}, u32[]{:S(2)}) %collective-permute-start.18) | collective-permute-done | bytes 524320 | tf_op jit(solution)/shard_map/ppermute | solution.py:70
  51.5 0.1 collective-permute-start.20
  51.6 0.0 collective-permute-done.19.block
  51.6 0.8 %collective-permute-start.21 = (bf16[128,2048]{1,0:T(8,128)(2,1)S(1)}, bf16[128,2048]{1,0:T(8,128)(2,1)S(1)}, u32[]{:S(2)}, u32[]{:S(2)}) collective-permute-start(bf16[128,2048]{1,0:T(8,128)(2,1)S(1)} %shard_map.144.refs_1_), channel_id=1, source_target_pairs={{0,1},{1,0},{2,3},{3,2},{4,5},{5,4},{6,7},{7,6},{8,9},{9,8},{10,11... | collective-permute-start | bytes 1572872 | tf_op jit(solution)/shard_map/ppermute | solution.py:70
  52.4 0.0 collective-permute-done.17.refs_2_
  52.4 0.0 collective-permute-done.16.refs_1_
  52.4 2.1 %shard_map.142.before = f32[8,336,128]{2,1,0:T(8,128)S(1)} custom-call(bf16[336,4096]{1,0:T(8,128)(2,1)S(1)} %get-tuple-element.21.left, f32[8,336,128]{2,1,0:T(8,128)S(1)} %get-tuple-element.22.before, bf16[128,2048]{1,0:T(8,128)(2,1)S(1)} %shard_map.140.refs_0_, bf16[128,2048]{1,0:T(8,128)(2,1)S(1)} %collective-permute-done.16.refs_1_, ...), custom_call_target="tpu_custom_call" | custom-call | flops 4294967296 | bytes 1024 | tf_op jit(solution)/shard_map/pallas_call | solution.py:260
  54.5 0.0 collective-permute-done.20.refs_2_
  54.5 0.0 collective-permute-done.21.refs_3_
  54.5 3.2 %shard_map.145 = (f32[8,320,128]{2,1,0:T(8,128)}, f32[8,128]{1,0:T(8,128)}) custom-call(s32[8]{0:T(128)S(1)} %copy-done.7, bf16[336,4096]{1,0:T(8,128)(2,1)S(1)} %get-tuple-element.21.left, f32[8,336,128]{2,1,0:T(8,128)S(1)} %shard_map.142.before, bf16[128,2048]{1,0:T(8,128)(2,1)S(1)} %shard_map.143.refs_0_, bf16[128,2048]{1,0:T(8,128)(2,1)S(1)} %shard_map.144.refs_1_, ...), custom_call_target="tpu_custom_call" | custom-call | flops 1073741824 | bytes 8388608 | tf_op jit(solution)/shard_map/pallas_call | solution.py:316
  (23 shorter events, 0.2 us)
Async XLA Ops:
  0.6 4.0 %copy-start = (bf16[1,64,4096]{2,1,0:T(8,128)(2,1)S(1)}, bf16[1,64,4096]{2,1,0:T(8,128)(2,1)}, u32[]{:S(2)}) copy-start(bf16[1,64,4096]{2,1,0:T(8,128)(2,1)} %param.14) | copy-start | bytes 1572868
  0.6 7.6 %copy-start.10 = (bf16[1,64,4096]{2,1,0:T(8,128)(2,1)S(1)}, bf16[1,64,4096]{2,1,0:T(8,128)(2,1)}, u32[]{:S(2)}) copy-start(bf16[1,64,4096]{2,1,0:T(8,128)(2,1)} %param.15) | copy-start | bytes 1572868
  0.7 7.5 %copy-start.9 = (bf16[1,2,256,4096]{3,2,1,0:T(8,128)(2,1)S(1)}, bf16[1,2,256,4096]{3,2,1,0:T(8,128)(2,1)}, u32[]{:S(2)}) copy-start(bf16[1,2,256,4096]{3,2,1,0:T(8,128)(2,1)} %param.13) | copy-start | bytes 12582916
  1.9 7.7 %copy-start.5 = (s32[2]{0:T(128)S(1)}, s32[2]{0:T(128)}, u32[]{:S(2)}) copy-start(s32[2]{0:T(128)} %lengths.1) | copy-start | bytes 28
  2.0 7.7 %copy-start.6 = (s32[2]{0:T(128)S(1)}, s32[2]{0:T(128)}, u32[]{:S(2)}) copy-start(s32[2]{0:T(128)} %owners.1) | copy-start | bytes 28
  2.0 9.6 %collective-permute-start.4 = (bf16[128,2048]{1,0:T(8,128)(2,1)S(1)}, bf16[128,2048]{1,0:T(8,128)(2,1)S(1)}, u32[]{:S(2)}, u32[]{:S(2)}) collective-permute-start(bf16[128,2048]{1,0:T(8,128)(2,1)S(1)} %constant_dynamic-slice_fusion), channel_id=1, source_target_pairs={{0,17},{1,4},{2,19},{3,6},{4,21},{5,0},{6,23},{7,2},{8,1},{9,12},{... | collective-permute-start | bytes 1572872 | tf_op jit(solution)/shard_map/ppermute | solution.py:70
  9.6 28.5 %copy-start.2 = (f32[1,64,64]{2,1,0:T(8,128)S(1)}, f32[1,64,64]{2,1,0:T(8,128)}, u32[]{:S(2)}) copy-start(f32[1,64,64]{2,1,0:T(8,128)} %param.16) | copy-start | bytes 49156
  9.6 28.5 %copy-start.3 = (f32[1,64,64]{2,1,0:T(8,128)S(1)}, f32[1,64,64]{2,1,0:T(8,128)}, u32[]{:S(2)}) copy-start(f32[1,64,64]{2,1,0:T(8,128)} %param.17) | copy-start | bytes 49156
  9.7 28.4 %copy-start.4 = (f32[1,64,64]{2,1,0:T(8,128)S(1)}, f32[1,64,64]{2,1,0:T(8,128)}, u32[]{:S(2)}) copy-start(f32[1,64,64]{2,1,0:T(8,128)} %param.18) | copy-start | bytes 49156
  11.6 11.8 %collective-permute-start.5 = (bf16[128,2048]{1,0:T(8,128)(2,1)S(1)}, bf16[128,2048]{1,0:T(8,128)(2,1)S(1)}, u32[]{:S(2)}, u32[]{:S(2)}) collective-permute-start(bf16[128,2048]{1,0:T(8,128)(2,1)S(1)} %shard_map.133.refs_0_), channel_id=1, source_target_pairs={{0,8},{1,5},{2,10},{3,7},{4,12},{5,1},{6,14},{7,3},{8,24},{9,13},{... | collective-permute-start | bytes 1572872 | tf_op jit(solution)/shard_map/ppermute | solution.py:70
  13.0 10.4 %collective-permute-start.9 = (bf16[128,1024]{1,0:T(8,128)(2,1)S(1)}, bf16[128,1024]{1,0:T(8,128)(2,1)S(1)}, u32[]{:S(2)}, u32[]{:S(2)}) collective-permute-start(bf16[128,1024]{1,0:T(8,128)(2,1)S(1)} %get-tuple-element.27), channel_id=1, source_target_pairs={{0,2},{1,3},{2,0},{3,1},{4,6},{5,7},{6,4},{7,5},{8,10},{9,11},{10,... | collective-permute-start | bytes 786440 | tf_op jit(solution)/shard_map/ppermute | solution.py:70
  14.3 2.0 %collective-permute-start = (f32[8,32,128]{2,1,0:T(8,128)S(1)}, f32[8,32,128]{2,1,0:T(8,128)S(1)}, u32[]{:S(2)}, u32[]{:S(2)}) collective-permute-start(f32[8,32,128]{2,1,0:T(8,128)S(1)} %shard_map.131.rows.refs_0_), channel_id=1, source_target_pairs={{0,1},{1,0},{2,3},{3,2},{4,5},{5,4},{6,7},{7,6},{8,9},{9,8},{10,11... | collective-permute-start | bytes 393224 | tf_op jit(solution)/shard_map/ppermute | solution.py:70
  16.3 5.2 %collective-permute-start.1 = (f32[4,32,128]{2,1,0:T(8,128)S(1)}, f32[4,32,128]{2,1,0:T(8,128)S(1)}, u32[]{:S(2)}, u32[]{:S(2)}) collective-permute-start(f32[4,32,128]{2,1,0:T(8,128)S(1)} %get-tuple-element.16), channel_id=1, source_target_pairs={{0,2},{1,3},{2,0},{3,1},{4,6},{5,7},{6,4},{7,5},{8,10},{9,11},{10,... | collective-permute-start | bytes 196616 | tf_op jit(solution)/shard_map/ppermute | solution.py:70
  16.6 4.9 %collective-permute-start.2 = (f32[4,32,128]{2,1,0:T(8,128)S(1)}, f32[4,32,128]{2,1,0:T(8,128)S(1)}, u32[]{:S(2)}, u32[]{:S(2)}) collective-permute-start(f32[4,32,128]{2,1,0:T(8,128)S(1)} %get-tuple-element.15.sent), channel_id=1, source_target_pairs={{0,4},{1,5},{2,6},{3,7},{4,0},{5,1},{6,2},{7,3},{8,12},{9,13},{10,... | collective-permute-start | bytes 196616 | tf_op jit(solution)/shard_map/ppermute | solution.py:70
  17.9 5.5 %collective-permute-start.3 = (f32[4,32,128]{2,1,0:T(8,128)S(1)}, f32[4,32,128]{2,1,0:T(8,128)S(1)}, u32[]{:S(2)}, u32[]{:S(2)}) collective-permute-start(f32[4,32,128]{2,1,0:T(8,128)S(1)} %get-tuple-element.15.sent), channel_id=1, source_target_pairs={{0,6},{1,7},{2,4},{3,5},{4,2},{5,3},{6,0},{7,1},{8,14},{9,15},{10,... | collective-permute-start | bytes 196616 | tf_op jit(solution)/shard_map/ppermute | solution.py:70
  23.4 12.4 %collective-permute-start.10 = (bf16[128,2048]{1,0:T(8,128)(2,1)S(1)}, bf16[128,2048]{1,0:T(8,128)(2,1)S(1)}, u32[]{:S(2)}, u32[]{:S(2)}) collective-permute-start(bf16[128,2048]{1,0:T(8,128)(2,1)S(1)} %shard_map.135.refs_2_), channel_id=1, source_target_pairs={{0,4},{1,17},{2,6},{3,19},{4,0},{5,21},{6,2},{7,23},{8,12},{9,1},{... | collective-permute-start | bytes 1572872 | tf_op jit(solution)/shard_map/ppermute | solution.py:70
  26.6 9.3 %collective-permute-start.12 = (bf16[128,1024]{1,0:T(8,128)(2,1)S(1)}, bf16[128,1024]{1,0:T(8,128)(2,1)S(1)}, u32[]{:S(2)}, u32[]{:S(2)}) collective-permute-start(bf16[128,1024]{1,0:T(8,128)(2,1)S(1)} %get-tuple-element.26), channel_id=1, source_target_pairs={{0,2},{1,3},{2,0},{3,1},{4,6},{5,7},{6,4},{7,5},{8,10},{9,11},{10,... | collective-permute-start | bytes 786440 | tf_op jit(solution)/shard_map/ppermute | solution.py:70
  27.7 5.7 %collective-permute-start.6 = (f32[1,32,128]{2,1,0:T(8,128)S(1)}, f32[1,32,128]{2,1,0:T(8,128)S(1)}, u32[]{:S(2)}, u32[]{:S(2)}) collective-permute-start(f32[1,32,128]{2,1,0:T(8,128)S(1)} %get-tuple-element.18), channel_id=1, source_target_pairs={{0,8},{1,9},{2,10},{3,11},{4,12},{5,13},{6,14},{7,15},{8,0},{9,1},... | collective-permute-start | bytes 49160 | tf_op jit(solution)/shard_map/ppermute | solution.py:70
  27.7 5.9 %collective-permute-start.7 = (f32[1,32,128]{2,1,0:T(8,128)S(1)}, f32[1,32,128]{2,1,0:T(8,128)S(1)}, u32[]{:S(2)}, u32[]{:S(2)}) collective-permute-start(f32[1,32,128]{2,1,0:T(8,128)S(1)} %get-tuple-element.19), channel_id=1, source_target_pairs={{0,16},{1,17},{2,18},{3,19},{4,20},{5,21},{6,22},{7,23},{8,24},{9,... | collective-permute-start | bytes 49160 | tf_op jit(solution)/shard_map/ppermute | solution.py:70
  29.1 6.7 %collective-permute-start.8 = (f32[1,32,128]{2,1,0:T(8,128)S(1)}, f32[1,32,128]{2,1,0:T(8,128)S(1)}, u32[]{:S(2)}, u32[]{:S(2)}) collective-permute-start(f32[1,32,128]{2,1,0:T(8,128)S(1)} %get-tuple-element.20), channel_id=1, source_target_pairs={{0,24},{1,25},{2,26},{3,27},{4,28},{5,29},{6,30},{7,31},{8,16},{9,... | collective-permute-start | bytes 49160 | tf_op jit(solution)/shard_map/ppermute | solution.py:70
  33.4 5.6 %collective-permute-start.11 = (bf16[128,2048]{1,0:T(8,128)(2,1)S(1)}, bf16[128,2048]{1,0:T(8,128)(2,1)}, u32[]{:S(2)}, u32[]{:S(2)}) collective-permute-start(bf16[128,2048]{1,0:T(8,128)(2,1)S(1)} %shard_map.133.refs_0_), channel_id=1, source_target_pairs={{0,1},{1,0},{2,3},{3,2},{4,5},{5,4},{6,7},{7,6},{8,9},{9,8},{10,11... | collective-permute-start | bytes 1572872 | tf_op jit(solution)/shard_map/ppermute | solution.py:70
  33.6 5.9 %collective-permute-start.13 = (bf16[128,2048]{1,0:T(8,128)(2,1)S(1)}, bf16[128,2048]{1,0:T(8,128)(2,1)}, u32[]{:S(2)}, u32[]{:S(2)}) collective-permute-start(bf16[128,2048]{1,0:T(8,128)(2,1)S(1)} %shard_map.135.refs_2_), channel_id=1, source_target_pairs={{0,1},{1,0},{2,3},{3,2},{4,5},{5,4},{6,7},{7,6},{8,9},{9,8},{10,11... | collective-permute-start | bytes 1572872 | tf_op jit(solution)/shard_map/ppermute | solution.py:70
  35.9 4.1 %collective-permute-start.14 = (bf16[128,2048]{1,0:T(8,128)(2,1)S(1)}, bf16[128,2048]{1,0:T(8,128)(2,1)}, u32[]{:S(2)}, u32[]{:S(2)}) collective-permute-start(bf16[128,2048]{1,0:T(8,128)(2,1)S(1)} %shard_map.138.refs_3_), channel_id=1, source_target_pairs={{0,1},{1,0},{2,3},{3,2},{4,5},{5,4},{6,7},{7,6},{8,9},{9,8},{10,11... | collective-permute-start | bytes 1572872 | tf_op jit(solution)/shard_map/ppermute | solution.py:70
  36.6 10.6 %collective-permute-start.15 = (bf16[128,2048]{1,0:T(8,128)(2,1)S(1)}, bf16[128,2048]{1,0:T(8,128)(2,1)}, u32[]{:S(2)}, u32[]{:S(2)}) collective-permute-start(bf16[128,2048]{1,0:T(8,128)(2,1)S(1)} %shard_map.138.refs_3_), channel_id=1, source_target_pairs={{0,8},{1,5},{2,10},{3,7},{4,12},{5,1},{6,14},{7,3},{8,24},{9,13},{... | collective-permute-start | bytes 1572872 | tf_op jit(solution)/shard_map/ppermute | solution.py:70
  37.9 13.6 %collective-permute-start.18 = (bf16[128,2048]{1,0:T(8,128)(2,1)S(1)}, bf16[128,2048]{1,0:T(8,128)(2,1)S(1)}, u32[]{:S(2)}, u32[]{:S(2)}) collective-permute-start(bf16[128,2048]{1,0:T(8,128)(2,1)S(1)} %shard_map.138.refs_3_), channel_id=1, source_target_pairs={{0,2},{1,3},{2,0},{3,1},{4,6},{5,7},{6,4},{7,5},{8,10},{9,11},{10,... | collective-permute-start | bytes 1572872 | tf_op jit(solution)/shard_map/ppermute | solution.py:70
  39.0 13.4 %collective-permute-start.17 = (bf16[128,2048]{1,0:T(8,128)(2,1)S(1)}, bf16[128,2048]{1,0:T(8,128)(2,1)S(1)}, u32[]{:S(2)}, u32[]{:S(2)}) collective-permute-start(bf16[128,2048]{1,0:T(8,128)(2,1)S(1)} %shard_map.140.refs_0_), channel_id=1, source_target_pairs={{0,1},{1,0},{2,3},{3,2},{4,5},{5,4},{6,7},{7,6},{8,9},{9,8},{10,11... | collective-permute-start | bytes 1572872 | tf_op jit(solution)/shard_map/ppermute | solution.py:70
  39.5 12.1 %collective-permute-start.19 = (bf16[128,2048]{1,0:T(8,128)(2,1)S(1)}, bf16[128,2048]{1,0:T(8,128)(2,1)S(1)}, u32[]{:S(2)}, u32[]{:S(2)}) collective-permute-start(bf16[128,2048]{1,0:T(8,128)(2,1)S(1)} %shard_map.140.refs_0_), channel_id=1, source_target_pairs={{0,8},{1,5},{2,10},{3,7},{4,12},{5,1},{6,14},{7,3},{8,24},{9,13},{... | collective-permute-start | bytes 1572872 | tf_op jit(solution)/shard_map/ppermute | solution.py:70
  40.0 1.2 %copy-start.1 = (bf16[128,4096]{1,0:T(8,128)(2,1)S(1)}, bf16[128,4096]{1,0:T(8,128)(2,1)}, u32[]{:S(2)}) copy-start(bf16[128,4096]{1,0:T(8,128)(2,1)} %own.1) | copy-start | bytes 3145732
  41.2 1.7 %copy-start.8 = (bf16[320,4096]{1,0:T(8,128)(2,1)S(1)}, bf16[320,4096]{1,0:T(8,128)(2,1)}, u32[]{:S(2)}) copy-start(bf16[320,4096]{1,0:T(8,128)(2,1)} %stored.1) | copy-start | bytes 7864324
  47.2 5.2 %collective-permute-start.16 = (bf16[128,2048]{1,0:T(8,128)(2,1)}, bf16[128,2048]{1,0:T(8,128)(2,1)S(1)}, u32[]{:S(2)}, u32[]{:S(2)}) collective-permute-start(bf16[128,2048]{1,0:T(8,128)(2,1)} %shard_map.141.refs_3_), channel_id=1, source_target_pairs={{0,1},{1,0},{2,3},{3,2},{4,5},{5,4},{6,7},{7,6},{8,9},{9,8},{10,11... | collective-permute-start | bytes 1572872 | tf_op jit(solution)/shard_map/ppermute | solution.py:70
  51.5 3.0 %collective-permute-start.20 = (bf16[128,2048]{1,0:T(8,128)(2,1)S(1)}, bf16[128,2048]{1,0:T(8,128)(2,1)S(1)}, u32[]{:S(2)}, u32[]{:S(2)}) collective-permute-start(bf16[128,2048]{1,0:T(8,128)(2,1)S(1)} %shard_map.143.refs_0_), channel_id=1, source_target_pairs={{0,1},{1,0},{2,3},{3,2},{4,5},{5,4},{6,7},{7,6},{8,9},{9,8},{10,11... | collective-permute-start | bytes 1572872 | tf_op jit(solution)/shard_map/ppermute | solution.py:70
  51.6 2.9 %collective-permute-start.21 = (bf16[128,2048]{1,0:T(8,128)(2,1)S(1)}, bf16[128,2048]{1,0:T(8,128)(2,1)S(1)}, u32[]{:S(2)}, u32[]{:S(2)}) collective-permute-start(bf16[128,2048]{1,0:T(8,128)(2,1)S(1)} %shard_map.144.refs_1_), channel_id=1, source_target_pairs={{0,1},{1,0},{2,3},{3,2},{4,5},{5,4},{6,7},{7,6},{8,9},{9,8},{10,11... | collective-permute-start | bytes 1572872 | tf_op jit(solution)/shard_map/ppermute | solution.py:70
  52.4 2.1 %copy-start.7 = (s32[8]{0:T(128)S(1)}, s32[8]{0:T(128)}, u32[]{:S(2)}) copy-start(s32[8]{0:T(128)} %query_owner.1) | copy-start | bytes 100
